TPU v7x, 32 devices: a whole 2x2x4 slice. The times are simulated.
32 devices in a mesh: dom: 8 (over y, x, core), rep: 4 (over z).
Axes of the slice: x: 2, y: 2, z: 4, core: 2. Of those that a mesh axis runs over, the one named last changes fastest.
Arguments:
- node_state: bfloat16 [32768, 256], P(('dom', 'rep')), may hold values from -6 to 6
- edge_tiles: bfloat16 [32768, 5, 128], P(('dom', 'rep')), may hold values from -0.25 to 0.25
- block_mask: int32 [256, 5], P(('dom', 'rep')), may hold values from 0 to 1, as said below
- block_len: int32 [256], P(('dom', 'rep')), may hold values from 64 to 128, as said below
- w_in: bfloat16 [512, 256], replicated, may hold values from -0.25 to 0.25
- w_out: bfloat16 [256, 256], replicated, may hold values from -0.375 to 0.375
- gain: float32 [256], replicated, may hold values from 0.5 to 1.5
- upstream: bfloat16 [32768, 256], P(('dom', 'rep')), may hold values from -6 to 6
Outputs:
- new_state: bfloat16 [32768, 256], P(('dom', 'rep'))
- grad_state: bfloat16 [32768, 256], P(('dom', 'rep'))
- grad_w_in: float32 [512, 256], replicated
- grad_w_out: float32 [256, 256], replicated
- grad_gain: float32 [256], replicated
Inputs may be any that keep to these rules, and one draw needn't show every extreme that they name: `block_mask`: the block at offset 2 (a block with itself) is always coupled. `block_len`: the largest length, 128, occurs in every draw.
All inputs are finite; a program needn't handle non-finite values.
Results may differ from a plain program's by a relative error of at most 0.0058.
Values may be sent and summed in bfloat16 or wider, within the bound.
No kernel may reach another device: no remote copies, remote signals or barrier semaphores. Data moves between devices by JAX's collectives and lax.ppermute only.
A program may use at most 64 MiB of HBM per device.

v0:
```python
import math

import jax
import jax.numpy as jnp
from jax import lax
from jax.sharding import PartitionSpec as P

EPSILON = 1e-05


def padded(block, sides, width):
    for axis, dim in sides:
        count = lax.axis_size(axis)
        forward = [(i, i + 1) for i in range(count - 1)]
        forward.append((count - 1, 0))
        backward = [(target, source) for source, target in forward]
        low = lax.ppermute(
            lax.slice_in_dim(block, block.shape[dim] - width, None, axis=dim), axis, forward
        )
        high = lax.ppermute(lax.slice_in_dim(block, 0, width, axis=dim), axis, backward)
        block = jnp.concatenate([low, block, high], axis=dim)
    return block


def swish_slope(preact):
    sigma = jax.nn.sigmoid(preact)
    return sigma * (1.0 + preact * (1.0 - sigma))


def node_update(node_state, message, w_in, w_out, gain, upstream, valid_rows):
    latent = node_state.shape[1]
    joined = jnp.concatenate([node_state, message], axis=1)
    preact = jnp.dot(joined, w_in, preferred_element_type=jnp.float32)
    activated = jax.nn.silu(preact).astype(jnp.bfloat16)
    output = jnp.dot(activated, w_out, preferred_element_type=jnp.float32)
    centred = output - jnp.mean(output, axis=1, keepdims=True)
    inverse = lax.rsqrt(jnp.mean(centred * centred, axis=1, keepdims=True) + EPSILON)
    normed = centred * inverse
    new_state = (node_state.astype(jnp.float32) + gain * normed * valid_rows).astype(jnp.bfloat16)
    masked_up = upstream.astype(jnp.float32) * valid_rows
    gain_terms = jnp.sum(masked_up * normed, axis=0)
    scaled = masked_up * gain
    grad_output = inverse * (
        scaled
        - jnp.mean(scaled, axis=1, keepdims=True)
        - normed * jnp.mean(scaled * normed, axis=1, keepdims=True)
    )
    grad_output = grad_output.astype(jnp.bfloat16)
    out_terms = jnp.dot(activated.T, grad_output, preferred_element_type=jnp.float32)
    grad_act = jnp.dot(grad_output, w_out.T, preferred_element_type=jnp.float32)
    grad_pre = (grad_act * swish_slope(preact)).astype(jnp.bfloat16)
    in_terms = jnp.dot(joined.T, grad_pre, preferred_element_type=jnp.float32)
    grad_joined = jnp.dot(grad_pre, w_in.T, preferred_element_type=jnp.float32)
    return (
        new_state,
        grad_joined[:, :latent],
        grad_joined[:, latent:].astype(jnp.bfloat16),
        in_terms,
        out_terms,
        gain_terms,
    )


def local(node_state, edge_tiles, block_mask, block_len, w_in, w_out, gain, upstream):
    row_count, latent = node_state.shape
    offsets = edge_tiles.shape[1]
    block_rows = edge_tiles.shape[2]
    band_blocks = (offsets - 1) // 2
    blocks = row_count // block_rows
    rim_rows = band_blocks * block_rows
    position = lax.broadcasted_iota(jnp.int32, (blocks, block_rows), 1)
    valid_mask = (position < block_len[:, None]).astype(jnp.float32)
    valid_rows = valid_mask.reshape(row_count, 1)
    coupling = block_mask.astype(jnp.float32)[:, None, :] * valid_mask[:, :, None]
    coupled = (
        edge_tiles.reshape(blocks, block_rows, offsets, block_rows)
        * coupling.astype(jnp.bfloat16)[..., None]
    )
    masked = node_state * valid_rows.astype(jnp.bfloat16)
    extended = padded(masked, ((("dom", "rep"), 0),), rim_rows)
    ext_blocks = extended.reshape(blocks + 2 * band_blocks, block_rows, latent)
    summed = jnp.zeros((blocks, block_rows, latent), jnp.float32)
    for offset in range(offsets):
        summed = summed + jnp.einsum(
            "bij,bjl->bil",
            coupled[:, :, offset, :],
            ext_blocks[offset : offset + blocks],
            preferred_element_type=jnp.float32,
        )
    message = summed.astype(jnp.bfloat16).reshape(row_count, latent)
    new_state, grad_direct, grad_message, in_terms, out_terms, gain_terms = node_update(
        node_state, message, w_in, w_out, gain, upstream, valid_rows
    )
    grad_blocks = grad_message.reshape(blocks, block_rows, latent)
    spread = jnp.zeros((blocks + 2 * band_blocks, block_rows, latent), jnp.float32)
    for offset in range(offsets):
        contrib = jnp.einsum(
            "bij,bil->bjl",
            coupled[:, :, offset, :],
            grad_blocks,
            preferred_element_type=jnp.float32,
        )
        spread = spread + jnp.pad(contrib, ((offset, offsets - 1 - offset), (0, 0), (0, 0)))
    own_rows = spread[band_blocks : band_blocks + blocks].reshape(row_count, latent)
    spill_rows = jnp.concatenate([spread[:band_blocks], spread[band_blocks + blocks :]], axis=0)
    spill_rows = spill_rows.reshape(2 * rim_rows, latent)
    received_rows = padded(
        spill_rows.astype(jnp.bfloat16), ((("dom", "rep"), 0),), rim_rows
    ).astype(spill_rows.dtype)
    head_rows = jnp.pad(received_rows[:rim_rows], ((0, row_count - rim_rows), (0, 0)))
    tail_rows = jnp.pad(
        received_rows[received_rows.shape[0] - rim_rows :], ((row_count - rim_rows, 0), (0, 0))
    )
    transposed = own_rows + head_rows + tail_rows
    transposed = transposed * valid_rows
    grad_state = (upstream.astype(jnp.float32) + grad_direct + transposed).astype(jnp.bfloat16)
    in_total, out_total, gain_total = lax.psum((in_terms, out_terms, gain_terms), ("dom", "rep"))
    grad_scale = 1.0 / math.sqrt(row_count * lax.axis_size("dom") * lax.axis_size("rep"))
    return (
        new_state,
        grad_state,
        in_total * grad_scale,
        out_total * grad_scale,
        gain_total * grad_scale,
    )


def solution(mesh):
    placed = (
        P(("dom", "rep"), None),
        P(("dom", "rep"), None, None),
        P(("dom", "rep"), None),
        P(("dom", "rep")),
        P(),
        P(),
        P(),
        P(("dom", "rep"), None),
    )
    return jax.shard_map(
        local,
        mesh=mesh,
        in_specs=placed,
        out_specs=(P(("dom", "rep"), None), P(("dom", "rep"), None), P(), P(), P()),
        check_vma=False,
    )
```

profile of v0, /device:TPU:0, one launch (start us, length us, event | category | flops | bytes accessed | tf_op | source)
XLA Modules:
  0.0 233.7 jit_solution(17877182548782741530)
XLA Ops:
  8.0 1.2 broadcast_multiply_fusion.2
  9.9 6.4 %collective-permute-start.1 = (bf16[256,256]{1,0:T(8,128)(2,1)}, bf16[256,256]{1,0:T(8,128)(2,1)S(1)}, u32[]{:S(2)}, u32[]{:S(2)}) collective-permute-start(bf16[256,256]{1,0:T(8,128)(2,1)} %get-tuple-element.27), channel_id=1, source_target_pairs={{1,0},{2,1},{3,2},{4,3},{5,4},{6,5},{7,6},{8,7},{9,8},{10,9},{11,1... | collective-permute-start | bytes 393224 | tf_op jit(solution)/shard_map/ppermute | solution.py:20
  16.5 2.0 broadcast_multiply_fusion
  19.5 1.2 copy.15
  20.7 4.0 %collective-permute-done = bf16[256,256]{1,0:T(8,128)(2,1)S(1)} collective-permute-done((bf16[256,256]{1,0:T(8,128)(2,1)S(1)}, bf16[256,256]{1,0:T(8,128)(2,1)S(1)}, u32[]{:S(2)}, u32[]{:S(2)}) %collective-permute-start) | collective-permute-done | bytes 131104 | tf_op jit(solution)/shard_map/ppermute | solution.py:17
  28.7 1.4 fusion.9
  31.7 1.3 fusion.14
  33.5 1.3 copy-done.1
  34.7 1.3 fusion.23
  36.1 1.3 fusion.22
  37.4 1.3 fusion.21
  38.7 1.4 fusion.19
  40.1 1.3 fusion.18
  41.4 37.7 %psum.23 = f32[256]{0:T(256)S(1)} all-reduce(f32[256]{0:T(256)S(1)} %get-tuple-element.10), channel_id=1, replica_groups=mesh['dom'=8,'rep'=4] {'dom','rep'}, use_global_device_ids=true, to_apply=%region_7.8 | all-reduce | flops 256 | bytes 2048 | tf_op jit(solution)/shard_map/psum | solution.py:117
  79.1 2.0 copy.26
  81.5 4.0 %fusion.29 = (bf16[12,128,256]{2,1,0:T(8,128)(2,1)S(1)}, f32[12,128,256]{2,1,0:T(8,128)}) fusion(f32[8,128,256]{2,1,0:T(8,128)} %fusion.23, f32[8,128,256]{2,1,0:T(8,128)} %fusion.22, f32[8,128,256]{2,1,0:T(8,128)} %fusion.21, f32[8,128,256]{2,1,0:T(8,128)} %fusion.19, f32[8,128,256]{2,1,0:T(8,128)} %fusion.18), kind=kLoop, calls=%fused_computation.68 | loop fusion | flops 1966080 | bytes 7602176 | tf_op jit(solution)/shard_map/convert.3
  86.5 2.0 collective-permute-start.2
  88.5 3.4 %collective-permute-start.3 = (bf16[256,256]{0,1:T(8,128)(2,1)S(1)}, bf16[256,256]{0,1:T(8,128)(2,1)S(1)}, u32[]{:S(2)}, u32[]{:S(2)}) collective-permute-start(bf16[256,256]{0,1:T(8,128)(2,1)S(1)} %copy.36), channel_id=1, source_target_pairs={{1,0},{2,1},{3,2},{4,3},{5,4},{6,5},{7,6},{8,7},{9,8},{10,9},{11,1... | collective-permute-start | bytes 393224 | tf_op jit(solution)/shard_map/ppermute | solution.py:20
  92.0 2.3 slice.126
  94.2 1.6 copy.33
  97.7 2.0 copy.27
  99.8 123.5 %all-reduce.9.cloned.1.call-done = (f32[512,256]{1,0:T(8,128)}, f32[256,256]{1,0:T(8,128)}) async-done(((f32[512,256]{1,0:T(8,128)}, f32[256,256]{1,0:T(8,128)}), (f32[512,256]{1,0:T(8,128)}, f32[256,256]{1,0:T(8,128)})) %all-reduce.9.cloned.1.call-update) | async-done | bytes 786448 | tf_op jit(solution)/shard_map/psum | solution.py:117
  223.2 1.9 broadcast_multiply_fusion.1
  225.1 1.7 broadcast_multiply_fusion.3
  (56 shorter events, 11.9 us)
Async XLA Ops:
  7.2 19.2 %copy-start = (bf16[512,256]{1,0:T(8,128)(2,1)S(1)}, bf16[512,256]{1,0:T(8,128)(2,1)}, u32[]{:S(2)}) copy-start(bf16[512,256]{1,0:T(8,128)(2,1)} %param.12) | copy-start | bytes 786436
  7.2 9.1 %copy-start.6 = (s32[8,5]{1,0:T(8,128)S(1)}, s32[8,5]{1,0:T(8,128)}, u32[]{:S(2)}) copy-start(s32[8,5]{1,0:T(8,128)} %param.10) | copy-start | bytes 484
  7.2 216.1 %all-reduce.9.cloned.1.call-start = ((), (), s32[]{:S(2)}) async-start(), calls=%async_computation | async-start | bytes 1572864 | tf_op jit(solution)/shard_map/psum | solution.py:117
  9.9 10.8 %collective-permute-start.1 = (bf16[256,256]{1,0:T(8,128)(2,1)}, bf16[256,256]{1,0:T(8,128)(2,1)S(1)}, u32[]{:S(2)}, u32[]{:S(2)}) collective-permute-start(bf16[256,256]{1,0:T(8,128)(2,1)} %get-tuple-element.27), channel_id=1, source_target_pairs={{1,0},{2,1},{3,2},{4,3},{5,4},{6,5},{7,6},{8,7},{9,8},{10,9},{11,1... | collective-permute-start | bytes 393224 | tf_op jit(solution)/shard_map/ppermute | solution.py:20
  16.3 8.5 %collective-permute-start = (bf16[256,256]{1,0:T(8,128)(2,1)S(1)}, bf16[256,256]{1,0:T(8,128)(2,1)S(1)}, u32[]{:S(2)}, u32[]{:S(2)}) collective-permute-start(bf16[256,256]{1,0:T(8,128)(2,1)S(1)} %get-tuple-element.28), channel_id=1, source_target_pairs={{0,1},{1,2},{2,3},{3,4},{4,5},{5,6},{6,7},{7,8},{8,9},{9,10},{10,1... | collective-permute-start | bytes 393224 | tf_op jit(solution)/shard_map/ppermute | solution.py:17
  16.5 2.0 copy-start.2
  26.4 0.9 copy-start.4
  27.3 0.7 copy-start.5
  27.7 1.0 copy-start.3
  33.4 1.3 copy-start.1
  40.1 41.1 %slice-start = ((f32[1024,512]{1,0:T(8,128)}), f32[1024,256]{1,0:T(8,128)S(1)}, s32[]{:S(2)}) async-start(f32[1024,512]{1,0:T(8,128)} %copy-done.1), calls=%async_computation.1 | async-start | bytes 2097152 | tf_op jit(solution)/shard_map/slice | solution.py:56
  86.5 9.9 %collective-permute-start.2 = (bf16[256,256]{0,1:T(8,128)(2,1)}, bf16[256,256]{0,1:T(8,128)(2,1)S(1)}, u32[]{:S(2)}, u32[]{:S(2)}) collective-permute-start(bf16[256,256]{0,1:T(8,128)(2,1)} %copy.34), channel_id=1, source_target_pairs={{0,1},{1,2},{2,3},{3,4},{4,5},{5,6},{6,7},{7,8},{8,9},{9,10},{10,1... | collective-permute-start | bytes 393224 | tf_op jit(solution)/shard_map/ppermute | solution.py:17
  88.5 7.9 %collective-permute-start.3 = (bf16[256,256]{0,1:T(8,128)(2,1)S(1)}, bf16[256,256]{0,1:T(8,128)(2,1)S(1)}, u32[]{:S(2)}, u32[]{:S(2)}) collective-permute-start(bf16[256,256]{0,1:T(8,128)(2,1)S(1)} %copy.36), channel_id=1, source_target_pairs={{1,0},{2,1},{3,2},{4,3},{5,4},{6,5},{7,6},{8,7},{9,8},{10,9},{11,1... | collective-permute-start | bytes 393224 | tf_op jit(solution)/shard_map/ppermute | solution.py:20
  95.8 0.8 copy-start.7
Sparse Core Ops, SparseCore 0:
  96.0 127.2 all-reduce.8
where the time goes:
time: 234 us
  waiting for transfers between devices  128 us (55%)
  blocking collectives  37.7 us (16%)
  other arithmetic  15.7 us (7%)
  local copies, waits for them, and re-layouts  14.4 us (6%)
  between operations  14.3 us (6%)
  matrix products  12.2 us (5%)
  starting transfers between devices  11.8 us (5%)
    psum x1, waiting for transfers between devices, local(): lax.psum((in_terms, out_terms, gain_terms), ('dom', 'rep'))  123 us
    psum x1, blocking collectives, local(): lax.psum((in_terms, out_terms, gain_terms), ('dom', 'rep'))  37.7 us
    ppermute x2, starting transfers between devices, padded(): lax.ppermute(lax.slice_in_dim(block, 0, width, axis=dim), axis, backward)  9.72 us
    unnamed x21, local copies, waits for them, and re-layouts  8.74 us
    dot_general x5, matrix products, local(): jnp.einsum('bij,bil->bjl', coupled[:, :, offset, :], grad_blocks, preferr...  6.68 us
  transfers between devices with their start and end apart: 5, of which 2 were waited for; matrix products, arithmetic and copies ran while one was open for 5% of the time, Pallas kernels for 0%

commit v1 on v0

v1 whole, which is shorter than its diff:
```python
import functools
import math

import jax
import jax.numpy as jnp
from jax import lax
from jax.experimental import pallas as pl
from jax.experimental.pallas import tpu as pltpu
from jax.sharding import PartitionSpec as P

EPSILON = 1e-05
F32 = jnp.float32
BF16 = jnp.bfloat16
GAIN_ROWS = 8
VMEM_LIMIT = 40 * 1024 * 1024


def dot(a, b, contract):
    return lax.dot_general(a, b, ((contract[:1], contract[1:]), ((), ())), preferred_element_type=F32)


def local_kernel(
    cfg,
    place_ref,
    len_ref,
    mask_ref,
    state_ref,
    tiles_ref,
    up_ref,
    w_in_ref,
    w_out_ref,
    gain_ref,
    odd_ref,
    even_ref,
    new_ref,
    inner_ref,
    rim_ref,
    spill_odd_ref,
    spill_even_ref,
    send_ref,
    ext_ref,
    band_ref,
    spread_ref,
    grad_in_ref,
    grad_out_ref,
    gain_sum_ref,
):
    bs, offsets, chunks, scale = cfg
    rim = (offsets - 1) // 2 * bs
    rows, latent = state_ref.shape
    size = rows // chunks
    per = size // bs
    width = size + 2 * rim
    side = place_ref[0]
    me = place_ref[1]
    far = rows + rim

    ext_ref[pl.ds(pl.multiple_of(side * far, bs), rim), :] = odd_ref[...]
    ext_ref[pl.ds(pl.multiple_of((1 - side) * far, bs), rim), :] = even_ref[...]

    def validity(block):
        position = lax.broadcasted_iota(jnp.int32, (bs, 1), 0)
        return (position < len_ref[block]).astype(F32)

    for block in range(rows // bs):
        here = slice(block * bs, (block + 1) * bs)
        ext_ref[rim + block * bs : rim + (block + 1) * bs, :] = (
            state_ref[here, :].astype(F32) * validity(block)
        ).astype(BF16)

    spread_ref[...] = jnp.zeros_like(spread_ref)
    grad_in_ref[...] = jnp.zeros_like(grad_in_ref)
    grad_out_ref[...] = jnp.zeros_like(grad_out_ref)
    gain_sum_ref[...] = jnp.zeros_like(gain_sum_ref)
    gain = gain_ref[...]

    for chunk in range(chunks):
        first = chunk * per
        here = slice(chunk * size, (chunk + 1) * size)
        valid = jnp.concatenate([validity(first + j) for j in range(per)], axis=0)
        for j in range(per):
            row = slice(j * bs, (j + 1) * bs)
            for column in range(width // bs):
                offset = column - j
                cols = slice(column * bs, (column + 1) * bs)
                if 0 <= offset < offsets:
                    tile = tiles_ref[offset, (first + j) * bs : (first + j + 1) * bs, :]
                    on = mask_ref[first + j, offset].astype(F32).astype(BF16)
                    band_ref[row, cols] = tile * on
                else:
                    band_ref[row, cols] = jnp.zeros((bs, bs), BF16)
        band = band_ref[...]
        reach = slice(chunk * size, chunk * size + width)
        message = (dot(band, ext_ref[reach, :], (1, 0)) * valid).astype(BF16)
        state = state_ref[here, :]
        preact = dot(state, w_in_ref[:latent, :], (1, 0)) + dot(message, w_in_ref[latent:, :], (1, 0))
        sigma = jax.nn.sigmoid(preact)
        activated = (preact * sigma).astype(BF16)
        output = dot(activated, w_out_ref[...], (1, 0))
        centred = output - jnp.mean(output, axis=1, keepdims=True)
        inverse = lax.rsqrt(jnp.mean(centred * centred, axis=1, keepdims=True) + EPSILON)
        normed = centred * inverse
        new_ref[here, :] = (state.astype(F32) + gain * normed * valid).astype(BF16)
        upstream = up_ref[here, :].astype(F32)
        masked_up = upstream * valid
        gain_sum_ref[...] += jnp.sum(masked_up * normed, axis=0, keepdims=True)
        scaled = masked_up * gain
        grad_output = (
            inverse
            * (
                scaled
                - jnp.mean(scaled, axis=1, keepdims=True)
                - normed * jnp.mean(scaled * normed, axis=1, keepdims=True)
            )
        ).astype(BF16)
        grad_out_ref[...] += dot(activated, grad_output, (0, 0))
        grad_act = dot(grad_output, w_out_ref[...], (1, 1))
        slope = sigma * (1.0 + preact * (1.0 - sigma))
        grad_pre = (grad_act * slope).astype(BF16)
        grad_in_ref[:latent, :] += dot(state, grad_pre, (0, 0))
        grad_in_ref[latent:, :] += dot(message, grad_pre, (0, 0))
        direct = dot(grad_pre, w_in_ref[:latent, :], (1, 1))
        grad_message = dot(grad_pre, w_in_ref[latent:, :], (1, 1)).astype(BF16)
        grad_message = (grad_message.astype(F32) * valid).astype(BF16)
        spread_ref[reach, :] += dot(band, grad_message, (0, 0))
        own = upstream + direct
        if chunk == 0:
            rim_ref[:size, :] = own
        elif chunk == chunks - 1:
            rim_ref[size:, :] = own
        else:
            inner_ref[here, :] = own

    for block in range(rows // bs):
        here = slice(block * bs, (block + 1) * bs)
        back = spread_ref[rim + block * bs : rim + (block + 1) * bs, :] * validity(block)
        if block < per:
            rim_ref[here, :] += back
        elif block >= rows // bs - per:
            there = slice(size - rows + here.start + size, size - rows + here.stop + size)
            rim_ref[there, :] += back
        else:
            inner_ref[here, :] += back
    spill_odd_ref[...] = spread_ref[pl.ds(pl.multiple_of(side * far, bs), rim), :].astype(BF16)
    spill_even_ref[...] = spread_ref[pl.ds(pl.multiple_of((1 - side) * far, bs), rim), :].astype(BF16)

    count = send_ref.shape[0] * send_ref.shape[1]
    n_in = grad_in_ref.shape[0] // count
    n_out = grad_out_ref.shape[0] // count
    top = lax.broadcasted_iota(jnp.int32, (GAIN_ROWS, latent), 0) == 0
    for piece in range(count):
        turn = lax.bitwise_xor(me, piece)
        half = lax.bitwise_and(turn, 1)
        slot = lax.shift_right_logical(turn, 1)
        send_ref[half, slot, :n_in, :] = (grad_in_ref[piece * n_in : (piece + 1) * n_in, :] * scale).astype(BF16)
        send_ref[half, slot, n_in : n_in + n_out, :] = (
            grad_out_ref[piece * n_out : (piece + 1) * n_out, :] * scale
        ).astype(BF16)
        if piece == 0:
            tail = jnp.where(top, gain_sum_ref[...] * scale, 0.0)
        else:
            tail = jnp.zeros((GAIN_ROWS, latent), F32)
        send_ref[half, slot, n_in + n_out :, :] = tail.astype(BF16)


def finish_kernel(bs, place_ref, len_ref, inner_ref, rim_ref, odd_ref, even_ref, out_ref, held_ref):
    rows = inner_ref.shape[0]
    size = odd_ref.shape[0]
    side = place_ref[0]
    held_ref[pl.ds(pl.multiple_of(side * size, bs), size), :] = odd_ref[...]
    held_ref[pl.ds(pl.multiple_of((1 - side) * size, bs), size), :] = even_ref[...]
    blocks = rows // bs
    per = size // bs
    position = lax.broadcasted_iota(jnp.int32, (bs, 1), 0)
    for block in range(blocks):
        here = slice(block * bs, (block + 1) * bs)
        if block < per:
            there = here
        elif block >= blocks - per:
            there = slice(2 * size - rows + here.start, 2 * size - rows + here.stop)
        else:
            out_ref[here, :] = inner_ref[here, :].astype(BF16)
            continue
        valid = (position < len_ref[block]).astype(F32)
        out_ref[here, :] = (rim_ref[there, :] + held_ref[there, :].astype(F32) * valid).astype(BF16)


def unpack_kernel(place_ref, near_ref, far_ref, grad_in_ref, grad_out_ref, gain_ref):
    me = place_ref[1]
    count = 2 * near_ref.shape[0]
    n_in = grad_in_ref.shape[0] // count
    n_out = grad_out_ref.shape[0] // count
    for turn in range(count):
        source = (far_ref if turn % 2 else near_ref).at[turn // 2]
        piece = lax.bitwise_xor(me, turn)
        at_in = pl.ds(pl.multiple_of(piece * n_in, n_in), n_in)
        at_out = pl.ds(pl.multiple_of(piece * n_out, n_out), n_out)
        grad_in_ref[at_in, :] = source[:n_in, :].astype(F32)
        grad_out_ref[at_out, :] = source[n_in : n_in + n_out, :].astype(F32)

        @pl.when(piece == 0)
        def _():
            gain_ref[...] = source[n_in + n_out :, :].astype(F32)[:1, :]


def swap(x, axis, turn):
    count = lax.axis_size(axis)
    return lax.ppermute(x, axis, [(i, i ^ turn) for i in range(count)])


def whole_sum(x, axis):
    count = lax.axis_size(axis)
    if count & (count - 1) == 0:
        parts = [x.astype(F32)] + [swap(x, axis, k).astype(F32) for k in range(1, count)]
        while len(parts) > 1:
            parts = [parts[i] + parts[i + 1] for i in range(0, len(parts), 2)]
        return parts[0].astype(x.dtype)
    moved = [x] + [
        lax.ppermute(x, axis, [(i, (i + k) % count) for i in range(count)]) for k in range(1, count)
    ]
    order = (lax.axis_index(axis) - jnp.arange(count)) % count
    stacked = jnp.stack(moved)[order]
    return jnp.sum(stacked.astype(F32), axis=0).astype(x.dtype)


def vmem(count):
    return [pl.BlockSpec(memory_space=pltpu.VMEM)] * count


def smem(count):
    return [pl.BlockSpec(memory_space=pltpu.SMEM)] * count


def local(node_state, edge_tiles, block_mask, block_len, w_in, w_out, gain, upstream):
    rows, latent = node_state.shape
    offsets, bs = edge_tiles.shape[1:]
    blocks = rows // bs
    rim = (offsets - 1) // 2 * bs
    size = rim
    chunks = rows // size
    dom = lax.axis_size("dom")
    rep = lax.axis_size("rep")
    total = dom * rep
    me = lax.axis_index("dom")
    side = (me * rep + lax.axis_index("rep")) % 2
    place = jnp.stack([side, me]).astype(jnp.int32)
    scale = 1.0 / math.sqrt(rows * total)
    ring = ("dom", "rep")
    even_pairs = [(i, i ^ 1) for i in range(total)]
    odd_pairs = [(i, (i + 1) % total if i % 2 else (i - 1) % total) for i in range(total)]

    position = lax.broadcasted_iota(jnp.int32, (blocks, bs), 1)
    valid = (position < block_len[:, None]).astype(BF16).reshape(rows, 1)
    masked = node_state * valid
    low, high = masked[:rim], masked[rows - rim :]
    to_odd = jnp.where(side == 0, low, high)
    to_even = jnp.where(side == 0, high, low)
    from_even = lax.ppermute(to_even, ring, even_pairs)
    from_odd = lax.ppermute(to_odd, ring, odd_pairs)

    tiles = jnp.transpose(edge_tiles, (1, 0, 2))
    n_in, n_out = w_in.shape[0] // dom, w_out.shape[0] // dom
    piece_rows = n_in + n_out + GAIN_ROWS
    params = pltpu.CompilerParams(vmem_limit_bytes=VMEM_LIMIT)
    new_state, inner, outer, spill_odd, spill_even, send = pl.pallas_call(
        functools.partial(local_kernel, (bs, offsets, chunks, scale)),
        out_shape=(
            jax.ShapeDtypeStruct((rows, latent), BF16),
            jax.ShapeDtypeStruct((rows, latent), F32),
            jax.ShapeDtypeStruct((2 * size, latent), F32),
            jax.ShapeDtypeStruct((rim, latent), BF16),
            jax.ShapeDtypeStruct((rim, latent), BF16),
            jax.ShapeDtypeStruct((2, dom // 2, piece_rows, latent), BF16),
        ),
        in_specs=smem(3) + vmem(8),
        out_specs=tuple(vmem(6)),
        scratch_shapes=[
            pltpu.VMEM((rows + 2 * rim, latent), BF16),
            pltpu.VMEM((size, size + 2 * rim), BF16),
            pltpu.VMEM((rows + 2 * rim, latent), F32),
            pltpu.VMEM(w_in.shape, F32),
            pltpu.VMEM(w_out.shape, F32),
            pltpu.VMEM((1, latent), F32),
        ],
        compiler_params=params,
        name="node_update",
    )(place, block_len, block_mask, node_state, tiles, upstream, w_in, w_out, gain.reshape(1, latent), from_odd, from_even)

    back_even = lax.ppermute(spill_even, ring, even_pairs)
    back_odd = lax.ppermute(spill_odd, ring, odd_pairs)
    grad_state = pl.pallas_call(
        functools.partial(finish_kernel, bs),
        out_shape=jax.ShapeDtypeStruct((rows, latent), BF16),
        in_specs=smem(2) + vmem(4),
        out_specs=vmem(1)[0],
        scratch_shapes=[pltpu.VMEM((2 * size, latent), BF16)],
        compiler_params=params,
        name="finish_state",
    )(place, block_len, inner, outer, back_odd, back_even)

    held = (send[0].astype(F32) + swap(send[1], "dom", 1).astype(F32)).astype(BF16)
    quarter = held[0].astype(F32)
    for k in range(1, dom // 2):
        quarter = quarter + swap(held[k], "dom", 2 * k).astype(F32)
    mine = whole_sum(quarter.astype(BF16), "rep")
    near = jnp.stack([mine] + [swap(mine, "dom", 2 * k) for k in range(1, dom // 2)])
    other = swap(near, "dom", 1)
    grad_w_in, grad_w_out, grad_gain = pl.pallas_call(
        unpack_kernel,
        out_shape=(
            jax.ShapeDtypeStruct(w_in.shape, F32),
            jax.ShapeDtypeStruct(w_out.shape, F32),
            jax.ShapeDtypeStruct((1, latent), F32),
        ),
        in_specs=smem(1) + vmem(2),
        out_specs=tuple(vmem(3)),
        compiler_params=params,
        name="unpack_sums",
    )(place, near, other)
    return new_state, grad_state, grad_w_in, grad_w_out, grad_gain.reshape(latent)


def solution(mesh):
    placed = (
        P(("dom", "rep"), None),
        P(("dom", "rep"), None, None),
        P(("dom", "rep"), None),
        P(("dom", "rep")),
        P(),
        P(),
        P(),
        P(("dom", "rep"), None),
    )
    return jax.shard_map(
        local,
        mesh=mesh,
        in_specs=placed,
        out_specs=(P(("dom", "rep"), None), P(("dom", "rep"), None), P(), P(), P()),
        check_vma=False,
    )
```

time: 234 us -> 60.5 us (0.26)
  waiting for transfers between devices: 128 us -> 24.4 us
  blocking collectives: 37.7 us -> 0 us
  between operations: 14.3 us -> 0.82 us
  other arithmetic: 15.7 us -> 2.31 us
  local copies, waits for them, and re-layouts: 14.4 us -> 1.37 us
  matrix products: 12.2 us -> 0 us
  Pallas kernels: 0 us -> 10.2 us
  starting transfers between devices: 11.8 us -> 21.3 us
    psum x1 -> x0, waiting for transfers between devices: 123 us -> none  [local(): lax.psum((in_terms, out_terms, gain_terms), ('dom', 'rep'))]
    psum x1 -> x0, blocking collectives: 37.7 us -> none  [local(): lax.psum((in_terms, out_terms, gain_terms), ('dom', 'rep'))]
    ppermute x4 -> x15, waiting for transfers between devices: 4.01 us -> 24.4 us  [the longest x11 11.1 us: swap(): return lax.ppermute(x, axis, [(i, i ^ turn) for i in range(count)])]
    dot_general x16 -> x0, matrix products: 12.2 us -> none  [the longest x5 6.68 us: local(): jnp.einsum('bij,bil->bjl', coupled[:, :, offset, :], grad_blocks, preferr...]
    pallas_call x0 -> x3, Pallas kernels: none -> 10.2 us  [the longest x1 7.25 us: local(): pl.pallas_call(functools.partial(local_kernel, (bs, offsets, chunks, scal...]
    ppermute x4 -> x15, starting transfers between devices: 11.7 us -> 21.3 us  [the longest x11 11.7 us: swap(): return lax.ppermute(x, axis, [(i, i ^ turn) for i in range(count)])]
    unnamed x21 -> x16, local copies, waits for them, and re-layouts: 8.74 us -> 1.34 us
    mul x5 -> x1, other arithmetic: 7.36 us -> 1.24 us  [local(): masked = node_state * valid]
  transfers between devices with their start and end apart: 5 -> 15, of which waited for: 2 -> 12; matrix products, arithmetic and copies ran while one was open for 5% -> 0% of each run, Pallas kernels for 0% -> 2%
where the time goes in v1:
time: 60.5 us; the launch traced here: 60.3 us
  waiting for transfers between devices  24.4 us (40%)
  starting transfers between devices  21.3 us (35%)
  Pallas kernels  10.2 us (17%)
  other arithmetic  2.31 us (4%)
  local copies, waits for them, and re-layouts  1.37 us (2%)
  between operations  0.82 us (1%)
    ppermute x11, starting transfers between devices, swap(): return lax.ppermute(x, axis, [(i, i ^ turn) for i in range(count)])  11.7 us
    ppermute x11, waiting for transfers between devices, swap(): return lax.ppermute(x, axis, [(i, i ^ turn) for i in range(count)])  11.1 us
    pallas_call x1, Pallas kernels, local(): pl.pallas_call(functools.partial(local_kernel, (bs, offsets, chunks, scal...  7.25 us
    ppermute x1, waiting for transfers between devices, local(): back_odd = lax.ppermute(spill_odd, ring, odd_pairs)  6.48 us
    ppermute x1, waiting for transfers between devices, local(): from_odd = lax.ppermute(to_odd, ring, odd_pairs)  5.8 us
    ppermute x1, starting transfers between devices, local(): from_odd = lax.ppermute(to_odd, ring, odd_pairs)  3.52 us
    ppermute x1, starting transfers between devices, local(): from_even = lax.ppermute(to_even, ring, even_pairs)  3.09 us
    ppermute x1, starting transfers between devices, local(): back_odd = lax.ppermute(spill_odd, ring, odd_pairs)  2.96 us
  transfers between devices with their start and end apart: 15, of which 12 were waited for; matrix products, arithmetic and copies ran while one was open for 0% of the time, Pallas kernels for 2%

profile of v1, /device:TPU:0, one launch (start us, length us, event | category | flops | bytes accessed | tf_op | source)
XLA Modules:
  0.0 60.3 jit_solution(2787957668426674683)
XLA Ops:
  0.7 0.8 %fusion.5 = bf16[1024]{0:T(1024)(128)(2,1)S(1)} fusion(s32[8]{0:T(128)} %len_ref.3), kind=kLoop, calls=%fused_computation.18 | loop fusion | flops 2048 | bytes 2080 | tf_op jit(solution)/shard_map/convert_element_type | solution.py:253
  1.5 1.2 %broadcast_multiply_fusion = bf16[1024,256]{1,0:T(8,128)(2,1)S(1)} fusion(bf16[1024,256]{1,0:T(8,128)(2,1)} %state_ref.1, bf16[1024]{0:T(1024)(128)(2,1)S(1)} %fusion.5), kind=kLoop, calls=%fused_computation.2 | loop fusion | flops 262144 | bytes 1050624 | tf_op jit(solution)/shard_map/mul | solution.py:254
  2.8 3.1 %collective-permute-start.1 = (bf16[256,256]{1,0:T(8,128)(2,1)S(1)}, bf16[256,256]{1,0:T(8,128)(2,1)S(1)}, u32[]{:S(2)}, u32[]{:S(2)}) collective-permute-start(bf16[256,256]{1,0:T(8,128)(2,1)S(1)} %get-tuple-element.23), channel_id=1, source_target_pairs={{0,1},{1,0},{2,3},{3,2},{4,5},{5,4},{6,7},{7,6},{8,9},{9,8},{10,11... | collective-permute-start | bytes 393224 | tf_op jit(solution)/shard_map/ppermute | solution.py:258
  5.9 3.5 %collective-permute-start = (bf16[256,256]{1,0:T(8,128)(2,1)S(1)}, bf16[256,256]{1,0:T(8,128)(2,1)S(1)}, u32[]{:S(2)}, u32[]{:S(2)}) collective-permute-start(bf16[256,256]{1,0:T(8,128)(2,1)S(1)} %get-tuple-element.24), channel_id=1, source_target_pairs={{0,31},{1,2},{2,1},{3,4},{4,3},{5,6},{6,5},{7,8},{8,7},{9,10},{10,... | collective-permute-start | bytes 393224 | tf_op jit(solution)/shard_map/ppermute | solution.py:259
  9.5 5.8 %collective-permute-done.odd_ref = bf16[256,256]{1,0:T(8,128)(2,1)S(1)} collective-permute-done((bf16[256,256]{1,0:T(8,128)(2,1)S(1)}, bf16[256,256]{1,0:T(8,128)(2,1)S(1)}, u32[]{:S(2)}, u32[]{:S(2)}) %collective-permute-start) | collective-permute-done | bytes 131104 | tf_op jit(solution)/shard_map/ppermute | solution.py:259
  15.4 1.3 %copy-done.1 = bf16[1024,5,128]{2,0,1:T(8,128)(2,1)S(1)} copy-done((bf16[1024,5,128]{2,0,1:T(8,128)(2,1)S(1)}, bf16[1024,5,128]{2,0,1:T(8,128)(2,1)}, u32[]{:S(2)}) %copy-start.1) | copy-done | bytes 1310744
  16.7 7.2 %node_update.1 = (bf16[1024,256]{1,0:T(8,128)(2,1)}, f32[1024,256]{1,0:T(8,128)S(1)}, f32[512,256]{1,0:T(8,128)S(1)}, bf16[256,256]{1,0:T(8,128)(2,1)S(1)}, bf16...) custom-call(s32[2]{0:T(128)S(1)} %pad_add_fusion.place_ref, s32[8]{0:T(128)S(1)} %copy-done.5, ...), custom_call_target="tpu_custom_call" | custom-call | tf_op jit(solution)/shard_map/node_update/pallas_call | solution.py:265
  24.0 1.5 %collective-permute-done.4 = bf16[4,104,256]{2,1,0:T(8,128)(2,1)S(1)} collective-permute-done((bf16[4,104,256]{2,1,0:T(8,128)(2,1)S(1)}, bf16[4,104,256]{2,1,0:T(8,128)(2,1)S(1)}, u32[]{:S(2)}, u32[]{:S(2)}) %collective-permute-start.4) | collective-permute-done | bytes 213024 | tf_op jit(solution)/shard_map/ppermute | solution.py:208
  26.3 2.4 %collective-permute-start.7 = (bf16[104,256]{1,0:T(8,128)(2,1)S(1)}, bf16[104,256]{1,0:T(8,128)(2,1)S(1)}, u32[]{:S(2)}, u32[]{:S(2)}) collective-permute-start(bf16[104,256]{1,0:T(8,128)(2,1)S(1)} %get-tuple-element.26), channel_id=1, source_target_pairs={{0,24},{4,28},{8,16},{12,20},{16,8},{20,12},{24,0},{28,4},{1,25},{... | collective-permute-start | bytes 159752 | tf_op jit(solution)/shard_map/ppermute | solution.py:208
  29.9 1.9 %collective-permute-done.7 = bf16[104,256]{1,0:T(8,128)(2,1)S(1)} collective-permute-done((bf16[104,256]{1,0:T(8,128)(2,1)S(1)}, bf16[104,256]{1,0:T(8,128)(2,1)S(1)}, u32[]{:S(2)}, u32[]{:S(2)}) %collective-permute-start.7) | collective-permute-done | bytes 53280 | tf_op jit(solution)/shard_map/ppermute | solution.py:208
  31.8 1.0 %collective-permute-done.6 = bf16[104,256]{1,0:T(8,128)(2,1)S(1)} collective-permute-done((bf16[104,256]{1,0:T(8,128)(2,1)S(1)}, bf16[104,256]{1,0:T(8,128)(2,1)S(1)}, u32[]{:S(2)}, u32[]{:S(2)}) %collective-permute-start.6) | collective-permute-done | bytes 53280 | tf_op jit(solution)/shard_map/ppermute | solution.py:208
  32.8 1.2 %collective-permute-start.10 = (bf16[104,256]{1,0:T(8,128)(2,1)S(1)}, bf16[104,256]{1,0:T(8,128)(2,1)S(1)}, u32[]{:S(2)}, u32[]{:S(2)}) collective-permute-start(bf16[104,256]{1,0:T(8,128)(2,1)S(1)} %fusion.3), channel_id=1, source_target_pairs={{0,3},{1,2},{2,1},{3,0},{4,7},{5,6},{6,5},{7,4},{8,11},{9,10},{10,... | collective-permute-start | bytes 159752 | tf_op jit(solution)/shard_map/ppermute | solution.py:208
  34.2 3.1 %collective-permute-start.8 = (bf16[104,256]{1,0:T(8,128)(2,1)S(1)}, bf16[104,256]{1,0:T(8,128)(2,1)S(1)}, u32[]{:S(2)}, u32[]{:S(2)}) collective-permute-start(bf16[104,256]{1,0:T(8,128)(2,1)S(1)} %fusion.3), channel_id=1, source_target_pairs={{0,1},{1,0},{2,3},{3,2},{4,5},{5,4},{6,7},{7,6},{8,9},{9,8},{10,11... | collective-permute-start | bytes 159752 | tf_op jit(solution)/shard_map/ppermute | solution.py:208
  37.3 2.0 %collective-permute-done.10 = bf16[104,256]{1,0:T(8,128)(2,1)S(1)} collective-permute-done((bf16[104,256]{1,0:T(8,128)(2,1)S(1)}, bf16[104,256]{1,0:T(8,128)(2,1)S(1)}, u32[]{:S(2)}, u32[]{:S(2)}) %collective-permute-start.10) | collective-permute-done | bytes 53280 | tf_op jit(solution)/shard_map/ppermute | solution.py:208
  40.2 1.2 %collective-permute-start.13 = (bf16[104,256]{1,0:T(8,128)(2,1)S(1)}, bf16[104,256]{1,0:T(8,128)(2,1)S(1)}, u32[]{:S(2)}, u32[]{:S(2)}) collective-permute-start(bf16[104,256]{1,0:T(8,128)(2,1)S(1)} %add_convert_fusion), channel_id=1, source_target_pairs={{0,24},{4,28},{8,16},{12,20},{16,8},{20,12},{24,0},{28,4},{1,25},{... | collective-permute-start | bytes 159752 | tf_op jit(solution)/shard_map/ppermute | solution.py:208
  41.4 1.3 %collective-permute-start.12 = (bf16[104,256]{1,0:T(8,128)(2,1)S(1)}, bf16[104,256]{1,0:T(8,128)(2,1)S(1)}, u32[]{:S(2)}, u32[]{:S(2)}) collective-permute-start(bf16[104,256]{1,0:T(8,128)(2,1)S(1)} %add_convert_fusion), channel_id=1, source_target_pairs={{0,16},{4,20},{8,24},{12,28},{16,0},{20,4},{24,8},{28,12},{1,17},{... | collective-permute-start | bytes 159752 | tf_op jit(solution)/shard_map/ppermute | solution.py:208
  42.7 1.0 %collective-permute-start.11 = (bf16[104,256]{1,0:T(8,128)(2,1)S(1)}, bf16[104,256]{1,0:T(8,128)(2,1)S(1)}, u32[]{:S(2)}, u32[]{:S(2)}) collective-permute-start(bf16[104,256]{1,0:T(8,128)(2,1)S(1)} %add_convert_fusion), channel_id=1, source_target_pairs={{0,8},{4,12},{8,0},{12,4},{16,24},{20,28},{24,16},{28,20},{1,9},{5... | collective-permute-start | bytes 159752 | tf_op jit(solution)/shard_map/ppermute | solution.py:208
  43.7 1.6 %collective-permute-done.13 = bf16[104,256]{1,0:T(8,128)(2,1)S(1)} collective-permute-done((bf16[104,256]{1,0:T(8,128)(2,1)S(1)}, bf16[104,256]{1,0:T(8,128)(2,1)S(1)}, u32[]{:S(2)}, u32[]{:S(2)}) %collective-permute-start.13) | collective-permute-done | bytes 53280 | tf_op jit(solution)/shard_map/ppermute | solution.py:208
  45.8 1.0 %collective-permute-done.11 = bf16[104,256]{1,0:T(8,128)(2,1)S(1)} collective-permute-done((bf16[104,256]{1,0:T(8,128)(2,1)S(1)}, bf16[104,256]{1,0:T(8,128)(2,1)S(1)}, u32[]{:S(2)}, u32[]{:S(2)}) %collective-permute-start.11) | collective-permute-done | bytes 53280 | tf_op jit(solution)/shard_map/ppermute | solution.py:208
  46.9 3.0 %collective-permute-start.2 = (bf16[256,256]{1,0:T(8,128)(2,1)S(1)}, bf16[256,256]{1,0:T(8,128)(2,1)S(1)}, u32[]{:S(2)}, u32[]{:S(2)}) collective-permute-start(bf16[256,256]{1,0:T(8,128)(2,1)S(1)} %get-tuple-element.17), channel_id=1, source_target_pairs={{0,31},{1,2},{2,1},{3,4},{4,3},{5,6},{6,5},{7,8},{8,7},{9,10},{10,... | collective-permute-start | bytes 393224 | tf_op jit(solution)/shard_map/ppermute | solution.py:290
  49.9 6.5 %collective-permute-done.2.odd_ref = bf16[256,256]{1,0:T(8,128)(2,1)S(1)} collective-permute-done((bf16[256,256]{1,0:T(8,128)(2,1)S(1)}, bf16[256,256]{1,0:T(8,128)(2,1)S(1)}, u32[]{:S(2)}, u32[]{:S(2)}) %collective-permute-start.2) | collective-permute-done | bytes 131104 | tf_op jit(solution)/shard_map/ppermute | solution.py:290
  56.4 1.0 %collective-permute-done.3.even_ref = bf16[256,256]{1,0:T(8,128)(2,1)S(1)} collective-permute-done((bf16[256,256]{1,0:T(8,128)(2,1)S(1)}, bf16[256,256]{1,0:T(8,128)(2,1)S(1)}, u32[]{:S(2)}, u32[]{:S(2)}) %collective-permute-start.3) | collective-permute-done | bytes 131104 | tf_op jit(solution)/shard_map/ppermute | solution.py:289
  57.4 1.5 %finish_state.1 = bf16[1024,256]{1,0:T(8,128)(2,1)} custom-call(s32[2]{0:T(128)S(1)} %pad_add_fusion.place_ref, s32[8]{0:T(128)S(1)} %copy-done.5, f32[1024,256]{1,0:T(8,128)S(1)} %get-tuple-element.15.inner_ref, f32[512,256]{1,0:T(8,128)S(1)} %get-tuple-element.16.rim_ref, bf16[256,256]{1,0:T(8,128)(2,1)S(1)} %collective-permute-done.2.odd_ref, ...), custom_call_target="tpu_custom_call" | custom-call | tf_op jit(solution)/shard_map/finish_state/pallas_call | solution.py:291
  58.8 1.5 %unpack_sums.1 = (f32[512,256]{1,0:T(8,128)}, f32[256,256]{1,0:T(8,128)}, f32[1,256]{1,0:T(1,128)}) custom-call(s32[2]{0:T(128)S(1)} %pad_add_fusion.place_ref, bf16[4,104,256]{2,1,0:T(8,128)(2,1)S(1)} %pad_maximum_fusion.near_ref, bf16[4,104,256]{2,1,0:T(8,128)(2,1)S(1)} %collective-permute-done.14.far_ref), custom_call_target="tpu_custom_call" | custom-call | tf_op jit(solution)/shard_map/unpack_sums/pallas_call | solution.py:308
  (35 shorter events, 3.9 us)
Async XLA Ops:
  0.6 14.7 %copy-start.5 = (s32[8]{0:T(128)S(1)}, s32[8]{0:T(128)}, u32[]{:S(2)}) copy-start(s32[8]{0:T(128)} %len_ref.3) | copy-start | bytes 100
  0.6 14.7 %copy-start = (bf16[1024,256]{1,0:T(8,128)(2,1)S(1)}, bf16[1024,256]{1,0:T(8,128)(2,1)}, u32[]{:S(2)}) copy-start(bf16[1024,256]{1,0:T(8,128)(2,1)} %state_ref.1) | copy-start | bytes 1572868
  0.7 14.7 %copy-start.2 = (bf16[1024,256]{1,0:T(8,128)(2,1)S(1)}, bf16[1024,256]{1,0:T(8,128)(2,1)}, u32[]{:S(2)}) copy-start(bf16[1024,256]{1,0:T(8,128)(2,1)} %up_ref.1) | copy-start | bytes 1572868
  0.7 14.7 %copy-start.7 = (f32[256]{0:T(256)S(1)}, f32[256]{0:T(256)}, u32[]{:S(2)}) copy-start(f32[256]{0:T(256)} %param.14) | copy-start | bytes 3076
  0.7 14.7 %copy-start.4 = (bf16[256,256]{1,0:T(8,128)(2,1)S(1)}, bf16[256,256]{1,0:T(8,128)(2,1)}, u32[]{:S(2)}) copy-start(bf16[256,256]{1,0:T(8,128)(2,1)} %w_out_ref.1) | copy-start | bytes 393220
  0.7 14.7 %copy-start.3 = (bf16[512,256]{1,0:T(8,128)(2,1)S(1)}, bf16[512,256]{1,0:T(8,128)(2,1)}, u32[]{:S(2)}) copy-start(bf16[512,256]{1,0:T(8,128)(2,1)} %w_in_ref.1) | copy-start | bytes 786436
  0.7 14.7 %copy-start.6 = (s32[8,5]{1,0:T(8,128)S(1)}, s32[8,5]{1,0:T(8,128)}, u32[]{:S(2)}) copy-start(s32[8,5]{1,0:T(8,128)} %mask_ref.1) | copy-start | bytes 484
  2.8 6.7 %collective-permute-start.1 = (bf16[256,256]{1,0:T(8,128)(2,1)S(1)}, bf16[256,256]{1,0:T(8,128)(2,1)S(1)}, u32[]{:S(2)}, u32[]{:S(2)}) collective-permute-start(bf16[256,256]{1,0:T(8,128)(2,1)S(1)} %get-tuple-element.23), channel_id=1, source_target_pairs={{0,1},{1,0},{2,3},{3,2},{4,5},{5,4},{6,7},{7,6},{8,9},{9,8},{10,11... | collective-permute-start | bytes 393224 | tf_op jit(solution)/shard_map/ppermute | solution.py:258
  5.9 9.4 %collective-permute-start = (bf16[256,256]{1,0:T(8,128)(2,1)S(1)}, bf16[256,256]{1,0:T(8,128)(2,1)S(1)}, u32[]{:S(2)}, u32[]{:S(2)}) collective-permute-start(bf16[256,256]{1,0:T(8,128)(2,1)S(1)} %get-tuple-element.24), channel_id=1, source_target_pairs={{0,31},{1,2},{2,1},{3,4},{4,3},{5,6},{6,5},{7,8},{8,7},{9,10},{10,... | collective-permute-start | bytes 393224 | tf_op jit(solution)/shard_map/ppermute | solution.py:259
  15.4 1.3 %copy-start.1 = (bf16[1024,5,128]{2,0,1:T(8,128)(2,1)S(1)}, bf16[1024,5,128]{2,0,1:T(8,128)(2,1)}, u32[]{:S(2)}) copy-start(bf16[1024,5,128]{2,0,1:T(8,128)(2,1)} %param.9) | copy-start | bytes 3932164
  23.9 1.5 %collective-permute-start.4 = (bf16[4,104,256]{2,1,0:T(8,128)(2,1)S(1)}, bf16[4,104,256]{2,1,0:T(8,128)(2,1)S(1)}, u32[]{:S(2)}, u32[]{:S(2)}) collective-permute-start(bf16[4,104,256]{2,1,0:T(8,128)(2,1)S(1)} %slice_bitcast_fusion), channel_id=1, source_target_pairs={{0,4},{4,0},{8,12},{12,8},{16,20},{20,16},{24,28},{28,24},{1,5},{5... | collective-permute-start | bytes 638984 | tf_op jit(solution)/shard_map/ppermute | solution.py:208
  25.6 4.3 %collective-permute-start.5 = (bf16[104,256]{1,0:T(8,128)(2,1)S(1)}, bf16[104,256]{1,0:T(8,128)(2,1)S(1)}, u32[]{:S(2)}, u32[]{:S(2)}) collective-permute-start(bf16[104,256]{1,0:T(8,128)(2,1)S(1)} %get-tuple-element.25), channel_id=1, source_target_pairs={{0,8},{4,12},{8,0},{12,4},{16,24},{20,28},{24,16},{28,20},{1,9},{5... | collective-permute-start | bytes 159752 | tf_op jit(solution)/shard_map/ppermute | solution.py:208
  26.3 5.5 %collective-permute-start.7 = (bf16[104,256]{1,0:T(8,128)(2,1)S(1)}, bf16[104,256]{1,0:T(8,128)(2,1)S(1)}, u32[]{:S(2)}, u32[]{:S(2)}) collective-permute-start(bf16[104,256]{1,0:T(8,128)(2,1)S(1)} %get-tuple-element.26), channel_id=1, source_target_pairs={{0,24},{4,28},{8,16},{12,20},{16,8},{20,12},{24,0},{28,4},{1,25},{... | collective-permute-start | bytes 159752 | tf_op jit(solution)/shard_map/ppermute | solution.py:208
  28.7 4.1 %collective-permute-start.6 = (bf16[104,256]{1,0:T(8,128)(2,1)S(1)}, bf16[104,256]{1,0:T(8,128)(2,1)S(1)}, u32[]{:S(2)}, u32[]{:S(2)}) collective-permute-start(bf16[104,256]{1,0:T(8,128)(2,1)S(1)} %get-tuple-element.27), channel_id=1, source_target_pairs={{0,16},{4,20},{8,24},{12,28},{16,0},{20,4},{24,8},{28,12},{1,17},{... | collective-permute-start | bytes 159752 | tf_op jit(solution)/shard_map/ppermute | solution.py:208
  32.8 6.5 %collective-permute-start.10 = (bf16[104,256]{1,0:T(8,128)(2,1)S(1)}, bf16[104,256]{1,0:T(8,128)(2,1)S(1)}, u32[]{:S(2)}, u32[]{:S(2)}) collective-permute-start(bf16[104,256]{1,0:T(8,128)(2,1)S(1)} %fusion.3), channel_id=1, source_target_pairs={{0,3},{1,2},{2,1},{3,0},{4,7},{5,6},{6,5},{7,4},{8,11},{9,10},{10,... | collective-permute-start | bytes 159752 | tf_op jit(solution)/shard_map/ppermute | solution.py:208
  34.1 6.0 %collective-permute-start.9 = (bf16[104,256]{1,0:T(8,128)(2,1)S(1)}, bf16[104,256]{1,0:T(8,128)(2,1)S(1)}, u32[]{:S(2)}, u32[]{:S(2)}) collective-permute-start(bf16[104,256]{1,0:T(8,128)(2,1)S(1)} %fusion.3), channel_id=1, source_target_pairs={{0,2},{1,3},{2,0},{3,1},{4,6},{5,7},{6,4},{7,5},{8,10},{9,11},{10,... | collective-permute-start | bytes 159752 | tf_op jit(solution)/shard_map/ppermute | solution.py:208
  34.2 5.9 %collective-permute-start.8 = (bf16[104,256]{1,0:T(8,128)(2,1)S(1)}, bf16[104,256]{1,0:T(8,128)(2,1)S(1)}, u32[]{:S(2)}, u32[]{:S(2)}) collective-permute-start(bf16[104,256]{1,0:T(8,128)(2,1)S(1)} %fusion.3), channel_id=1, source_target_pairs={{0,1},{1,0},{2,3},{3,2},{4,5},{5,4},{6,7},{7,6},{8,9},{9,8},{10,11... | collective-permute-start | bytes 159752 | tf_op jit(solution)/shard_map/ppermute | solution.py:208
  40.2 5.1 %collective-permute-start.13 = (bf16[104,256]{1,0:T(8,128)(2,1)S(1)}, bf16[104,256]{1,0:T(8,128)(2,1)S(1)}, u32[]{:S(2)}, u32[]{:S(2)}) collective-permute-start(bf16[104,256]{1,0:T(8,128)(2,1)S(1)} %add_convert_fusion), channel_id=1, source_target_pairs={{0,24},{4,28},{8,16},{12,20},{16,8},{20,12},{24,0},{28,4},{1,25},{... | collective-permute-start | bytes 159752 | tf_op jit(solution)/shard_map/ppermute | solution.py:208
  41.4 4.4 %collective-permute-start.12 = (bf16[104,256]{1,0:T(8,128)(2,1)S(1)}, bf16[104,256]{1,0:T(8,128)(2,1)S(1)}, u32[]{:S(2)}, u32[]{:S(2)}) collective-permute-start(bf16[104,256]{1,0:T(8,128)(2,1)S(1)} %add_convert_fusion), channel_id=1, source_target_pairs={{0,16},{4,20},{8,24},{12,28},{16,0},{20,4},{24,8},{28,12},{1,17},{... | collective-permute-start | bytes 159752 | tf_op jit(solution)/shard_map/ppermute | solution.py:208
  42.7 4.1 %collective-permute-start.11 = (bf16[104,256]{1,0:T(8,128)(2,1)S(1)}, bf16[104,256]{1,0:T(8,128)(2,1)S(1)}, u32[]{:S(2)}, u32[]{:S(2)}) collective-permute-start(bf16[104,256]{1,0:T(8,128)(2,1)S(1)} %add_convert_fusion), channel_id=1, source_target_pairs={{0,8},{4,12},{8,0},{12,4},{16,24},{20,28},{24,16},{28,20},{1,9},{5... | collective-permute-start | bytes 159752 | tf_op jit(solution)/shard_map/ppermute | solution.py:208
  46.8 12.0 %collective-permute-start.14 = (bf16[4,104,256]{2,1,0:T(8,128)(2,1)S(1)}, bf16[4,104,256]{2,1,0:T(8,128)(2,1)S(1)}, u32[]{:S(2)}, u32[]{:S(2)}) collective-permute-start(bf16[4,104,256]{2,1,0:T(8,128)(2,1)S(1)} %pad_maximum_fusion.near_ref), channel_id=1, source_target_pairs={{0,4},{4,0},{8,12},{12,8},{16,20},{20,16},{24,28},{28,24},{1,5},{5... | collective-permute-start | bytes 638984 | tf_op jit(solution)/shard_map/ppermute | solution.py:208
  46.9 9.4 %collective-permute-start.2 = (bf16[256,256]{1,0:T(8,128)(2,1)S(1)}, bf16[256,256]{1,0:T(8,128)(2,1)S(1)}, u32[]{:S(2)}, u32[]{:S(2)}) collective-permute-start(bf16[256,256]{1,0:T(8,128)(2,1)S(1)} %get-tuple-element.17), channel_id=1, source_target_pairs={{0,31},{1,2},{2,1},{3,4},{4,3},{5,6},{6,5},{7,8},{8,7},{9,10},{10,... | collective-permute-start | bytes 393224 | tf_op jit(solution)/shard_map/ppermute | solution.py:290
  49.9 7.5 %collective-permute-start.3 = (bf16[256,256]{1,0:T(8,128)(2,1)S(1)}, bf16[256,256]{1,0:T(8,128)(2,1)S(1)}, u32[]{:S(2)}, u32[]{:S(2)}) collective-permute-start(bf16[256,256]{1,0:T(8,128)(2,1)S(1)} %get-tuple-element.18), channel_id=1, source_target_pairs={{0,1},{1,0},{2,3},{3,2},{4,5},{5,4},{6,7},{7,6},{8,9},{9,8},{10,11... | collective-permute-start | bytes 393224 | tf_op jit(solution)/shard_map/ppermute | solution.py:289

commit v2 on v1

v2 whole, which is shorter than its diff:
```python
import functools
import math

import jax
import jax.numpy as jnp
from jax import lax
from jax.experimental import pallas as pl
from jax.experimental.pallas import tpu as pltpu
from jax.sharding import PartitionSpec as P

EPSILON = 1e-05
F32 = jnp.float32
BF16 = jnp.bfloat16
GAIN_ROWS = 8
VMEM_LIMIT = 40 * 1024 * 1024


def dot(a, b, contract):
    return lax.dot_general(a, b, ((contract[:1], contract[1:]), ((), ())), preferred_element_type=F32)


def sublane(bs):
    return lax.broadcasted_iota(jnp.int32, (bs, 1), 0)


def validity(len_ref, first, count, bs):
    return jnp.concatenate(
        [(sublane(bs) < len_ref[first + j]).astype(F32) for j in range(count)], axis=0
    )


def pack_kernel(bs, place_ref, len_ref, state_ref, odd_ref, even_ref, held_ref, sems):
    rows = state_ref.shape[0]
    rim = odd_ref.shape[0]
    per = rim // bs
    low = pltpu.make_async_copy(state_ref.at[pl.ds(0, rim), :], held_ref.at[0], sems.at[0])
    high = pltpu.make_async_copy(state_ref.at[pl.ds(rows - rim, rim), :], held_ref.at[1], sems.at[1])
    low.start()
    high.start()
    side = place_ref[0]
    low.wait()
    high.wait()
    blocks = rows // bs
    for j in range(per):
        here = slice(j * bs, (j + 1) * bs)
        top = held_ref[0, here, :] * (sublane(bs) < len_ref[j]).astype(F32).astype(BF16)
        end = held_ref[1, here, :] * (sublane(bs) < len_ref[blocks - per + j]).astype(F32).astype(BF16)
        odd_ref[here, :] = jnp.where(side == 0, top, end)
        even_ref[here, :] = jnp.where(side == 0, end, top)


def fill_band(band_ref, tiles_ref, mask_ref, first, per, bs, offsets):
    for j in range(per):
        row = slice(j * bs, (j + 1) * bs)
        for column in range(per + offsets - 1):
            offset = column - j
            cols = slice(column * bs, (column + 1) * bs)
            if 0 <= offset < offsets:
                tile = tiles_ref[offset, (first + j) * bs : (first + j + 1) * bs, :]
                band_ref[row, cols] = tile * mask_ref[first + j, offset].astype(F32).astype(BF16)
            else:
                band_ref[row, cols] = jnp.zeros((bs, bs), BF16)


def node_rows(state, message, direct_part, upstream, valid, w_in_ref, w_out_ref, gain):
    latent = state.shape[1]
    preact = direct_part + dot(message, w_in_ref[latent:, :], (1, 0))
    sigma = jax.nn.sigmoid(preact)
    activated = (preact * sigma).astype(BF16)
    output = dot(activated, w_out_ref[...], (1, 0))
    centred = output - jnp.mean(output, axis=1, keepdims=True)
    inverse = lax.rsqrt(jnp.mean(centred * centred, axis=1, keepdims=True) + EPSILON)
    normed = centred * inverse
    new_state = (state.astype(F32) + gain * normed * valid).astype(BF16)
    masked_up = upstream * valid
    gain_sum = jnp.sum(masked_up * normed, axis=0, keepdims=True)
    scaled = masked_up * gain
    grad_output = (
        inverse
        * (
            scaled
            - jnp.mean(scaled, axis=1, keepdims=True)
            - normed * jnp.mean(scaled * normed, axis=1, keepdims=True)
        )
    ).astype(BF16)
    grad_act = dot(grad_output, w_out_ref[...], (1, 1))
    slope = sigma * (1.0 + preact * (1.0 - sigma))
    grad_pre = (grad_act * slope).astype(BF16)
    return new_state, gain_sum, activated, grad_output, grad_pre


def inner_kernel(
    cfg,
    len_ref,
    mask_ref,
    state_ref,
    tiles_ref,
    up_ref,
    w_in_ref,
    w_out_ref,
    gain_ref,
    new_ref,
    own_ref,
    spread_ref,
    grad_in_ref,
    grad_out_ref,
    gain_sum_ref,
    rim_band_ref,
    rim_message_ref,
    rim_direct_ref,
    ext_ref,
    band_ref,
):
    bs, offsets = cfg
    rim = (offsets - 1) // 2 * bs
    rows, latent = state_ref.shape
    per = rim // bs
    blocks = rows // bs
    inside = rows - 2 * rim
    width = 3 * rim

    ext_ref[...] = (state_ref[...].astype(F32) * validity(len_ref, 0, blocks, bs)).astype(BF16)
    message = []
    for chunk in range(1, rows // rim - 1):
        band = band_ref.at[chunk - 1]
        fill_band(band, tiles_ref, mask_ref, chunk * per, per, bs, offsets)
        message.append(dot(band[...], ext_ref[(chunk - 1) * rim : (chunk - 1) * rim + width, :], (1, 0)))
    inner = slice(rim, rows - rim)
    valid = validity(len_ref, per, blocks - 2 * per, bs)
    message = (jnp.concatenate(message, axis=0) * valid).astype(BF16)
    state = state_ref[inner, :]
    upstream = up_ref[inner, :].astype(F32)
    direct_part = dot(state, w_in_ref[:latent, :], (1, 0))
    new_state, gain_sum, activated, grad_output, grad_pre = node_rows(
        state, message, direct_part, upstream, valid, w_in_ref, w_out_ref, gain_ref[...]
    )
    new_ref[...] = new_state
    gain_sum_ref[...] = gain_sum
    grad_out_ref[...] = dot(activated, grad_output, (0, 0))
    grad_in_ref[:latent, :] = dot(state, grad_pre, (0, 0))
    grad_in_ref[latent:, :] = dot(message, grad_pre, (0, 0))
    own_ref[...] = upstream + dot(grad_pre, w_in_ref[:latent, :], (1, 1))
    grad_message = dot(grad_pre, w_in_ref[latent:, :], (1, 1)).astype(BF16)
    grad_message = (grad_message.astype(F32) * valid).astype(BF16)
    spread_ref[...] = jnp.zeros_like(spread_ref)
    for chunk in range(1, rows // rim - 1):
        reach = slice((chunk - 1) * rim, (chunk - 1) * rim + width)
        spread_ref[reach, :] += dot(
            band_ref[chunk - 1], grad_message[(chunk - 1) * rim : chunk * rim, :], (0, 0)
        )

    for end in range(2):
        first = end * (blocks - per)
        band = rim_band_ref.at[end]
        fill_band(band, tiles_ref, mask_ref, first, per, bs, offsets)
        here = slice(end * rim, (end + 1) * rim)
        if end == 0:
            rim_message_ref[here, :] = dot(band[:, rim:], ext_ref[: 2 * rim, :], (1, 0))
        else:
            rim_message_ref[here, :] = dot(band[:, : 2 * rim], ext_ref[rows - 2 * rim :, :], (1, 0))
        rim_direct_ref[here, :] = dot(
            state_ref[first * bs : first * bs + rim, :], w_in_ref[:latent, :], (1, 0)
        )


def rim_kernel(
    cfg,
    place_ref,
    len_ref,
    state_ref,
    up_ref,
    w_in_ref,
    w_out_ref,
    gain_ref,
    band_ref,
    message_ref,
    direct_ref,
    inner_in_ref,
    inner_out_ref,
    inner_gain_ref,
    odd_ref,
    even_ref,
    send_ref,
    spill_odd_ref,
    spill_even_ref,
    new_ref,
    own_ref,
    spread_ref,
    grad_in_ref,
    grad_out_ref,
):
    bs, scale = cfg
    rows, latent = state_ref.shape
    rim = odd_ref.shape[0]
    per = rim // bs
    blocks = rows // bs
    side = place_ref[0]
    me = place_ref[1]
    odd = odd_ref[...]
    even = even_ref[...]
    low = jnp.where(side == 0, odd, even)
    high = jnp.where(side == 0, even, odd)
    valid = jnp.concatenate(
        [validity(len_ref, 0, per, bs), validity(len_ref, blocks - per, per, bs)], axis=0
    )
    arrived = jnp.concatenate(
        [dot(band_ref[0, :, :rim], low, (1, 0)), dot(band_ref[1, :, 2 * rim :], high, (1, 0))], axis=0
    )
    message = ((message_ref[...] + arrived) * valid).astype(BF16)
    state = jnp.concatenate([state_ref[:rim, :], state_ref[rows - rim :, :]], axis=0)
    upstream = jnp.concatenate([up_ref[:rim, :], up_ref[rows - rim :, :]], axis=0).astype(F32)
    new_state, gain_sum, activated, grad_output, grad_pre = node_rows(
        state, message, direct_ref[...], upstream, valid, w_in_ref, w_out_ref, gain_ref[...]
    )
    new_ref[...] = new_state
    gain_sum = gain_sum + inner_gain_ref[...]
    grad_out_ref[...] = inner_out_ref[...] + dot(activated, grad_output, (0, 0))
    grad_in_ref[:latent, :] = inner_in_ref[:latent, :] + dot(state, grad_pre, (0, 0))
    grad_in_ref[latent:, :] = inner_in_ref[latent:, :] + dot(message, grad_pre, (0, 0))
    own_ref[...] = upstream + dot(grad_pre, w_in_ref[:latent, :], (1, 1))
    grad_message = dot(grad_pre, w_in_ref[latent:, :], (1, 1)).astype(BF16)
    grad_message = (grad_message.astype(F32) * valid).astype(BF16)
    left = dot(band_ref[0], grad_message[:rim, :], (0, 0))
    right = dot(band_ref[1], grad_message[rim:, :], (0, 0))
    spread_ref[: 2 * rim, :] = left[rim:, :]
    spread_ref[2 * rim :, :] = right[: 2 * rim, :]
    low = left[:rim, :].astype(BF16)
    high = right[2 * rim :, :].astype(BF16)
    spill_odd_ref[...] = jnp.where(side == 0, low, high)
    spill_even_ref[...] = jnp.where(side == 0, high, low)

    count = send_ref.shape[0] * send_ref.shape[1]
    n_in = grad_in_ref.shape[0] // count
    n_out = grad_out_ref.shape[0] // count
    top = lax.broadcasted_iota(jnp.int32, (GAIN_ROWS, latent), 0) == 0
    for piece in range(count):
        turn = lax.bitwise_xor(me, piece)
        half = lax.bitwise_and(turn, 1)
        slot = lax.shift_right_logical(turn, 1)
        send_ref[half, slot, :n_in, :] = (grad_in_ref[piece * n_in : (piece + 1) * n_in, :] * scale).astype(BF16)
        send_ref[half, slot, n_in : n_in + n_out, :] = (
            grad_out_ref[piece * n_out : (piece + 1) * n_out, :] * scale
        ).astype(BF16)
        if piece == 0:
            tail = jnp.where(top, gain_sum * scale, 0.0)
        else:
            tail = jnp.zeros((GAIN_ROWS, latent), F32)
        send_ref[half, slot, n_in + n_out :, :] = tail.astype(BF16)


def finish_kernel(
    bs,
    place_ref,
    len_ref,
    new_inner_ref,
    new_rim_ref,
    own_inner_ref,
    own_rim_ref,
    spread_inner_ref,
    spread_rim_ref,
    odd_ref,
    even_ref,
    new_ref,
    out_ref,
):
    rows = out_ref.shape[0]
    rim = odd_ref.shape[0]
    per = rim // bs
    blocks = rows // bs
    side = place_ref[0]
    odd = odd_ref[...].astype(F32)
    even = even_ref[...].astype(F32)
    new_ref[:rim, :] = new_rim_ref[:rim, :]
    new_ref[rim : rows - rim, :] = new_inner_ref[...]
    new_ref[rows - rim :, :] = new_rim_ref[rim:, :]
    inner = slice(rim, rows - rim)
    out_ref[inner, :] = (
        own_inner_ref[...]
        + (spread_inner_ref[inner, :] + spread_rim_ref[inner, :])
        * validity(len_ref, per, blocks - 2 * per, bs)
    ).astype(BF16)
    for end in range(2):
        first = end * (blocks - per)
        here = slice(first * bs, first * bs + rim)
        there = slice(end * rim, (end + 1) * rim)
        back = jnp.where(side == end, odd, even)
        out_ref[here, :] = (
            own_rim_ref[there, :]
            + (spread_inner_ref[here, :] + spread_rim_ref[here, :] + back)
            * validity(len_ref, first, per, bs)
        ).astype(BF16)


def unpack_kernel(place_ref, near_ref, far_ref, grad_in_ref, grad_out_ref, gain_ref):
    me = place_ref[1]
    count = 2 * near_ref.shape[0]
    n_in = grad_in_ref.shape[0] // count
    n_out = grad_out_ref.shape[0] // count
    for turn in range(count):
        source = (far_ref if turn % 2 else near_ref).at[turn // 2]
        piece = lax.bitwise_xor(me, turn)
        at_in = pl.ds(pl.multiple_of(piece * n_in, n_in), n_in)
        at_out = pl.ds(pl.multiple_of(piece * n_out, n_out), n_out)
        grad_in_ref[at_in, :] = source[:n_in, :].astype(F32)
        grad_out_ref[at_out, :] = source[n_in : n_in + n_out, :].astype(F32)

        @pl.when(piece == 0)
        def _():
            gain_ref[...] = source[n_in + n_out :, :].astype(F32)[:1, :]


def swap(x, axis, turn):
    count = lax.axis_size(axis)
    return lax.ppermute(x, axis, [(i, i ^ turn) for i in range(count)])


def whole_sum(x, axis):
    count = lax.axis_size(axis)
    if count & (count - 1) == 0:
        parts = [x.astype(F32)] + [swap(x, axis, k).astype(F32) for k in range(1, count)]
        while len(parts) > 1:
            parts = [parts[i] + parts[i + 1] for i in range(0, len(parts), 2)]
        return parts[0].astype(x.dtype)
    moved = [x] + [
        lax.ppermute(x, axis, [(i, (i + k) % count) for i in range(count)]) for k in range(1, count)
    ]
    order = (lax.axis_index(axis) - jnp.arange(count)) % count
    stacked = jnp.stack(moved)[order]
    return jnp.sum(stacked.astype(F32), axis=0).astype(x.dtype)


def vmem(count):
    return [pl.BlockSpec(memory_space=pltpu.VMEM)] * count


def smem(count):
    return [pl.BlockSpec(memory_space=pltpu.SMEM)] * count


def shapes(*given):
    return tuple(jax.ShapeDtypeStruct(shape, dtype) for shape, dtype in given)


def kernel(body, name, inputs, outputs, scratch=(), flops=0, moved=0):
    scalars, arrays, anywhere = inputs
    return pl.pallas_call(
        body,
        out_shape=outputs,
        in_specs=smem(scalars) + [pl.BlockSpec(memory_space=pl.ANY)] * anywhere + vmem(arrays),
        out_specs=tuple(vmem(len(outputs))),
        scratch_shapes=list(scratch),
        compiler_params=pltpu.CompilerParams(vmem_limit_bytes=VMEM_LIMIT),
        cost_estimate=pl.CostEstimate(flops=flops, bytes_accessed=moved, transcendentals=0),
        name=name,
    )


def local(node_state, edge_tiles, block_mask, block_len, w_in, w_out, gain, upstream):
    rows, latent = node_state.shape
    offsets, bs = edge_tiles.shape[1:]
    rim = (offsets - 1) // 2 * bs
    inside = rows - 2 * rim
    width = 3 * rim
    dom = lax.axis_size("dom")
    rep = lax.axis_size("rep")
    total = dom * rep
    me = lax.axis_index("dom")
    side = (me * rep + lax.axis_index("rep")) % 2
    place = jnp.stack([side, me]).astype(jnp.int32)
    scale = 1.0 / math.sqrt(rows * total)
    ring = ("dom", "rep")
    even_pairs = [(i, i ^ 1) for i in range(total)]
    odd_pairs = [(i, (i + 1) % total if i % 2 else (i - 1) % total) for i in range(total)]
    gain_row = gain.reshape(1, latent)
    tiles = jnp.transpose(edge_tiles, (1, 0, 2))

    to_odd, to_even = kernel(
        functools.partial(pack_kernel, bs),
        "pack_rims",
        (2, 0, 1),
        shapes(((rim, latent), BF16), ((rim, latent), BF16)),
        [pltpu.VMEM((2, rim, latent), BF16), pltpu.SemaphoreType.DMA((2,))],
    )(place, block_len, node_state)
    from_odd = lax.ppermute(to_odd, ring, odd_pairs)
    from_even = lax.ppermute(to_even, ring, even_pairs)

    work = 2 * inside * latent * (width + 5 * latent + 2 * latent + 2 * latent + width)
    new_inner, own_inner, spread_inner, sum_in, sum_out, sum_gain, band, message, direct = kernel(
        functools.partial(inner_kernel, (bs, offsets)),
        "inner_rows",
        (2, 6, 0),
        shapes(
            ((inside, latent), BF16),
            ((inside, latent), F32),
            ((rows, latent), F32),
            (w_in.shape, F32),
            (w_out.shape, F32),
            ((1, latent), F32),
            ((2, rim, width), BF16),
            ((2 * rim, latent), F32),
            ((2 * rim, latent), F32),
        ),
        [pltpu.VMEM((rows, latent), BF16), pltpu.VMEM((inside // rim, rim, width), BF16)],
        flops=work,
        moved=10 * 1024 * 1024,
    )(block_len, block_mask, node_state, tiles, upstream, w_in, w_out, gain_row)

    n_in, n_out = w_in.shape[0] // dom, w_out.shape[0] // dom
    piece_rows = n_in + n_out + GAIN_ROWS
    send, spill_odd, spill_even, new_rim, own_rim, spread_rim = kernel(
        functools.partial(rim_kernel, (bs, scale)),
        "rim_rows",
        (2, 13, 0),
        shapes(
            ((2, dom // 2, piece_rows, latent), BF16),
            ((rim, latent), BF16),
            ((rim, latent), BF16),
            ((2 * rim, latent), BF16),
            ((2 * rim, latent), F32),
            ((rows, latent), F32),
        ),
        [pltpu.VMEM(w_in.shape, F32), pltpu.VMEM(w_out.shape, F32)],
        flops=work,
        moved=8 * 1024 * 1024,
    )(
        place, block_len, node_state, upstream, w_in, w_out, gain_row,
        band, message, direct, sum_in, sum_out, sum_gain, from_odd, from_even,
    )

    back_odd = lax.ppermute(spill_odd, ring, odd_pairs)
    back_even = lax.ppermute(spill_even, ring, even_pairs)
    new_state, grad_state = kernel(
        functools.partial(finish_kernel, bs),
        "finish_state",
        (2, 8, 0),
        shapes(((rows, latent), BF16), ((rows, latent), BF16)),
    )(place, block_len, new_inner, new_rim, own_inner, own_rim, spread_inner, spread_rim, back_odd, back_even)

    held = (send[0].astype(F32) + swap(send[1], "dom", 1).astype(F32)).astype(BF16)
    quarter = held[0].astype(F32)
    for k in range(1, dom // 2):
        quarter = quarter + swap(held[k], "dom", 2 * k).astype(F32)
    mine = whole_sum(quarter.astype(BF16), "rep")
    mine, grad_state, new_state = lax.optimization_barrier((mine, grad_state, new_state))
    near = jnp.stack([mine] + [swap(mine, "dom", 2 * k) for k in range(1, dom // 2)])
    other = swap(near, "dom", 1)
    grad_w_in, grad_w_out, grad_gain = kernel(
        unpack_kernel,
        "unpack_sums",
        (1, 2, 0),
        shapes((w_in.shape, F32), (w_out.shape, F32), ((1, latent), F32)),
    )(place, near, other)
    return new_state, grad_state, grad_w_in, grad_w_out, grad_gain.reshape(latent)


def solution(mesh):
    placed = (
        P(("dom", "rep"), None),
        P(("dom", "rep"), None, None),
        P(("dom", "rep"), None),
        P(("dom", "rep")),
        P(),
        P(),
        P(),
        P(("dom", "rep"), None),
    )
    return jax.shard_map(
        local,
        mesh=mesh,
        in_specs=placed,
        out_specs=(P(("dom", "rep"), None), P(("dom", "rep"), None), P(), P(), P()),
        check_vma=False,
    )
```

time: 60.5 us -> 50.2 us (0.83)
  waiting for transfers between devices: 24.4 us -> 10.6 us
  local copies, waits for them, and re-layouts: 1.37 us -> 8.35 us
  other arithmetic: 2.31 us -> 0.22 us
  starting transfers between devices: 21.3 us -> 20.1 us
    unnamed x16 -> x22, local copies, waits for them, and re-layouts: 1.34 us -> 8.32 us
    ppermute x1, waiting for transfers between devices: 5.8 us -> 0.01 us  [local(): from_odd = lax.ppermute(to_odd, ring, odd_pairs)]
    ppermute x1, waiting for transfers between devices: 6.48 us -> 2.21 us  [local(): back_odd = lax.ppermute(spill_odd, ring, odd_pairs)]
    ppermute x1, starting transfers between devices: 3.09 us -> 0.01 us  [local(): from_even = lax.ppermute(to_even, ring, even_pairs)]
    ppermute x1, starting transfers between devices: 3.52 us -> 6.44 us  [local(): from_odd = lax.ppermute(to_odd, ring, odd_pairs)]
    ppermute x11, waiting for transfers between devices: 11.1 us -> 8.4 us  [swap(): return lax.ppermute(x, axis, [(i, i ^ turn) for i in range(count)])]
    ppermute x1, starting transfers between devices: 2.96 us -> 0.35 us  [local(): back_odd = lax.ppermute(spill_odd, ring, odd_pairs)]
    ppermute x1, starting transfers between devices: 0.01 us -> 1.67 us  [local(): back_even = lax.ppermute(spill_even, ring, even_pairs)]
  transfers between devices with their start and end apart: 15 -> 15, of which waited for: 12 -> 8; matrix products, arithmetic and copies ran while one was open for 0% -> 0% of each run, Pallas kernels for 2% -> 10%
where the time goes in v2:
time: 50.2 us; the launch traced here: 49.8 us
  starting transfers between devices  20.1 us (40%)
  waiting for transfers between devices  10.6 us (21%)
  Pallas kernels  9.74 us (19%)
  local copies, waits for them, and re-layouts  8.35 us (17%)
  between operations  0.77 us (2%)
    ppermute x11, starting transfers between devices, swap(): return lax.ppermute(x, axis, [(i, i ^ turn) for i in range(count)])  11.7 us
    ppermute x11, waiting for transfers between devices, swap(): return lax.ppermute(x, axis, [(i, i ^ turn) for i in range(count)])  8.4 us
    unnamed x22, local copies, waits for them, and re-layouts  8.32 us
    ppermute x1, starting transfers between devices, local(): from_odd = lax.ppermute(to_odd, ring, odd_pairs)  6.44 us
    pallas_call x1, Pallas kernels, local(): kernel(functools.partial(inner_kernel, (bs, offsets)), 'inner_rows', (2,...  3.11 us
    pallas_call x1, Pallas kernels, local(): kernel(functools.partial(rim_kernel, (bs, scale)), 'rim_rows', (2, 13, 0)...  2.4 us
    ppermute x1, waiting for transfers between devices, local(): back_odd = lax.ppermute(spill_odd, ring, odd_pairs)  2.21 us
    pallas_call x1, Pallas kernels, local(): kernel(functools.partial(finish_kernel, bs), 'finish_state', (2, 8, 0), s...  1.77 us
  transfers between devices with their start and end apart: 15, of which 8 were waited for; matrix products, arithmetic and copies ran while one was open for 0% of the time, Pallas kernels for 10%

profile of v2, /device:TPU:0, one launch (start us, length us, event | category | flops | bytes accessed | tf_op | source)
XLA Modules:
  0.0 49.8 jit_solution(1113747297463379839)
XLA Ops:
  0.7 1.0 %copy-done = bf16[1024,256]{1,0:T(8,128)(2,1)S(1)} copy-done((bf16[1024,256]{1,0:T(8,128)(2,1)S(1)}, bf16[1024,256]{1,0:T(8,128)(2,1)}, u32[]{:S(2)}) %copy-start) | copy-done | bytes 524312
  2.4 1.0 %pack_rims.1 = (bf16[256,256]{1,0:T(8,128)(2,1)S(1)}, bf16[256,256]{1,0:T(8,128)(2,1)S(1)}) custom-call(s32[2]{0:T(128)S(1)} %pad_add_fusion.place_ref, s32[8]{0:T(128)S(1)} %copy-done.7, bf16[1024,256]{1,0:T(8,128)(2,1)S(1)} %copy-done), custom_call_target="tpu_custom_call" | custom-call | tf_op jit(solution)/shard_map/pack_rims/pallas_call | solution.py:377
  3.4 6.4 %collective-permute-start = (bf16[256,256]{1,0:T(8,128)(2,1)S(1)}, bf16[256,256]{1,0:T(8,128)(2,1)S(1)}, u32[]{:S(2)}, u32[]{:S(2)}) collective-permute-start(bf16[256,256]{1,0:T(8,128)(2,1)S(1)} %get-tuple-element.36), channel_id=1, source_target_pairs={{0,31},{1,2},{2,1},{3,4},{4,3},{5,6},{6,5},{7,8},{8,7},{9,10},{10,... | collective-permute-start | bytes 393224 | tf_op jit(solution)/shard_map/ppermute | solution.py:384
  9.8 1.0 %copy-done.1 = bf16[1024,256]{1,0:T(8,128)(2,1)S(1)} copy-done((bf16[1024,256]{1,0:T(8,128)(2,1)S(1)}, bf16[1024,256]{1,0:T(8,128)(2,1)}, u32[]{:S(2)}) %copy-start.1) | copy-done | bytes 524312
  10.9 1.0 %copy-done.3 = bf16[1024,256]{1,0:T(8,128)(2,1)S(1)} copy-done((bf16[1024,256]{1,0:T(8,128)(2,1)S(1)}, bf16[1024,256]{1,0:T(8,128)(2,1)}, u32[]{:S(2)}) %copy-start.3) | copy-done | bytes 524312
  11.9 0.9 %copy-done.5 = bf16[512,256]{1,0:T(8,128)(2,1)S(1)} copy-done((bf16[512,256]{1,0:T(8,128)(2,1)S(1)}, bf16[512,256]{1,0:T(8,128)(2,1)}, u32[]{:S(2)}) %copy-start.5) | copy-done | bytes 262168
  14.4 1.3 %copy-done.9 = bf16[1024,5,128]{2,0,1:T(8,128)(2,1)S(1)} copy-done((bf16[1024,5,128]{2,0,1:T(8,128)(2,1)S(1)}, bf16[1024,5,128]{2,0,1:T(8,128)(2,1)}, u32[]{:S(2)}) %copy-start.9) | copy-done | bytes 1310744
  16.4 3.1 %inner_rows.1 = (bf16[512,256]{1,0:T(8,128)(2,1)S(1)}, f32[512,256]{1,0:T(8,128)S(1)}, f32[1024,256]{1,0:T(8,128)S(1)}, f32[512,256]{1,0:T(8,128)S(1)}, f32[256,...) custom-call(s32[8]{0:T(128)S(1)} %copy-done.7, ...), custom_call_target="tpu_custom_call" | custom-call | flops 1006632960 | bytes 10485760 | tf_op jit(solution)/shard_map/inner_rows/pallas_call | solution.py:388
  19.6 2.4 %rim_rows.1 = (bf16[2,4,104,256]{3,2,1,0:T(8,128)(2,1)S(1)}, bf16[256,256]{1,0:T(8,128)(2,1)S(1)}, bf16[256,256]{1,0:T(8,128)(2,1)S(1)}, bf16[512,256]{1,0:T(8,1...) custom-call(s32[2]{0:T(128)S(1)} %pad_add_fusion.place_ref, s32[8]{0:T(128)S(1)} %copy-done.7, ...), custom_call_target="tpu_custom_call" | custom-call | flops 1006632960 | bytes 8388608 | tf_op jit(solution)/shard_map/rim_rows/pallas_call | solution.py:410
  22.1 1.5 %collective-permute-done.2 = bf16[4,104,256]{2,1,0:T(8,128)(2,1)S(1)} collective-permute-done((bf16[4,104,256]{2,1,0:T(8,128)(2,1)S(1)}, bf16[4,104,256]{2,1,0:T(8,128)(2,1)S(1)}, u32[]{:S(2)}, u32[]{:S(2)}) %collective-permute-start.2) | collective-permute-done | bytes 213024 | tf_op jit(solution)/shard_map/ppermute | solution.py:314
  23.7 1.9 %collective-permute-start.5 = (bf16[104,256]{1,0:T(8,128)(2,1)S(1)}, bf16[104,256]{1,0:T(8,128)(2,1)S(1)}, u32[]{:S(2)}, u32[]{:S(2)}) collective-permute-start(bf16[104,256]{1,0:T(8,128)(2,1)S(1)} %get-tuple-element.56), channel_id=1, source_target_pairs={{0,24},{4,28},{8,16},{12,20},{16,8},{20,12},{24,0},{28,4},{1,25},{... | collective-permute-start | bytes 159752 | tf_op jit(solution)/shard_map/ppermute | solution.py:314
  25.7 1.5 %collective-permute-start.4 = (bf16[104,256]{1,0:T(8,128)(2,1)S(1)}, bf16[104,256]{1,0:T(8,128)(2,1)S(1)}, u32[]{:S(2)}, u32[]{:S(2)}) collective-permute-start(bf16[104,256]{1,0:T(8,128)(2,1)S(1)} %get-tuple-element.57), channel_id=1, source_target_pairs={{0,16},{4,20},{8,24},{12,28},{16,0},{20,4},{24,8},{28,12},{1,17},{... | collective-permute-start | bytes 159752 | tf_op jit(solution)/shard_map/ppermute | solution.py:314
  27.6 1.7 %collective-permute-start.10 = (bf16[256,256]{1,0:T(8,128)(2,1)S(1)}, bf16[256,256]{1,0:T(8,128)(2,1)S(1)}, u32[]{:S(2)}, u32[]{:S(2)}) collective-permute-start(bf16[256,256]{1,0:T(8,128)(2,1)S(1)} %get-tuple-element.46), channel_id=1, source_target_pairs={{0,1},{1,0},{2,3},{3,2},{4,5},{5,4},{6,7},{7,6},{8,9},{9,8},{10,11... | collective-permute-start | bytes 393224 | tf_op jit(solution)/shard_map/ppermute | solution.py:431
  29.9 2.3 %collective-permute-start.8 = (bf16[104,256]{1,0:T(8,128)(2,1)S(1)}, bf16[104,256]{1,0:T(8,128)(2,1)S(1)}, u32[]{:S(2)}, u32[]{:S(2)}) collective-permute-start(bf16[104,256]{1,0:T(8,128)(2,1)S(1)} %fusion.3), channel_id=1, source_target_pairs={{0,3},{1,2},{2,1},{3,0},{4,7},{5,6},{6,5},{7,4},{8,11},{9,10},{10,... | collective-permute-start | bytes 159752 | tf_op jit(solution)/shard_map/ppermute | solution.py:314
  32.3 1.2 %collective-permute-start.7 = (bf16[104,256]{1,0:T(8,128)(2,1)S(1)}, bf16[104,256]{1,0:T(8,128)(2,1)S(1)}, u32[]{:S(2)}, u32[]{:S(2)}) collective-permute-start(bf16[104,256]{1,0:T(8,128)(2,1)S(1)} %fusion.3), channel_id=1, source_target_pairs={{0,2},{1,3},{2,0},{3,1},{4,6},{5,7},{6,4},{7,5},{8,10},{9,11},{10,... | collective-permute-start | bytes 159752 | tf_op jit(solution)/shard_map/ppermute | solution.py:314
  33.5 0.9 %collective-permute-start.6 = (bf16[104,256]{1,0:T(8,128)(2,1)S(1)}, bf16[104,256]{1,0:T(8,128)(2,1)S(1)}, u32[]{:S(2)}, u32[]{:S(2)}) collective-permute-start(bf16[104,256]{1,0:T(8,128)(2,1)S(1)} %fusion.3), channel_id=1, source_target_pairs={{0,1},{1,0},{2,3},{3,2},{4,5},{5,4},{6,7},{7,6},{8,9},{9,8},{10,11... | collective-permute-start | bytes 159752 | tf_op jit(solution)/shard_map/ppermute | solution.py:314
  34.4 2.2 %collective-permute-done.9.odd_ref = bf16[256,256]{1,0:T(8,128)(2,1)S(1)} collective-permute-done((bf16[256,256]{1,0:T(8,128)(2,1)S(1)}, bf16[256,256]{1,0:T(8,128)(2,1)S(1)}, u32[]{:S(2)}, u32[]{:S(2)}) %collective-permute-start.9) | collective-permute-done | bytes 131104 | tf_op jit(solution)/shard_map/ppermute | solution.py:430
  36.6 1.8 %finish_state.1 = (bf16[1024,256]{1,0:T(8,128)(2,1)}, bf16[1024,256]{1,0:T(8,128)(2,1)}) custom-call(s32[2]{0:T(128)S(1)} %pad_add_fusion.place_ref, s32[8]{0:T(128)S(1)} %copy-done.7, bf16[512,256]{1,0:T(8,128)(2,1)S(1)} %get-tuple-element.39.new_inner_ref, bf16[512,256]{1,0:T(8,128)(2,1)S(1)} %get-tuple-element.40.new_rim_ref, ...), custom_call_target="tpu_custom_call" | custom-call | tf_op jit(solution)/shard_map/finish_state/pallas_call | solution.py:432
  38.4 2.3 %collective-permute-done.7 = bf16[104,256]{1,0:T(8,128)(2,1)S(1)} collective-permute-done((bf16[104,256]{1,0:T(8,128)(2,1)S(1)}, bf16[104,256]{1,0:T(8,128)(2,1)S(1)}, u32[]{:S(2)}, u32[]{:S(2)}) %collective-permute-start.7) | collective-permute-done | bytes 53280 | tf_op jit(solution)/shard_map/ppermute | solution.py:314
  41.7 1.0 %collective-permute-start.12 = (bf16[104,256]{1,0:T(8,128)(2,1)S(1)}, bf16[104,256]{1,0:T(8,128)(2,1)S(1)}, u32[]{:S(2)}, u32[]{:S(2)}) collective-permute-start(bf16[104,256]{1,0:T(8,128)(2,1)S(1)} %add_convert_fusion), channel_id=1, source_target_pairs={{0,16},{4,20},{8,24},{12,28},{16,0},{20,4},{24,8},{28,12},{1,17},{... | collective-permute-start | bytes 159752 | tf_op jit(solution)/shard_map/ppermute | solution.py:314
  42.6 1.7 %collective-permute-start.11 = (bf16[104,256]{1,0:T(8,128)(2,1)S(1)}, bf16[104,256]{1,0:T(8,128)(2,1)S(1)}, u32[]{:S(2)}, u32[]{:S(2)}) collective-permute-start(bf16[104,256]{1,0:T(8,128)(2,1)S(1)} %add_convert_fusion), channel_id=1, source_target_pairs={{0,8},{4,12},{8,0},{12,4},{16,24},{20,28},{24,16},{28,20},{1,9},{5... | collective-permute-start | bytes 159752 | tf_op jit(solution)/shard_map/ppermute | solution.py:314
  44.3 1.7 %collective-permute-done.13 = bf16[104,256]{1,0:T(8,128)(2,1)S(1)} collective-permute-done((bf16[104,256]{1,0:T(8,128)(2,1)S(1)}, bf16[104,256]{1,0:T(8,128)(2,1)S(1)}, u32[]{:S(2)}, u32[]{:S(2)}) %collective-permute-start.13) | collective-permute-done | bytes 53280 | tf_op jit(solution)/shard_map/ppermute | solution.py:314
  46.9 1.5 %collective-permute-done.14.far_ref = bf16[4,104,256]{2,1,0:T(8,128)(2,1)S(1)} collective-permute-done((bf16[4,104,256]{2,1,0:T(8,128)(2,1)S(1)}, bf16[4,104,256]{2,1,0:T(8,128)(2,1)S(1)}, u32[]{:S(2)}, u32[]{:S(2)}) %collective-permute-start.14) | collective-permute-done | bytes 213024 | tf_op jit(solution)/shard_map/ppermute | solution.py:314
  48.3 1.5 %unpack_sums.1 = (f32[512,256]{1,0:T(8,128)}, f32[256,256]{1,0:T(8,128)}, f32[1,256]{1,0:T(1,128)}) custom-call(s32[2]{0:T(128)S(1)} %pad_add_fusion.place_ref, bf16[4,104,256]{2,1,0:T(8,128)(2,1)S(1)} %pad_maximum_fusion.near_ref, bf16[4,104,256]{2,1,0:T(8,128)(2,1)S(1)} %collective-permute-done.14.far_ref), custom_call_target="tpu_custom_call" | custom-call | tf_op jit(solution)/shard_map/unpack_sums/pallas_call | solution.py:447
  (40 shorter events, 6.2 us)
Async XLA Ops:
  0.7 1.0 %copy-start = (bf16[1024,256]{1,0:T(8,128)(2,1)S(1)}, bf16[1024,256]{1,0:T(8,128)(2,1)}, u32[]{:S(2)}) copy-start(bf16[1024,256]{1,0:T(8,128)(2,1)} %state_ref.5) | copy-start | bytes 1572868
  3.4 16.2 %collective-permute-start = (bf16[256,256]{1,0:T(8,128)(2,1)S(1)}, bf16[256,256]{1,0:T(8,128)(2,1)S(1)}, u32[]{:S(2)}, u32[]{:S(2)}) collective-permute-start(bf16[256,256]{1,0:T(8,128)(2,1)S(1)} %get-tuple-element.36), channel_id=1, source_target_pairs={{0,31},{1,2},{2,1},{3,4},{4,3},{5,6},{6,5},{7,8},{8,7},{9,10},{10,... | collective-permute-start | bytes 393224 | tf_op jit(solution)/shard_map/ppermute | solution.py:384
  9.8 9.8 %collective-permute-start.1 = (bf16[256,256]{1,0:T(8,128)(2,1)S(1)}, bf16[256,256]{1,0:T(8,128)(2,1)S(1)}, u32[]{:S(2)}, u32[]{:S(2)}) collective-permute-start(bf16[256,256]{1,0:T(8,128)(2,1)S(1)} %get-tuple-element.37), channel_id=1, source_target_pairs={{0,1},{1,0},{2,3},{3,2},{4,5},{5,4},{6,7},{7,6},{8,9},{9,8},{10,11... | collective-permute-start | bytes 393224 | tf_op jit(solution)/shard_map/ppermute | solution.py:385
  9.8 1.0 %copy-start.1 = (bf16[1024,256]{1,0:T(8,128)(2,1)S(1)}, bf16[1024,256]{1,0:T(8,128)(2,1)}, u32[]{:S(2)}) copy-start(bf16[1024,256]{1,0:T(8,128)(2,1)} %state_ref.5) | copy-start | bytes 1572868
  10.9 1.0 %copy-start.3 = (bf16[1024,256]{1,0:T(8,128)(2,1)S(1)}, bf16[1024,256]{1,0:T(8,128)(2,1)}, u32[]{:S(2)}) copy-start(bf16[1024,256]{1,0:T(8,128)(2,1)} %up_ref.3) | copy-start | bytes 1572868
  11.9 0.9 %copy-start.5 = (bf16[512,256]{1,0:T(8,128)(2,1)S(1)}, bf16[512,256]{1,0:T(8,128)(2,1)}, u32[]{:S(2)}) copy-start(bf16[512,256]{1,0:T(8,128)(2,1)} %w_in_ref.3) | copy-start | bytes 786436
  12.9 0.9 %copy-start.6 = (bf16[256,256]{1,0:T(8,128)(2,1)S(1)}, bf16[256,256]{1,0:T(8,128)(2,1)}, u32[]{:S(2)}) copy-start(bf16[256,256]{1,0:T(8,128)(2,1)} %w_out_ref.3) | copy-start | bytes 393220
  14.4 1.3 %copy-start.9 = (bf16[1024,5,128]{2,0,1:T(8,128)(2,1)S(1)}, bf16[1024,5,128]{2,0,1:T(8,128)(2,1)}, u32[]{:S(2)}) copy-start(bf16[1024,5,128]{2,0,1:T(8,128)(2,1)} %param.9) | copy-start | bytes 3932164
  15.8 0.7 %copy-start.10 = (s32[8,5]{1,0:T(8,128)S(1)}, s32[8,5]{1,0:T(8,128)}, u32[]{:S(2)}) copy-start(s32[8,5]{1,0:T(8,128)} %mask_ref.1) | copy-start | bytes 484
  16.4 3.1 %copy-start.2 = (bf16[1024,256]{1,0:T(8,128)(2,1)S(1)}, bf16[1024,256]{1,0:T(8,128)(2,1)}, u32[]{:S(2)}) copy-start(bf16[1024,256]{1,0:T(8,128)(2,1)} %state_ref.5) | copy-start | bytes 1572868
  16.4 3.2 %copy-start.4 = (bf16[1024,256]{1,0:T(8,128)(2,1)S(1)}, bf16[1024,256]{1,0:T(8,128)(2,1)}, u32[]{:S(2)}) copy-start(bf16[1024,256]{1,0:T(8,128)(2,1)} %up_ref.3) | copy-start | bytes 1572868
  22.0 1.5 %collective-permute-start.2 = (bf16[4,104,256]{2,1,0:T(8,128)(2,1)S(1)}, bf16[4,104,256]{2,1,0:T(8,128)(2,1)S(1)}, u32[]{:S(2)}, u32[]{:S(2)}) collective-permute-start(bf16[4,104,256]{2,1,0:T(8,128)(2,1)S(1)} %slice_bitcast_fusion), channel_id=1, source_target_pairs={{0,4},{4,0},{8,12},{12,8},{16,20},{20,16},{24,28},{28,24},{1,5},{5... | collective-permute-start | bytes 638984 | tf_op jit(solution)/shard_map/ppermute | solution.py:314
  23.6 5.6 %collective-permute-start.3 = (bf16[104,256]{1,0:T(8,128)(2,1)S(1)}, bf16[104,256]{1,0:T(8,128)(2,1)S(1)}, u32[]{:S(2)}, u32[]{:S(2)}) collective-permute-start(bf16[104,256]{1,0:T(8,128)(2,1)S(1)} %get-tuple-element.55), channel_id=1, source_target_pairs={{0,8},{4,12},{8,0},{12,4},{16,24},{20,28},{24,16},{28,20},{1,9},{5... | collective-permute-start | bytes 159752 | tf_op jit(solution)/shard_map/ppermute | solution.py:314
  23.7 5.5 %collective-permute-start.5 = (bf16[104,256]{1,0:T(8,128)(2,1)S(1)}, bf16[104,256]{1,0:T(8,128)(2,1)S(1)}, u32[]{:S(2)}, u32[]{:S(2)}) collective-permute-start(bf16[104,256]{1,0:T(8,128)(2,1)S(1)} %get-tuple-element.56), channel_id=1, source_target_pairs={{0,24},{4,28},{8,16},{12,20},{16,8},{20,12},{24,0},{28,4},{1,25},{... | collective-permute-start | bytes 159752 | tf_op jit(solution)/shard_map/ppermute | solution.py:314
  25.7 4.2 %collective-permute-start.4 = (bf16[104,256]{1,0:T(8,128)(2,1)S(1)}, bf16[104,256]{1,0:T(8,128)(2,1)S(1)}, u32[]{:S(2)}, u32[]{:S(2)}) collective-permute-start(bf16[104,256]{1,0:T(8,128)(2,1)S(1)} %get-tuple-element.57), channel_id=1, source_target_pairs={{0,16},{4,20},{8,24},{12,28},{16,0},{20,4},{24,8},{28,12},{1,17},{... | collective-permute-start | bytes 159752 | tf_op jit(solution)/shard_map/ppermute | solution.py:314
  27.2 9.4 %collective-permute-start.9 = (bf16[256,256]{1,0:T(8,128)(2,1)S(1)}, bf16[256,256]{1,0:T(8,128)(2,1)S(1)}, u32[]{:S(2)}, u32[]{:S(2)}) collective-permute-start(bf16[256,256]{1,0:T(8,128)(2,1)S(1)} %get-tuple-element.45), channel_id=1, source_target_pairs={{0,31},{1,2},{2,1},{3,4},{4,3},{5,6},{6,5},{7,8},{8,7},{9,10},{10,... | collective-permute-start | bytes 393224 | tf_op jit(solution)/shard_map/ppermute | solution.py:430
  27.6 9.1 %collective-permute-start.10 = (bf16[256,256]{1,0:T(8,128)(2,1)S(1)}, bf16[256,256]{1,0:T(8,128)(2,1)S(1)}, u32[]{:S(2)}, u32[]{:S(2)}) collective-permute-start(bf16[256,256]{1,0:T(8,128)(2,1)S(1)} %get-tuple-element.46), channel_id=1, source_target_pairs={{0,1},{1,0},{2,3},{3,2},{4,5},{5,4},{6,7},{7,6},{8,9},{9,8},{10,11... | collective-permute-start | bytes 393224 | tf_op jit(solution)/shard_map/ppermute | solution.py:431
  29.9 8.4 %collective-permute-start.8 = (bf16[104,256]{1,0:T(8,128)(2,1)S(1)}, bf16[104,256]{1,0:T(8,128)(2,1)S(1)}, u32[]{:S(2)}, u32[]{:S(2)}) collective-permute-start(bf16[104,256]{1,0:T(8,128)(2,1)S(1)} %fusion.3), channel_id=1, source_target_pairs={{0,3},{1,2},{2,1},{3,0},{4,7},{5,6},{6,5},{7,4},{8,11},{9,10},{10,... | collective-permute-start | bytes 159752 | tf_op jit(solution)/shard_map/ppermute | solution.py:314
  32.3 8.5 %collective-permute-start.7 = (bf16[104,256]{1,0:T(8,128)(2,1)S(1)}, bf16[104,256]{1,0:T(8,128)(2,1)S(1)}, u32[]{:S(2)}, u32[]{:S(2)}) collective-permute-start(bf16[104,256]{1,0:T(8,128)(2,1)S(1)} %fusion.3), channel_id=1, source_target_pairs={{0,2},{1,3},{2,0},{3,1},{4,6},{5,7},{6,4},{7,5},{8,10},{9,11},{10,... | collective-permute-start | bytes 159752 | tf_op jit(solution)/shard_map/ppermute | solution.py:314
  33.5 7.2 %collective-permute-start.6 = (bf16[104,256]{1,0:T(8,128)(2,1)S(1)}, bf16[104,256]{1,0:T(8,128)(2,1)S(1)}, u32[]{:S(2)}, u32[]{:S(2)}) collective-permute-start(bf16[104,256]{1,0:T(8,128)(2,1)S(1)} %fusion.3), channel_id=1, source_target_pairs={{0,1},{1,0},{2,3},{3,2},{4,5},{5,4},{6,7},{7,6},{8,9},{9,8},{10,11... | collective-permute-start | bytes 159752 | tf_op jit(solution)/shard_map/ppermute | solution.py:314
  40.8 5.2 %collective-permute-start.13 = (bf16[104,256]{1,0:T(8,128)(2,1)S(1)}, bf16[104,256]{1,0:T(8,128)(2,1)S(1)}, u32[]{:S(2)}, u32[]{:S(2)}) collective-permute-start(bf16[104,256]{1,0:T(8,128)(2,1)S(1)} %add_convert_fusion), channel_id=1, source_target_pairs={{0,24},{4,28},{8,16},{12,20},{16,8},{20,12},{24,0},{28,4},{1,25},{... | collective-permute-start | bytes 159752 | tf_op jit(solution)/shard_map/ppermute | solution.py:314
  41.7 4.7 %collective-permute-start.12 = (bf16[104,256]{1,0:T(8,128)(2,1)S(1)}, bf16[104,256]{1,0:T(8,128)(2,1)S(1)}, u32[]{:S(2)}, u32[]{:S(2)}) collective-permute-start(bf16[104,256]{1,0:T(8,128)(2,1)S(1)} %add_convert_fusion), channel_id=1, source_target_pairs={{0,16},{4,20},{8,24},{12,28},{16,0},{20,4},{24,8},{28,12},{1,17},{... | collective-permute-start | bytes 159752 | tf_op jit(solution)/shard_map/ppermute | solution.py:314
  42.6 4.1 %collective-permute-start.11 = (bf16[104,256]{1,0:T(8,128)(2,1)S(1)}, bf16[104,256]{1,0:T(8,128)(2,1)S(1)}, u32[]{:S(2)}, u32[]{:S(2)}) collective-permute-start(bf16[104,256]{1,0:T(8,128)(2,1)S(1)} %add_convert_fusion), channel_id=1, source_target_pairs={{0,8},{4,12},{8,0},{12,4},{16,24},{20,28},{24,16},{28,20},{1,9},{5... | collective-permute-start | bytes 159752 | tf_op jit(solution)/shard_map/ppermute | solution.py:314
  46.8 1.5 %collective-permute-start.14 = (bf16[4,104,256]{2,1,0:T(8,128)(2,1)S(1)}, bf16[4,104,256]{2,1,0:T(8,128)(2,1)S(1)}, u32[]{:S(2)}, u32[]{:S(2)}) collective-permute-start(bf16[4,104,256]{2,1,0:T(8,128)(2,1)S(1)} %pad_maximum_fusion.near_ref), channel_id=1, source_target_pairs={{0,4},{4,0},{8,12},{12,8},{16,20},{20,16},{24,28},{28,24},{1,5},{5... | collective-permute-start | bytes 638984 | tf_op jit(solution)/shard_map/ppermute | solution.py:314
  (2 other events, 1.3 us)

commit v3 on v2

v3 whole, which is shorter than its diff:
```python
import functools
import math

import jax
import jax.numpy as jnp
from jax import lax
from jax.experimental import pallas as pl
from jax.experimental.pallas import tpu as pltpu
from jax.sharding import PartitionSpec as P

EPSILON = 1e-05
F32 = jnp.float32
BF16 = jnp.bfloat16
GAIN_ROWS = 8
VMEM_LIMIT = 40 * 1024 * 1024


def dot(a, b, contract):
    return lax.dot_general(a, b, ((contract[:1], contract[1:]), ((), ())), preferred_element_type=F32)


def sublane(bs):
    return lax.broadcasted_iota(jnp.int32, (bs, 1), 0)


def validity(len_ref, first, count, bs):
    return jnp.concatenate(
        [(sublane(bs) < len_ref[first + j]).astype(F32) for j in range(count)], axis=0
    )


def place():
    me = lax.axis_index("dom")
    index = me * lax.axis_size("rep") + lax.axis_index("rep")
    return lax.rem(index, 2), me


def pack_kernel(bs, len_ref, state_ref, odd_ref, even_ref, held_ref, lens_ref, sems):
    rows = state_ref.shape[0]
    rim = odd_ref.shape[0]
    per = rim // bs
    copies = [
        pltpu.make_async_copy(len_ref, lens_ref, sems.at[0]),
        pltpu.make_async_copy(state_ref.at[pl.ds(0, rim), :], held_ref.at[0], sems.at[1]),
        pltpu.make_async_copy(state_ref.at[pl.ds(rows - rim, rim), :], held_ref.at[1], sems.at[2]),
    ]
    for copy in copies:
        copy.start()
    side, _ = place()
    for copy in copies:
        copy.wait()
    blocks = rows // bs
    for j in range(per):
        here = slice(j * bs, (j + 1) * bs)
        top = held_ref[0, here, :] * (sublane(bs) < lens_ref[j]).astype(F32).astype(BF16)
        end = held_ref[1, here, :] * (sublane(bs) < lens_ref[blocks - per + j]).astype(F32).astype(BF16)
        odd_ref[here, :] = jnp.where(side == 0, top, end)
        even_ref[here, :] = jnp.where(side == 0, end, top)


def fill_band(band_ref, tiles_ref, mask_ref, first, per, bs, offsets):
    for j in range(per):
        row = slice(j * bs, (j + 1) * bs)
        for column in range(per + offsets - 1):
            offset = column - j
            cols = slice(column * bs, (column + 1) * bs)
            if 0 <= offset < offsets:
                tile = tiles_ref[offset, (first + j) * bs : (first + j + 1) * bs, :]
                band_ref[row, cols] = tile * mask_ref[first + j, offset].astype(F32).astype(BF16)
            else:
                band_ref[row, cols] = jnp.zeros((bs, bs), BF16)


def node_rows(state, message, direct_part, upstream, valid, w_in_ref, w_out_ref, gain):
    latent = state.shape[1]
    preact = direct_part + dot(message, w_in_ref[latent:, :], (1, 0))
    sigma = jax.nn.sigmoid(preact)
    activated = (preact * sigma).astype(BF16)
    output = dot(activated, w_out_ref[...], (1, 0))
    centred = output - jnp.mean(output, axis=1, keepdims=True)
    inverse = lax.rsqrt(jnp.mean(centred * centred, axis=1, keepdims=True) + EPSILON)
    normed = centred * inverse
    new_state = (state.astype(F32) + gain * normed * valid).astype(BF16)
    masked_up = upstream * valid
    gain_sum = jnp.sum(masked_up * normed, axis=0, keepdims=True)
    scaled = masked_up * gain
    grad_output = (
        inverse
        * (
            scaled
            - jnp.mean(scaled, axis=1, keepdims=True)
            - normed * jnp.mean(scaled * normed, axis=1, keepdims=True)
        )
    ).astype(BF16)
    grad_act = dot(grad_output, w_out_ref[...], (1, 1))
    slope = sigma * (1.0 + preact * (1.0 - sigma))
    grad_pre = (grad_act * slope).astype(BF16)
    return new_state, gain_sum, activated, grad_output, grad_pre


def inner_kernel(
    cfg,
    len_hbm,
    mask_hbm,
    state_hbm,
    tiles_hbm,
    up_hbm,
    w_in_hbm,
    w_out_hbm,
    gain_hbm,
    new_ref,
    own_ref,
    spread_ref,
    grad_in_ref,
    grad_out_ref,
    gain_sum_ref,
    rim_band_ref,
    rim_message_ref,
    rim_direct_ref,
    valid_ref,
    state_rim_ref,
    up_rim_ref,
    w_in_ref,
    w_out_ref,
    gain_ref,
    len_ref,
    mask_ref,
    state_ref,
    tiles_ref,
    up_ref,
    ext_ref,
    band_ref,
    sems,
):
    bs, offsets = cfg
    rim = (offsets - 1) // 2 * bs
    rows, latent = state_ref.shape
    per = rim // bs
    blocks = rows // bs
    width = 3 * rim
    low, inner, high = pl.ds(0, rim), pl.ds(rim, rows - 2 * rim), pl.ds(rows - rim, rim)
    late = pl.ds(rim, rim)

    pairs = [(len_hbm, len_ref), (mask_hbm, mask_ref), (state_hbm, state_ref)]
    pairs += [(tiles_hbm.at[o], tiles_ref.at[o]) for o in range(offsets)]
    first = len(pairs)
    pairs += [(w_in_hbm, w_in_ref), (w_out_hbm, w_out_ref), (gain_hbm, gain_ref)]
    pairs += [(up_hbm.at[inner, :], up_ref)]
    second = len(pairs)
    pairs += [(state_hbm.at[low, :], state_rim_ref.at[low, :]), (state_hbm.at[high, :], state_rim_ref.at[late, :])]
    pairs += [(up_hbm.at[low, :], up_rim_ref.at[low, :]), (up_hbm.at[high, :], up_rim_ref.at[late, :])]
    copies = [pltpu.make_async_copy(a, b, sems.at[i]) for i, (a, b) in enumerate(pairs)]
    for copy in copies:
        copy.start()
    for copy in copies[:first]:
        copy.wait()

    valid_ref[...] = validity(len_ref, 0, blocks, bs)
    ext_ref[...] = (state_ref[...].astype(F32) * valid_ref[...]).astype(BF16)
    message = []
    for chunk in range(1, rows // rim - 1):
        band = band_ref.at[chunk - 1]
        fill_band(band, tiles_ref, mask_ref, chunk * per, per, bs, offsets)
        message.append(dot(band[...], ext_ref[(chunk - 1) * rim : (chunk - 1) * rim + width, :], (1, 0)))
    inner = slice(rim, rows - rim)
    valid = valid_ref[inner, :]
    message = (jnp.concatenate(message, axis=0) * valid).astype(BF16)
    for copy in copies[first:second]:
        copy.wait()
    state = state_ref[inner, :]
    upstream = up_ref[...].astype(F32)
    direct_part = dot(state, w_in_ref[:latent, :], (1, 0))
    new_state, gain_sum, activated, grad_output, grad_pre = node_rows(
        state, message, direct_part, upstream, valid, w_in_ref, w_out_ref, gain_ref[...]
    )
    new_ref[...] = new_state
    gain_sum_ref[...] = gain_sum
    grad_out_ref[...] = dot(activated, grad_output, (0, 0))
    grad_in_ref[:latent, :] = dot(state, grad_pre, (0, 0))
    grad_in_ref[latent:, :] = dot(message, grad_pre, (0, 0))
    own_ref[...] = upstream + dot(grad_pre, w_in_ref[:latent, :], (1, 1))
    grad_message = dot(grad_pre, w_in_ref[latent:, :], (1, 1)).astype(BF16)
    grad_message = (grad_message.astype(F32) * valid).astype(BF16)
    spread_ref[...] = jnp.zeros_like(spread_ref)
    for chunk in range(1, rows // rim - 1):
        reach = slice((chunk - 1) * rim, (chunk - 1) * rim + width)
        spread_ref[reach, :] += dot(
            band_ref[chunk - 1], grad_message[(chunk - 1) * rim : chunk * rim, :], (0, 0)
        )

    for end in range(2):
        first = end * (blocks - per)
        band = rim_band_ref.at[end]
        fill_band(band, tiles_ref, mask_ref, first, per, bs, offsets)
        here = slice(end * rim, (end + 1) * rim)
        if end == 0:
            rim_message_ref[here, :] = dot(band[:, rim:], ext_ref[: 2 * rim, :], (1, 0))
        else:
            rim_message_ref[here, :] = dot(band[:, : 2 * rim], ext_ref[rows - 2 * rim :, :], (1, 0))
        rim_direct_ref[here, :] = dot(
            state_ref[first * bs : first * bs + rim, :], w_in_ref[:latent, :], (1, 0)
        )
    for copy in copies[second:]:
        copy.wait()


def rim_kernel(
    scale,
    valid_ref,
    state_ref,
    up_ref,
    w_in_ref,
    w_out_ref,
    gain_ref,
    band_ref,
    message_ref,
    direct_ref,
    inner_in_ref,
    inner_out_ref,
    inner_gain_ref,
    odd_ref,
    even_ref,
    send_ref,
    new_ref,
    pre_ref,
    grad_in_ref,
    grad_out_ref,
):
    rows = valid_ref.shape[0]
    rim, latent = odd_ref.shape
    side, me = place()
    odd = odd_ref[...]
    even = even_ref[...]
    low = jnp.where(side == 0, odd, even)
    high = jnp.where(side == 0, even, odd)
    valid = jnp.concatenate([valid_ref[:rim, :], valid_ref[rows - rim :, :]], axis=0)
    arrived = jnp.concatenate(
        [dot(band_ref[0, :, :rim], low, (1, 0)), dot(band_ref[1, :, 2 * rim :], high, (1, 0))], axis=0
    )
    message = ((message_ref[...] + arrived) * valid).astype(BF16)
    state = state_ref[...]
    upstream = up_ref[...].astype(F32)
    new_state, gain_sum, activated, grad_output, grad_pre = node_rows(
        state, message, direct_ref[...], upstream, valid, w_in_ref, w_out_ref, gain_ref[...]
    )
    new_ref[...] = new_state
    gain_sum = gain_sum + inner_gain_ref[...]
    grad_out_ref[...] = inner_out_ref[...] + dot(activated, grad_output, (0, 0))
    grad_in_ref[:latent, :] = inner_in_ref[:latent, :] + dot(state, grad_pre, (0, 0))
    grad_in_ref[latent:, :] = inner_in_ref[latent:, :] + dot(message, grad_pre, (0, 0))
    pre_ref[...] = grad_pre

    count = send_ref.shape[0] * send_ref.shape[1]
    n_in = grad_in_ref.shape[0] // count
    n_out = grad_out_ref.shape[0] // count
    top = lax.broadcasted_iota(jnp.int32, (GAIN_ROWS, latent), 0) == 0
    for piece in range(count):
        turn = lax.bitwise_xor(me, piece)
        half = lax.bitwise_and(turn, 1)
        slot = lax.shift_right_logical(turn, 1)
        send_ref[half, slot, :n_in, :] = (grad_in_ref[piece * n_in : (piece + 1) * n_in, :] * scale).astype(BF16)
        send_ref[half, slot, n_in : n_in + n_out, :] = (
            grad_out_ref[piece * n_out : (piece + 1) * n_out, :] * scale
        ).astype(BF16)
        if piece == 0:
            tail = jnp.where(top, gain_sum * scale, 0.0)
        else:
            tail = jnp.zeros((GAIN_ROWS, latent), F32)
        send_ref[half, slot, n_in + n_out :, :] = tail.astype(BF16)


def back_kernel(
    valid_ref,
    up_ref,
    w_in_ref,
    band_ref,
    pre_ref,
    new_inner_ref,
    new_rim_ref,
    own_inner_ref,
    spread_inner_ref,
    spill_odd_ref,
    spill_even_ref,
    own_ref,
    new_ref,
    out_ref,
    inner_ref,
    sems,
):
    rim, latent = spill_odd_ref.shape
    rows = valid_ref.shape[0]
    side, _ = place()
    inner = pl.ds(rim, rows - 2 * rim)
    news = [
        pltpu.make_async_copy(new_rim_ref.at[pl.ds(0, rim), :], new_ref.at[pl.ds(0, rim), :], sems.at[0]),
        pltpu.make_async_copy(new_inner_ref, new_ref.at[inner, :], sems.at[1]),
        pltpu.make_async_copy(
            new_rim_ref.at[pl.ds(rim, rim), :], new_ref.at[pl.ds(rows - rim, rim), :], sems.at[2]
        ),
    ]
    for copy in news:
        copy.start()
    valid = jnp.concatenate([valid_ref[:rim, :], valid_ref[rows - rim :, :]], axis=0)
    grad_pre = pre_ref[...]
    grad_message = dot(grad_pre, w_in_ref[latent:, :], (1, 1)).astype(BF16)
    grad_message = (grad_message.astype(F32) * valid).astype(BF16)
    left = dot(band_ref[0], grad_message[:rim, :], (0, 0))
    right = dot(band_ref[1], grad_message[rim:, :], (0, 0))
    low = left[:rim, :].astype(BF16)
    high = right[2 * rim :, :].astype(BF16)
    spill_odd_ref[...] = jnp.where(side == 0, low, high)
    spill_even_ref[...] = jnp.where(side == 0, high, low)
    spread = spread_inner_ref[...] + jnp.concatenate([left[rim:, :], right[: 2 * rim, :]], axis=0)
    spread = spread * valid_ref[...]
    inner_ref[...] = (own_inner_ref[...] + spread[rim : rows - rim, :]).astype(BF16)
    inside = pltpu.make_async_copy(inner_ref, out_ref.at[inner, :], sems.at[3])
    inside.start()
    own = up_ref[...].astype(F32) + dot(grad_pre, w_in_ref[:latent, :], (1, 1))
    own_ref[...] = own + jnp.concatenate([spread[:rim, :], spread[rows - rim :, :]], axis=0)
    for copy in news:
        copy.wait()
    inside.wait()


def finish_kernel(started_ref, valid_ref, own_ref, odd_ref, even_ref, out_ref, held_ref, sems):
    rows = valid_ref.shape[0]
    rim = odd_ref.shape[0]
    side, _ = place()
    odd = odd_ref[...].astype(F32)
    even = even_ref[...].astype(F32)
    copies = []
    for end in range(2):
        first = end * (rows - rim)
        there = slice(end * rim, (end + 1) * rim)
        back = jnp.where(side == end, odd, even)
        held_ref[there, :] = (own_ref[there, :] + back * valid_ref[first : first + rim, :]).astype(BF16)
        copy = pltpu.make_async_copy(
            held_ref.at[pl.ds(end * rim, rim), :], out_ref.at[pl.ds(first, rim), :], sems.at[end]
        )
        copy.start()
        copies.append(copy)
    for copy in copies:
        copy.wait()


def unpack_kernel(*refs):
    pieces = refs[:-3]
    grad_in_ref, grad_out_ref, gain_ref = refs[-3:]
    _, me = place()
    count = len(pieces)
    n_in = grad_in_ref.shape[0] // count
    n_out = grad_out_ref.shape[0] // count
    for turn in range(count):
        source = pieces[turn // 2 + turn % 2 * (count // 2)]
        piece = lax.bitwise_xor(me, turn)
        at_in = pl.ds(pl.multiple_of(piece * n_in, n_in), n_in)
        at_out = pl.ds(pl.multiple_of(piece * n_out, n_out), n_out)
        grad_in_ref[at_in, :] = source[:n_in, :].astype(F32)
        grad_out_ref[at_out, :] = source[n_in : n_in + n_out, :].astype(F32)

        @pl.when(piece == 0)
        def _():
            gain_ref[...] = source[n_in + n_out :, :].astype(F32)[:1, :]


def swap(x, axis, turn):
    count = lax.axis_size(axis)
    return lax.ppermute(x, axis, [(i, i ^ turn) for i in range(count)])


def gathered(x, axis):
    count = lax.axis_size(axis)
    if count & (count - 1) == 0:
        return [x] + [swap(x, axis, k) for k in range(1, count)]
    moved = [x] + [
        lax.ppermute(x, axis, [(i, (i + k) % count) for i in range(count)]) for k in range(1, count)
    ]
    order = (lax.axis_index(axis) - jnp.arange(count)) % count
    stacked = jnp.stack(moved)[order]
    return [stacked[k] for k in range(count)]


def tree_sum(parts):
    parts = [part.astype(F32) for part in parts]
    while len(parts) > 1:
        paired = [parts[i] + parts[i + 1] for i in range(0, len(parts) - 1, 2)]
        parts = paired + parts[len(parts) - len(parts) % 2 :]
    return parts[0]


def vmem(count):
    return [pl.BlockSpec(memory_space=pltpu.VMEM)] * count


def shapes(*given):
    return tuple(jax.ShapeDtypeStruct(shape, dtype) for shape, dtype in given)


def kernel(body, name, inputs, outputs, scratch=(), flops=0, moved=0, aliases=None):
    far, arrays = inputs
    spaces = [out.memory_space if hasattr(out, "memory_space") else pltpu.VMEM for out in outputs]
    call = pl.pallas_call(
        body,
        out_shape=outputs,
        in_specs=[pl.BlockSpec(memory_space=pltpu.HBM)] * far + vmem(arrays),
        out_specs=tuple(pl.BlockSpec(memory_space=space) for space in spaces),
        scratch_shapes=list(scratch),
        input_output_aliases=aliases or {},
        compiler_params=pltpu.CompilerParams(vmem_limit_bytes=VMEM_LIMIT),
        cost_estimate=pl.CostEstimate(flops=flops, bytes_accessed=moved, transcendentals=0),
        name=name,
    )

    def run(*given):
        placed = [pltpu.with_memory_space_constraint(x, pltpu.HBM) for x in given[:far]]
        return call(*placed, *given[far:])

    return run


def local(node_state, edge_tiles, block_mask, block_len, w_in, w_out, gain, upstream):
    rows, latent = node_state.shape
    offsets, bs = edge_tiles.shape[1:]
    rim = (offsets - 1) // 2 * bs
    inside = rows - 2 * rim
    width = 3 * rim
    dom = lax.axis_size("dom")
    rep = lax.axis_size("rep")
    total = dom * rep
    scale = 1.0 / math.sqrt(rows * total)
    ring = ("dom", "rep")
    even_pairs = [(i, i ^ 1) for i in range(total)]
    odd_pairs = [(i, (i + 1) % total if i % 2 else (i - 1) % total) for i in range(total)]
    gain_row = gain.reshape(1, latent)
    tiles = jnp.transpose(edge_tiles, (1, 0, 2))

    to_odd, to_even = kernel(
        functools.partial(pack_kernel, bs),
        "pack_rims",
        (2, 0),
        shapes(((rim, latent), BF16), ((rim, latent), BF16)),
        [
            pltpu.VMEM((2, rim, latent), BF16),
            pltpu.SMEM(block_len.shape, jnp.int32),
            pltpu.SemaphoreType.DMA((3,)),
        ],
    )(block_len, node_state)
    from_odd = lax.ppermute(to_odd, ring, odd_pairs)
    from_even = lax.ppermute(to_even, ring, even_pairs)

    work = 2 * inside * latent * (width + 5 * latent + 2 * latent + 2 * latent + width)
    new_inner, own_inner, spread_inner, sum_in, sum_out, sum_gain, band, message, direct, *kept = kernel(
        functools.partial(inner_kernel, (bs, offsets)),
        "inner_rows",
        (8, 0),
        shapes(
            ((inside, latent), BF16),
            ((inside, latent), F32),
            ((rows, latent), F32),
            (w_in.shape, F32),
            (w_out.shape, F32),
            ((1, latent), F32),
            ((2, rim, width), BF16),
            ((2 * rim, latent), F32),
            ((2 * rim, latent), F32),
            ((rows, 1), F32),
            ((2 * rim, latent), BF16),
            ((2 * rim, latent), BF16),
            (w_in.shape, BF16),
            (w_out.shape, BF16),
            ((1, latent), F32),
        ),
        [
            pltpu.SMEM(block_len.shape, jnp.int32),
            pltpu.SMEM(block_mask.shape, jnp.int32),
            pltpu.VMEM((rows, latent), BF16),
            pltpu.VMEM(tiles.shape, BF16),
            pltpu.VMEM((inside, latent), BF16),
            pltpu.VMEM((rows, latent), BF16),
            pltpu.VMEM((inside // rim, rim, width), BF16),
            pltpu.SemaphoreType.DMA((11 + offsets,)),
        ],
        flops=work,
        moved=10 * 1024 * 1024,
    )(block_len, block_mask, node_state, tiles, upstream, w_in, w_out, gain_row)

    n_in, n_out = w_in.shape[0] // dom, w_out.shape[0] // dom
    piece_rows = n_in + n_out + GAIN_ROWS
    send, new_rim, pre_rim = kernel(
        functools.partial(rim_kernel, scale),
        "rim_rows",
        (0, 14),
        shapes(
            ((2, dom // 2, piece_rows, latent), BF16),
            ((2 * rim, latent), BF16),
            ((2 * rim, latent), BF16),
        ),
        [pltpu.VMEM(w_in.shape, F32), pltpu.VMEM(w_out.shape, F32)],
        flops=work,
        moved=8 * 1024 * 1024,
    )(
        *kept,
        band, message, direct, sum_in, sum_out, sum_gain, from_odd, from_even,
    )

    valid, _, up_rim, w_in_near, _, _ = kept
    other = swap(send[1], "dom", 1)
    held = (send[0].astype(F32) + other.astype(F32)).astype(BF16)
    held = [held[k] for k in range(dom // 2)]
    spill_odd, spill_even, own_rim, new_state, grad_state = kernel(
        back_kernel,
        "rim_back",
        (0, 9),
        shapes(((rim, latent), BF16), ((rim, latent), BF16), ((2 * rim, latent), F32))
        + (pltpu.HBM((rows, latent), BF16), pltpu.HBM((rows, latent), BF16)),
        [pltpu.VMEM((inside, latent), BF16), pltpu.SemaphoreType.DMA((4,))],
        flops=2 * inside * latent * (2 * latent + width),
        moved=4 * 1024 * 1024,
    )(valid, up_rim, w_in_near, band, pre_rim, new_inner, new_rim, own_inner, spread_inner)

    parts = [held[0]] + [swap(held[k], "dom", 2 * k) for k in range(1, dom // 2)]
    quarter = sum(part.astype(F32) for part in parts).astype(BF16)
    planes = gathered(quarter, "rep")
    back_odd = lax.ppermute(spill_odd, ring, odd_pairs)
    back_even = lax.ppermute(spill_even, ring, even_pairs)
    mine = tree_sum(planes).astype(BF16)
    near = [mine] + [swap(mine, "dom", 2 * k) for k in range(1, dom // 2)]
    near[-1], back_odd, back_even = lax.optimization_barrier((near[-1], back_odd, back_even))
    (grad_state,) = kernel(
        finish_kernel,
        "finish_state",
        (1, 4),
        (pltpu.HBM((rows, latent), BF16),),
        [pltpu.VMEM((2 * rim, latent), BF16), pltpu.SemaphoreType.DMA((2,))],
        aliases={0: 0},
    )(grad_state, valid, own_rim, back_odd, back_even)
    other = swap(jnp.stack(near), "dom", 1)
    other = [other[k] for k in range(dom // 2)]
    *other, grad_state = lax.optimization_barrier((*other, grad_state))
    grad_w_in, grad_w_out, grad_gain = kernel(
        unpack_kernel,
        "unpack_sums",
        (0, dom),
        shapes((w_in.shape, F32), (w_out.shape, F32), ((1, latent), F32)),
    )(*near, *other)
    return new_state, grad_state, grad_w_in, grad_w_out, grad_gain.reshape(latent)


def solution(mesh):
    placed = (
        P(("dom", "rep"), None),
        P(("dom", "rep"), None, None),
        P(("dom", "rep"), None),
        P(("dom", "rep")),
        P(),
        P(),
        P(),
        P(("dom", "rep"), None),
    )
    return jax.shard_map(
        local,
        mesh=mesh,
        in_specs=placed,
        out_specs=(P(("dom", "rep"), None), P(("dom", "rep"), None), P(), P(), P()),
        check_vma=False,
    )
```

time: 50.2 us -> 42.8 us (0.85)
  local copies, waits for them, and re-layouts: 8.35 us -> 0.04 us
  waiting for transfers between devices: 10.6 us -> 12.5 us
  starting transfers between devices: 20.1 us -> 19.3 us
    unnamed x22 -> x0, local copies, waits for them, and re-layouts: 8.32 us -> none
    ppermute x1, waiting for transfers between devices: 0.01 us -> 1.74 us  [local(): from_even = lax.ppermute(to_even, ring, even_pairs)]
    ppermute x1, starting transfers between devices: 1.67 us -> 0.01 us  [local(): back_even = lax.ppermute(spill_even, ring, even_pairs)]
    ppermute x11, waiting for transfers between devices: 8.4 us -> 7.54 us  [swap(): return lax.ppermute(x, axis, [(i, i ^ turn) for i in range(count)])]
    ppermute x1, starting transfers between devices: 0.35 us -> 1.11 us  [local(): back_odd = lax.ppermute(spill_odd, ring, odd_pairs)]
    ppermute x1, waiting for transfers between devices: 2.21 us -> 2.74 us  [local(): back_odd = lax.ppermute(spill_odd, ring, odd_pairs)]
    pallas_call x5 -> x6, Pallas kernels: 9.74 us -> 9.86 us  [run(): return call(*placed, *given[far:])]
  transfers between devices with their start and end apart: 15 -> 15, of which waited for: 8 -> 10; matrix products, arithmetic and copies ran while one was open for 0% -> 0% of each run, Pallas kernels for 10% -> 15%
where the time goes in v3:
time: 42.8 us; the launch traced here: 42.6 us
  starting transfers between devices  19.3 us (45%)
  waiting for transfers between devices  12.5 us (29%)
  Pallas kernels  9.86 us (23%)
  between operations  0.74 us (2%)
    ppermute x11, starting transfers between devices, swap(): return lax.ppermute(x, axis, [(i, i ^ turn) for i in range(count)])  11.7 us
    pallas_call x6, Pallas kernels, run(): return call(*placed, *given[far:])  9.86 us
    ppermute x11, waiting for transfers between devices, swap(): return lax.ppermute(x, axis, [(i, i ^ turn) for i in range(count)])  7.54 us
    ppermute x1, starting transfers between devices, local(): from_odd = lax.ppermute(to_odd, ring, odd_pairs)  6.44 us
    ppermute x1, waiting for transfers between devices, local(): back_odd = lax.ppermute(spill_odd, ring, odd_pairs)  2.74 us
    ppermute x1, waiting for transfers between devices, local(): from_even = lax.ppermute(to_even, ring, even_pairs)  1.74 us
    ppermute x1, starting transfers between devices, local(): back_odd = lax.ppermute(spill_odd, ring, odd_pairs)  1.11 us
  transfers between devices with their start and end apart: 15, of which 10 were waited for; matrix products, arithmetic and copies ran while one was open for 0% of the time, Pallas kernels for 15%

profile of v3, /device:TPU:0, one launch (start us, length us, event | category | flops | bytes accessed | tf_op | source)
XLA Modules:
  0.0 42.6 jit_solution(6731598121012763257)
XLA Ops:
  0.6 1.1 %pack_rims.1 = (bf16[256,256]{1,0:T(8,128)(2,1)S(1)}, bf16[256,256]{1,0:T(8,128)(2,1)S(1)}) custom-call(s32[8]{0:T(128)} %len_ref.1, bf16[1024,256]{1,0:T(8,128)(2,1)} %state_ref.1), custom_call_target="tpu_custom_call" | custom-call | tf_op jit(solution)/shard_map/pack_rims/pallas_call | solution.py:416
  1.7 6.4 %collective-permute-start = (bf16[256,256]{1,0:T(8,128)(2,1)S(1)}, bf16[256,256]{1,0:T(8,128)(2,1)S(1)}, u32[]{:S(2)}, u32[]{:S(2)}) collective-permute-start(bf16[256,256]{1,0:T(8,128)(2,1)S(1)} %get-tuple-element.53), channel_id=1, source_target_pairs={{0,31},{1,2},{2,1},{3,4},{4,3},{5,6},{6,5},{7,8},{8,7},{9,10},{10,... | collective-permute-start | bytes 393224 | tf_op jit(solution)/shard_map/ppermute | solution.py:448
  8.1 4.2 %inner_rows.1 = (bf16[512,256]{1,0:T(8,128)(2,1)S(1)}, f32[512,256]{1,0:T(8,128)S(1)}, f32[1024,256]{1,0:T(8,128)S(1)}, f32[512,256]{1,0:T(8,128)S(1)}, f32[256,...) custom-call(s32[8]{0:T(128)} %len_ref.1, ...), custom_call_target="tpu_custom_call" | custom-call | flops 1006632960 | bytes 10485760 | tf_op jit(solution)/shard_map/inner_rows/pallas_call | solution.py:416
  12.3 1.7 %collective-permute-done.1.even_ref = bf16[256,256]{1,0:T(8,128)(2,1)S(1)} collective-permute-done((bf16[256,256]{1,0:T(8,128)(2,1)S(1)}, bf16[256,256]{1,0:T(8,128)(2,1)S(1)}, u32[]{:S(2)}, u32[]{:S(2)}) %collective-permute-start.1) | collective-permute-done | bytes 131104 | tf_op jit(solution)/shard_map/ppermute | solution.py:449
  14.1 1.4 %rim_rows.1 = (bf16[2,4,104,256]{3,2,1,0:T(8,128)(2,1)S(1)}, bf16[512,256]{1,0:T(8,128)(2,1)S(1)}, bf16[512,256]{1,0:T(8,128)(2,1)S(1)}) custom-call(f32[1024,1]{1,0:T(8,128)S(1)} %get-tuple-element.41.valid_ref, bf16[512,256]{1,0:T(8,128)(2,1)S(1)} %get-tuple-element.45.state_ref, bf16[512,256]{1,0:T(8,128)(2,1)S(1)} %get-tuple-element.42.up_ref, ...), custom_call_target="tpu_custom_call" | custom-call | flops 1006632960 | bytes 8388608 | tf_op jit(solution)/shard_map/rim_rows/pallas_call | solution.py:416
  15.5 1.5 %collective-permute-done.2 = bf16[4,104,256]{2,1,0:T(8,128)(2,1)S(1)} collective-permute-done((bf16[4,104,256]{2,1,0:T(8,128)(2,1)S(1)}, bf16[4,104,256]{2,1,0:T(8,128)(2,1)S(1)}, u32[]{:S(2)}, u32[]{:S(2)}) %collective-permute-start.2) | collective-permute-done | bytes 213024 | tf_op jit(solution)/shard_map/ppermute | solution.py:368
  17.1 1.6 %collective-permute-start.3 = (bf16[104,256]{1,0:T(8,128)(2,1)S(1)}, bf16[104,256]{1,0:T(8,128)(2,1)S(1)}, u32[]{:S(2)}, u32[]{:S(2)}) collective-permute-start(bf16[104,256]{1,0:T(8,128)(2,1)S(1)} %get-tuple-element.81), channel_id=1, source_target_pairs={{0,8},{4,12},{8,0},{12,4},{16,24},{20,28},{24,16},{28,20},{1,9},{5... | collective-permute-start | bytes 159752 | tf_op jit(solution)/shard_map/ppermute | solution.py:368
  18.6 1.5 %collective-permute-start.5 = (bf16[104,256]{1,0:T(8,128)(2,1)S(1)}, bf16[104,256]{1,0:T(8,128)(2,1)S(1)}, u32[]{:S(2)}, u32[]{:S(2)}) collective-permute-start(bf16[104,256]{1,0:T(8,128)(2,1)S(1)} %get-tuple-element.82), channel_id=1, source_target_pairs={{0,24},{4,28},{8,16},{12,20},{16,8},{20,12},{24,0},{28,4},{1,25},{... | collective-permute-start | bytes 159752 | tf_op jit(solution)/shard_map/ppermute | solution.py:368
  20.6 0.8 %collective-permute-done.3 = bf16[104,256]{1,0:T(8,128)(2,1)S(1)} collective-permute-done((bf16[104,256]{1,0:T(8,128)(2,1)S(1)}, bf16[104,256]{1,0:T(8,128)(2,1)S(1)}, u32[]{:S(2)}, u32[]{:S(2)}) %collective-permute-start.3) | collective-permute-done | bytes 53280 | tf_op jit(solution)/shard_map/ppermute | solution.py:368
  21.4 2.3 %collective-permute-done.5 = bf16[104,256]{1,0:T(8,128)(2,1)S(1)} collective-permute-done((bf16[104,256]{1,0:T(8,128)(2,1)S(1)}, bf16[104,256]{1,0:T(8,128)(2,1)S(1)}, u32[]{:S(2)}, u32[]{:S(2)}) %collective-permute-start.5) | collective-permute-done | bytes 53280 | tf_op jit(solution)/shard_map/ppermute | solution.py:368
  23.7 0.7 %collective-permute-done.4 = bf16[104,256]{1,0:T(8,128)(2,1)S(1)} collective-permute-done((bf16[104,256]{1,0:T(8,128)(2,1)S(1)}, bf16[104,256]{1,0:T(8,128)(2,1)S(1)}, u32[]{:S(2)}, u32[]{:S(2)}) %collective-permute-start.4) | collective-permute-done | bytes 53280 | tf_op jit(solution)/shard_map/ppermute | solution.py:368
  24.4 1.8 %collective-permute-start.8 = (bf16[104,256]{1,0:T(8,128)(2,1)S(1)}, bf16[104,256]{1,0:T(8,128)(2,1)S(1)}, u32[]{:S(2)}, u32[]{:S(2)}) collective-permute-start(bf16[104,256]{1,0:T(8,128)(2,1)S(1)} %fusion.3), channel_id=1, source_target_pairs={{0,3},{1,2},{2,1},{3,0},{4,7},{5,6},{6,5},{7,4},{8,11},{9,10},{10,... | collective-permute-start | bytes 159752 | tf_op jit(solution)/shard_map/ppermute | solution.py:368
  26.3 1.1 %collective-permute-start.7 = (bf16[104,256]{1,0:T(8,128)(2,1)S(1)}, bf16[104,256]{1,0:T(8,128)(2,1)S(1)}, u32[]{:S(2)}, u32[]{:S(2)}) collective-permute-start(bf16[104,256]{1,0:T(8,128)(2,1)S(1)} %fusion.3), channel_id=1, source_target_pairs={{0,2},{1,3},{2,0},{3,1},{4,6},{5,7},{6,4},{7,5},{8,10},{9,11},{10,... | collective-permute-start | bytes 159752 | tf_op jit(solution)/shard_map/ppermute | solution.py:368
  27.3 1.6 %collective-permute-start.6 = (bf16[104,256]{1,0:T(8,128)(2,1)S(1)}, bf16[104,256]{1,0:T(8,128)(2,1)S(1)}, u32[]{:S(2)}, u32[]{:S(2)}) collective-permute-start(bf16[104,256]{1,0:T(8,128)(2,1)S(1)} %fusion.3), channel_id=1, source_target_pairs={{0,1},{1,0},{2,3},{3,2},{4,5},{5,4},{6,7},{7,6},{8,9},{9,8},{10,11... | collective-permute-start | bytes 159752 | tf_op jit(solution)/shard_map/ppermute | solution.py:368
  28.9 1.5 %rim_back.1 = (bf16[256,256]{1,0:T(8,128)(2,1)S(1)}, bf16[256,256]{1,0:T(8,128)(2,1)S(1)}, f32[512,256]{1,0:T(8,128)S(1)}, bf16[1024,256]{1,0:T(8,128)(2,1)}, bf16[1024,256]{1,0:T(8,128)(2,1)}) custom-call(f32[1024,1]{1,0:T(8,128)S(1)} %get-tuple-element.41.valid_ref, bf16[512,256]{1,0:T(8,128)(2,1)S(1)} %get-tuple-element.42.up_ref, ...), custom_call_target="tpu_custom_call" | custom-call | flops 335544320 | bytes 4194304 | tf_op jit(solution)/shard_map/rim_back/pallas_call | solution.py:416
  30.4 1.1 %collective-permute-start.12 = (bf16[256,256]{1,0:T(8,128)(2,1)S(1)}, bf16[256,256]{1,0:T(8,128)(2,1)S(1)}, u32[]{:S(2)}, u32[]{:S(2)}) collective-permute-start(bf16[256,256]{1,0:T(8,128)(2,1)S(1)} %get-tuple-element.62), channel_id=1, source_target_pairs={{0,31},{1,2},{2,1},{3,4},{4,3},{5,6},{6,5},{7,8},{8,7},{9,10},{10,... | collective-permute-start | bytes 393224 | tf_op jit(solution)/shard_map/ppermute | solution.py:524
  31.5 1.6 %collective-permute-done.7 = bf16[104,256]{1,0:T(8,128)(2,1)S(1)} collective-permute-done((bf16[104,256]{1,0:T(8,128)(2,1)S(1)}, bf16[104,256]{1,0:T(8,128)(2,1)S(1)}, u32[]{:S(2)}, u32[]{:S(2)}) %collective-permute-start.7) | collective-permute-done | bytes 53280 | tf_op jit(solution)/shard_map/ppermute | solution.py:368
  33.1 1.4 %collective-permute-start.11 = (bf16[104,256]{1,0:T(8,128)(2,1)S(1)}, bf16[104,256]{1,0:T(8,128)(2,1)S(1)}, u32[]{:S(2)}, u32[]{:S(2)}) collective-permute-start(bf16[104,256]{1,0:T(8,128)(2,1)S(1)} %add_convert_fusion.refs_0_), channel_id=1, source_target_pairs={{0,24},{4,28},{8,16},{12,20},{16,8},{20,12},{24,0},{28,4},{1,25},{... | collective-permute-start | bytes 159752 | tf_op jit(solution)/shard_map/ppermute | solution.py:368
  34.5 0.7 %collective-permute-start.10 = (bf16[104,256]{1,0:T(8,128)(2,1)S(1)}, bf16[104,256]{1,0:T(8,128)(2,1)S(1)}, u32[]{:S(2)}, u32[]{:S(2)}) collective-permute-start(bf16[104,256]{1,0:T(8,128)(2,1)S(1)} %add_convert_fusion.refs_0_), channel_id=1, source_target_pairs={{0,16},{4,20},{8,24},{12,28},{16,0},{20,4},{24,8},{28,12},{1,17},{... | collective-permute-start | bytes 159752 | tf_op jit(solution)/shard_map/ppermute | solution.py:368
  35.2 1.4 %collective-permute-start.9 = (bf16[104,256]{1,0:T(8,128)(2,1)S(1)}, bf16[104,256]{1,0:T(8,128)(2,1)S(1)}, u32[]{:S(2)}, u32[]{:S(2)}) collective-permute-start(bf16[104,256]{1,0:T(8,128)(2,1)S(1)} %add_convert_fusion.refs_0_), channel_id=1, source_target_pairs={{0,8},{4,12},{8,0},{12,4},{16,24},{20,28},{24,16},{28,20},{1,9},{5... | collective-permute-start | bytes 159752 | tf_op jit(solution)/shard_map/ppermute | solution.py:368
  36.7 2.7 %collective-permute-done.12.odd_ref = bf16[256,256]{1,0:T(8,128)(2,1)S(1)} collective-permute-done((bf16[256,256]{1,0:T(8,128)(2,1)S(1)}, bf16[256,256]{1,0:T(8,128)(2,1)S(1)}, u32[]{:S(2)}, u32[]{:S(2)}) %collective-permute-start.12) | collective-permute-done | bytes 131104 | tf_op jit(solution)/shard_map/ppermute | solution.py:524
  40.1 0.8 %finish_state.1 = bf16[1024,256]{1,0:T(8,128)(2,1)} custom-call(bf16[1024,256]{1,0:T(8,128)(2,1)} %get-tuple-element.65.started_ref, f32[1024,1]{1,0:T(8,128)S(1)} %get-tuple-element.41.valid_ref, f32[512,256]{1,0:T(8,128)S(1)} %get-tuple-element.66.own_ref, bf16[256,256]{1,0:T(8,128)(2,1)S(1)} %collective-permute-done.12.odd_ref, ...), custom_call_target="tpu_custom_call", output_to_operand_aliasing={{}: (0, {})} | custom-call | tf_op jit(solution)/shard_map/finish_state/pallas_call | solution.py:416
  41.0 0.6 %collective-permute-done.14 = bf16[4,104,256]{2,1,0:T(8,128)(2,1)S(1)} collective-permute-done((bf16[4,104,256]{2,1,0:T(8,128)(2,1)S(1)}, bf16[4,104,256]{2,1,0:T(8,128)(2,1)S(1)}, u32[]{:S(2)}, u32[]{:S(2)}) %collective-permute-start.14) | collective-permute-done | bytes 213024 | tf_op jit(solution)/shard_map/ppermute | solution.py:368
  41.6 1.0 %unpack_sums.1 = (f32[512,256]{1,0:T(8,128)}, f32[256,256]{1,0:T(8,128)}, f32[1,256]{1,0:T(1,128)}) custom-call(bf16[104,256]{1,0:T(8,128)(2,1)S(1)} %add_convert_fusion.refs_0_, bf16[104,256]{1,0:T(8,128)(2,1)S(1)} %collective-permute-done.9.refs_1_, bf16[104,256]{1,0:T(8,128)(2,1)S(1)} %collective-permute-done.10.refs_2_, ...), custom_call_target="tpu_custom_call" | custom-call | tf_op jit(solution)/shard_map/unpack_sums/pallas_call | solution.py:416
  (19 shorter events, 1.5 us)
Async XLA Ops:
  1.7 10.6 %collective-permute-start = (bf16[256,256]{1,0:T(8,128)(2,1)S(1)}, bf16[256,256]{1,0:T(8,128)(2,1)S(1)}, u32[]{:S(2)}, u32[]{:S(2)}) collective-permute-start(bf16[256,256]{1,0:T(8,128)(2,1)S(1)} %get-tuple-element.53), channel_id=1, source_target_pairs={{0,31},{1,2},{2,1},{3,4},{4,3},{5,6},{6,5},{7,8},{8,7},{9,10},{10,... | collective-permute-start | bytes 393224 | tf_op jit(solution)/shard_map/ppermute | solution.py:448
  8.1 5.9 %collective-permute-start.1 = (bf16[256,256]{1,0:T(8,128)(2,1)S(1)}, bf16[256,256]{1,0:T(8,128)(2,1)S(1)}, u32[]{:S(2)}, u32[]{:S(2)}) collective-permute-start(bf16[256,256]{1,0:T(8,128)(2,1)S(1)} %get-tuple-element.54), channel_id=1, source_target_pairs={{0,1},{1,0},{2,3},{3,2},{4,5},{5,4},{6,7},{7,6},{8,9},{9,8},{10,11... | collective-permute-start | bytes 393224 | tf_op jit(solution)/shard_map/ppermute | solution.py:449
  15.5 1.5 %collective-permute-start.2 = (bf16[4,104,256]{2,1,0:T(8,128)(2,1)S(1)}, bf16[4,104,256]{2,1,0:T(8,128)(2,1)S(1)}, u32[]{:S(2)}, u32[]{:S(2)}) collective-permute-start(bf16[4,104,256]{2,1,0:T(8,128)(2,1)S(1)} %slice_bitcast_fusion), channel_id=1, source_target_pairs={{0,4},{4,0},{8,12},{12,8},{16,20},{20,16},{24,28},{28,24},{1,5},{5... | collective-permute-start | bytes 638984 | tf_op jit(solution)/shard_map/ppermute | solution.py:368
  17.1 4.4 %collective-permute-start.3 = (bf16[104,256]{1,0:T(8,128)(2,1)S(1)}, bf16[104,256]{1,0:T(8,128)(2,1)S(1)}, u32[]{:S(2)}, u32[]{:S(2)}) collective-permute-start(bf16[104,256]{1,0:T(8,128)(2,1)S(1)} %get-tuple-element.81), channel_id=1, source_target_pairs={{0,8},{4,12},{8,0},{12,4},{16,24},{20,28},{24,16},{28,20},{1,9},{5... | collective-permute-start | bytes 159752 | tf_op jit(solution)/shard_map/ppermute | solution.py:368
  18.6 5.1 %collective-permute-start.5 = (bf16[104,256]{1,0:T(8,128)(2,1)S(1)}, bf16[104,256]{1,0:T(8,128)(2,1)S(1)}, u32[]{:S(2)}, u32[]{:S(2)}) collective-permute-start(bf16[104,256]{1,0:T(8,128)(2,1)S(1)} %get-tuple-element.82), channel_id=1, source_target_pairs={{0,24},{4,28},{8,16},{12,20},{16,8},{20,12},{24,0},{28,4},{1,25},{... | collective-permute-start | bytes 159752 | tf_op jit(solution)/shard_map/ppermute | solution.py:368
  20.1 4.3 %collective-permute-start.4 = (bf16[104,256]{1,0:T(8,128)(2,1)S(1)}, bf16[104,256]{1,0:T(8,128)(2,1)S(1)}, u32[]{:S(2)}, u32[]{:S(2)}) collective-permute-start(bf16[104,256]{1,0:T(8,128)(2,1)S(1)} %get-tuple-element.83), channel_id=1, source_target_pairs={{0,16},{4,20},{8,24},{12,28},{16,0},{20,4},{24,8},{28,12},{1,17},{... | collective-permute-start | bytes 159752 | tf_op jit(solution)/shard_map/ppermute | solution.py:368
  24.4 7.1 %collective-permute-start.8 = (bf16[104,256]{1,0:T(8,128)(2,1)S(1)}, bf16[104,256]{1,0:T(8,128)(2,1)S(1)}, u32[]{:S(2)}, u32[]{:S(2)}) collective-permute-start(bf16[104,256]{1,0:T(8,128)(2,1)S(1)} %fusion.3), channel_id=1, source_target_pairs={{0,3},{1,2},{2,1},{3,0},{4,7},{5,6},{6,5},{7,4},{8,11},{9,10},{10,... | collective-permute-start | bytes 159752 | tf_op jit(solution)/shard_map/ppermute | solution.py:368
  26.3 6.8 %collective-permute-start.7 = (bf16[104,256]{1,0:T(8,128)(2,1)S(1)}, bf16[104,256]{1,0:T(8,128)(2,1)S(1)}, u32[]{:S(2)}, u32[]{:S(2)}) collective-permute-start(bf16[104,256]{1,0:T(8,128)(2,1)S(1)} %fusion.3), channel_id=1, source_target_pairs={{0,2},{1,3},{2,0},{3,1},{4,6},{5,7},{6,4},{7,5},{8,10},{9,11},{10,... | collective-permute-start | bytes 159752 | tf_op jit(solution)/shard_map/ppermute | solution.py:368
  27.3 5.7 %collective-permute-start.6 = (bf16[104,256]{1,0:T(8,128)(2,1)S(1)}, bf16[104,256]{1,0:T(8,128)(2,1)S(1)}, u32[]{:S(2)}, u32[]{:S(2)}) collective-permute-start(bf16[104,256]{1,0:T(8,128)(2,1)S(1)} %fusion.3), channel_id=1, source_target_pairs={{0,1},{1,0},{2,3},{3,2},{4,5},{5,4},{6,7},{7,6},{8,9},{9,8},{10,11... | collective-permute-start | bytes 159752 | tf_op jit(solution)/shard_map/ppermute | solution.py:368
  30.4 9.0 %collective-permute-start.12 = (bf16[256,256]{1,0:T(8,128)(2,1)S(1)}, bf16[256,256]{1,0:T(8,128)(2,1)S(1)}, u32[]{:S(2)}, u32[]{:S(2)}) collective-permute-start(bf16[256,256]{1,0:T(8,128)(2,1)S(1)} %get-tuple-element.62), channel_id=1, source_target_pairs={{0,31},{1,2},{2,1},{3,4},{4,3},{5,6},{6,5},{7,8},{8,7},{9,10},{10,... | collective-permute-start | bytes 393224 | tf_op jit(solution)/shard_map/ppermute | solution.py:524
  31.5 8.4 %collective-permute-start.13 = (bf16[256,256]{1,0:T(8,128)(2,1)S(1)}, bf16[256,256]{1,0:T(8,128)(2,1)S(1)}, u32[]{:S(2)}, u32[]{:S(2)}) collective-permute-start(bf16[256,256]{1,0:T(8,128)(2,1)S(1)} %get-tuple-element.63), channel_id=1, source_target_pairs={{0,1},{1,0},{2,3},{3,2},{4,5},{5,4},{6,7},{7,6},{8,9},{9,8},{10,11... | collective-permute-start | bytes 393224 | tf_op jit(solution)/shard_map/ppermute | solution.py:525
  33.1 6.8 %collective-permute-start.11 = (bf16[104,256]{1,0:T(8,128)(2,1)S(1)}, bf16[104,256]{1,0:T(8,128)(2,1)S(1)}, u32[]{:S(2)}, u32[]{:S(2)}) collective-permute-start(bf16[104,256]{1,0:T(8,128)(2,1)S(1)} %add_convert_fusion.refs_0_), channel_id=1, source_target_pairs={{0,24},{4,28},{8,16},{12,20},{16,8},{20,12},{24,0},{28,4},{1,25},{... | collective-permute-start | bytes 159752 | tf_op jit(solution)/shard_map/ppermute | solution.py:368
  34.5 5.5 %collective-permute-start.10 = (bf16[104,256]{1,0:T(8,128)(2,1)S(1)}, bf16[104,256]{1,0:T(8,128)(2,1)S(1)}, u32[]{:S(2)}, u32[]{:S(2)}) collective-permute-start(bf16[104,256]{1,0:T(8,128)(2,1)S(1)} %add_convert_fusion.refs_0_), channel_id=1, source_target_pairs={{0,16},{4,20},{8,24},{12,28},{16,0},{20,4},{24,8},{28,12},{1,17},{... | collective-permute-start | bytes 159752 | tf_op jit(solution)/shard_map/ppermute | solution.py:368
  35.2 4.8 %collective-permute-start.9 = (bf16[104,256]{1,0:T(8,128)(2,1)S(1)}, bf16[104,256]{1,0:T(8,128)(2,1)S(1)}, u32[]{:S(2)}, u32[]{:S(2)}) collective-permute-start(bf16[104,256]{1,0:T(8,128)(2,1)S(1)} %add_convert_fusion.refs_0_), channel_id=1, source_target_pairs={{0,8},{4,12},{8,0},{12,4},{16,24},{20,28},{24,16},{28,20},{1,9},{5... | collective-permute-start | bytes 159752 | tf_op jit(solution)/shard_map/ppermute | solution.py:368
  40.1 1.5 %collective-permute-start.14 = (bf16[4,104,256]{2,1,0:T(8,128)(2,1)S(1)}, bf16[4,104,256]{2,1,0:T(8,128)(2,1)S(1)}, u32[]{:S(2)}, u32[]{:S(2)}) collective-permute-start(bf16[4,104,256]{2,1,0:T(8,128)(2,1)S(1)} %pad_maximum_fusion), channel_id=1, source_target_pairs={{0,4},{4,0},{8,12},{12,8},{16,20},{20,16},{24,28},{28,24},{1,5},{5... | collective-permute-start | bytes 638984 | tf_op jit(solution)/shard_map/ppermute | solution.py:368

commit v4 on v3

--- a/solution.py
+++ b/solution.py
@@ -35,27 +35,26 @@
     return lax.rem(index, 2), me
 
 
-def pack_kernel(bs, len_ref, state_ref, odd_ref, even_ref, held_ref, lens_ref, sems):
+def pack_kernel(bs, len_ref, state_ref, first_ref, last_ref, held_ref, lens_ref, sems):
     rows = state_ref.shape[0]
-    rim = odd_ref.shape[0]
+    rim = first_ref.shape[0]
     per = rim // bs
     copies = [
         pltpu.make_async_copy(len_ref, lens_ref, sems.at[0]),
-        pltpu.make_async_copy(state_ref.at[pl.ds(0, rim), :], held_ref.at[0], sems.at[1]),
-        pltpu.make_async_copy(state_ref.at[pl.ds(rows - rim, rim), :], held_ref.at[1], sems.at[2]),
+        pltpu.make_async_copy(state_ref.at[pl.ds(rows - rim, rim), :], held_ref.at[1], sems.at[1]),
+        pltpu.make_async_copy(state_ref.at[pl.ds(0, rim), :], held_ref.at[0], sems.at[2]),
     ]
     for copy in copies:
         copy.start()
-    side, _ = place()
     for copy in copies:
         copy.wait()
     blocks = rows // bs
     for j in range(per):
         here = slice(j * bs, (j + 1) * bs)
-        top = held_ref[0, here, :] * (sublane(bs) < lens_ref[j]).astype(F32).astype(BF16)
-        end = held_ref[1, here, :] * (sublane(bs) < lens_ref[blocks - per + j]).astype(F32).astype(BF16)
-        odd_ref[here, :] = jnp.where(side == 0, top, end)
-        even_ref[here, :] = jnp.where(side == 0, end, top)
+        first_ref[here, :] = held_ref[0, here, :] * (sublane(bs) < lens_ref[j]).astype(F32).astype(BF16)
+        last_ref[here, :] = held_ref[1, here, :] * (
+            sublane(bs) < lens_ref[blocks - per + j]
+        ).astype(F32).astype(BF16)
 
 
 def fill_band(band_ref, tiles_ref, mask_ref, first, per, bs, offsets):
@@ -218,8 +217,8 @@
     inner_in_ref,
     inner_out_ref,
     inner_gain_ref,
-    odd_ref,
-    even_ref,
+    low_ref,
+    high_ref,
     send_ref,
     new_ref,
     pre_ref,
@@ -227,15 +226,11 @@
     grad_out_ref,
 ):
     rows = valid_ref.shape[0]
-    rim, latent = odd_ref.shape
-    side, me = place()
-    odd = odd_ref[...]
-    even = even_ref[...]
-    low = jnp.where(side == 0, odd, even)
-    high = jnp.where(side == 0, even, odd)
+    rim, latent = low_ref.shape
+    _, me = place()
     valid = jnp.concatenate([valid_ref[:rim, :], valid_ref[rows - rim :, :]], axis=0)
     arrived = jnp.concatenate(
-        [dot(band_ref[0, :, :rim], low, (1, 0)), dot(band_ref[1, :, 2 * rim :], high, (1, 0))], axis=0
+        [dot(band_ref[0, :, :rim], low_ref[...], (1, 0)), dot(band_ref[1, :, 2 * rim :], high_ref[...], (1, 0))], axis=0
     )
     message = ((message_ref[...] + arrived) * valid).astype(BF16)
     state = state_ref[...]
@@ -429,12 +424,14 @@
     total = dom * rep
     scale = 1.0 / math.sqrt(rows * total)
     ring = ("dom", "rep")
+    next_pairs = [(i, (i + 1) % total) for i in range(total)]
+    back_pairs = [(i, (i - 1) % total) for i in range(total)]
     even_pairs = [(i, i ^ 1) for i in range(total)]
     odd_pairs = [(i, (i + 1) % total if i % 2 else (i - 1) % total) for i in range(total)]
     gain_row = gain.reshape(1, latent)
     tiles = jnp.transpose(edge_tiles, (1, 0, 2))
 
-    to_odd, to_even = kernel(
+    to_back, to_next = kernel(
         functools.partial(pack_kernel, bs),
         "pack_rims",
         (2, 0),
@@ -445,8 +442,8 @@
             pltpu.SemaphoreType.DMA((3,)),
         ],
     )(block_len, node_state)
-    from_odd = lax.ppermute(to_odd, ring, odd_pairs)
-    from_even = lax.ppermute(to_even, ring, even_pairs)
+    from_back = lax.ppermute(to_next, ring, next_pairs)
+    from_next = lax.ppermute(to_back, ring, back_pairs)
 
     work = 2 * inside * latent * (width + 5 * latent + 2 * latent + 2 * latent + width)
     new_inner, own_inner, spread_inner, sum_in, sum_out, sum_gain, band, message, direct, *kept = kernel(
@@ -500,7 +497,7 @@
         moved=8 * 1024 * 1024,
     )(
         *kept,
-        band, message, direct, sum_in, sum_out, sum_gain, from_odd, from_even,
+        band, message, direct, sum_in, sum_out, sum_gain, from_back, from_next,
     )
 
     valid, _, up_rim, w_in_near, _, _ = kept

time: 42.8 us -> 42.1 us (0.984)
  waiting for transfers between devices: 12.5 us -> 10.5 us
  starting transfers between devices: 19.3 us -> 20.7 us
    ppermute x2, waiting for transfers between devices: 1.75 us -> 0.17 us  [the longest x1 0.17 us: local(): from_next = lax.ppermute(to_back, ring, back_pairs)]
    ppermute x1, starting transfers between devices: 1.11 us -> 2.4 us  [local(): back_odd = lax.ppermute(spill_odd, ring, odd_pairs)]
    ppermute x11, waiting for transfers between devices: 7.54 us -> 6.38 us  [swap(): return lax.ppermute(x, axis, [(i, i ^ turn) for i in range(count)])]
    ppermute x1, waiting for transfers between devices: 2.74 us -> 3.19 us  [local(): back_odd = lax.ppermute(spill_odd, ring, odd_pairs)]
where the time goes in v4:
time: 42.1 us; the launch traced here: 41.9 us
  starting transfers between devices  20.7 us (49%)
  waiting for transfers between devices  10.5 us (25%)
  Pallas kernels  9.84 us (23%)
  between operations  0.73 us (2%)
    ppermute x11, starting transfers between devices, swap(): return lax.ppermute(x, axis, [(i, i ^ turn) for i in range(count)])  11.8 us
    pallas_call x6, Pallas kernels, run(): return call(*placed, *given[far:])  9.84 us
    ppermute x11, waiting for transfers between devices, swap(): return lax.ppermute(x, axis, [(i, i ^ turn) for i in range(count)])  6.38 us
    ppermute x1, starting transfers between devices, local(): from_next = lax.ppermute(to_back, ring, back_pairs)  3.42 us
    ppermute x1, waiting for transfers between devices, local(): back_odd = lax.ppermute(spill_odd, ring, odd_pairs)  3.19 us
    ppermute x1, starting transfers between devices, local(): from_back = lax.ppermute(to_next, ring, next_pairs)  3.08 us
    ppermute x1, starting transfers between devices, local(): back_odd = lax.ppermute(spill_odd, ring, odd_pairs)  2.4 us
  transfers between devices with their start and end apart: 15, of which 10 were waited for; matrix products, arithmetic and copies ran while one was open for 0% of the time, Pallas kernels for 15%

profile of v4, /device:TPU:0, one launch (start us, length us, event | category | flops | bytes accessed | tf_op | source)
XLA Modules:
  0.0 41.9 jit_solution(14433225385773689303)
XLA Ops:
  0.6 1.0 %pack_rims.1 = (bf16[256,256]{1,0:T(8,128)(2,1)S(1)}, bf16[256,256]{1,0:T(8,128)(2,1)S(1)}) custom-call(s32[8]{0:T(128)} %len_ref.1, bf16[1024,256]{1,0:T(8,128)(2,1)} %state_ref.1), custom_call_target="tpu_custom_call" | custom-call | tf_op jit(solution)/shard_map/pack_rims/pallas_call | solution.py:411
  1.7 3.1 %collective-permute-start = (bf16[256,256]{1,0:T(8,128)(2,1)S(1)}, bf16[256,256]{1,0:T(8,128)(2,1)S(1)}, u32[]{:S(2)}, u32[]{:S(2)}) collective-permute-start(bf16[256,256]{1,0:T(8,128)(2,1)S(1)} %get-tuple-element.53), channel_id=1, source_target_pairs={{0,1},{1,2},{2,3},{3,4},{4,5},{5,6},{6,7},{7,8},{8,9},{9,10},{10,1... | collective-permute-start | bytes 393224 | tf_op jit(solution)/shard_map/ppermute | solution.py:445
  4.8 3.4 %collective-permute-start.1 = (bf16[256,256]{1,0:T(8,128)(2,1)S(1)}, bf16[256,256]{1,0:T(8,128)(2,1)S(1)}, u32[]{:S(2)}, u32[]{:S(2)}) collective-permute-start(bf16[256,256]{1,0:T(8,128)(2,1)S(1)} %get-tuple-element.54), channel_id=1, source_target_pairs={{0,31},{1,0},{2,1},{3,2},{4,3},{5,4},{6,5},{7,6},{8,7},{9,8},{10,9... | collective-permute-start | bytes 393224 | tf_op jit(solution)/shard_map/ppermute | solution.py:446
  8.2 4.2 %inner_rows.1 = (bf16[512,256]{1,0:T(8,128)(2,1)S(1)}, f32[512,256]{1,0:T(8,128)S(1)}, f32[1024,256]{1,0:T(8,128)S(1)}, f32[512,256]{1,0:T(8,128)S(1)}, f32[256,...) custom-call(s32[8]{0:T(128)} %len_ref.1, ...), custom_call_target="tpu_custom_call" | custom-call | flops 1006632960 | bytes 10485760 | tf_op jit(solution)/shard_map/inner_rows/pallas_call | solution.py:411
  12.5 1.3 %rim_rows.1 = (bf16[2,4,104,256]{3,2,1,0:T(8,128)(2,1)S(1)}, bf16[512,256]{1,0:T(8,128)(2,1)S(1)}, bf16[512,256]{1,0:T(8,128)(2,1)S(1)}) custom-call(f32[1024,1]{1,0:T(8,128)S(1)} %get-tuple-element.41.valid_ref, bf16[512,256]{1,0:T(8,128)(2,1)S(1)} %get-tuple-element.45.state_ref, bf16[512,256]{1,0:T(8,128)(2,1)S(1)} %get-tuple-element.42.up_ref, ...), custom_call_target="tpu_custom_call" | custom-call | flops 1006632960 | bytes 8388608 | tf_op jit(solution)/shard_map/rim_rows/pallas_call | solution.py:411
  14.0 1.5 %collective-permute-done.2 = bf16[4,104,256]{2,1,0:T(8,128)(2,1)S(1)} collective-permute-done((bf16[4,104,256]{2,1,0:T(8,128)(2,1)S(1)}, bf16[4,104,256]{2,1,0:T(8,128)(2,1)S(1)}, u32[]{:S(2)}, u32[]{:S(2)}) %collective-permute-start.2) | collective-permute-done | bytes 213024 | tf_op jit(solution)/shard_map/ppermute | solution.py:363
  15.5 1.6 %collective-permute-start.3 = (bf16[104,256]{1,0:T(8,128)(2,1)S(1)}, bf16[104,256]{1,0:T(8,128)(2,1)S(1)}, u32[]{:S(2)}, u32[]{:S(2)}) collective-permute-start(bf16[104,256]{1,0:T(8,128)(2,1)S(1)} %get-tuple-element.81), channel_id=1, source_target_pairs={{0,8},{4,12},{8,0},{12,4},{16,24},{20,28},{24,16},{28,20},{1,9},{5... | collective-permute-start | bytes 159752 | tf_op jit(solution)/shard_map/ppermute | solution.py:363
  17.1 1.7 %collective-permute-start.5 = (bf16[104,256]{1,0:T(8,128)(2,1)S(1)}, bf16[104,256]{1,0:T(8,128)(2,1)S(1)}, u32[]{:S(2)}, u32[]{:S(2)}) collective-permute-start(bf16[104,256]{1,0:T(8,128)(2,1)S(1)} %get-tuple-element.82), channel_id=1, source_target_pairs={{0,24},{4,28},{8,16},{12,20},{16,8},{20,12},{24,0},{28,4},{1,25},{... | collective-permute-start | bytes 159752 | tf_op jit(solution)/shard_map/ppermute | solution.py:363
  18.8 0.3 collective-permute-start.4
  19.1 0.6 %collective-permute-done.3 = bf16[104,256]{1,0:T(8,128)(2,1)S(1)} collective-permute-done((bf16[104,256]{1,0:T(8,128)(2,1)S(1)}, bf16[104,256]{1,0:T(8,128)(2,1)S(1)}, u32[]{:S(2)}, u32[]{:S(2)}) %collective-permute-start.3) | collective-permute-done | bytes 53280 | tf_op jit(solution)/shard_map/ppermute | solution.py:363
  19.7 2.4 %collective-permute-done.5 = bf16[104,256]{1,0:T(8,128)(2,1)S(1)} collective-permute-done((bf16[104,256]{1,0:T(8,128)(2,1)S(1)}, bf16[104,256]{1,0:T(8,128)(2,1)S(1)}, u32[]{:S(2)}, u32[]{:S(2)}) %collective-permute-start.5) | collective-permute-done | bytes 53280 | tf_op jit(solution)/shard_map/ppermute | solution.py:363
  22.2 0.8 %collective-permute-done.4 = bf16[104,256]{1,0:T(8,128)(2,1)S(1)} collective-permute-done((bf16[104,256]{1,0:T(8,128)(2,1)S(1)}, bf16[104,256]{1,0:T(8,128)(2,1)S(1)}, u32[]{:S(2)}, u32[]{:S(2)}) %collective-permute-start.4) | collective-permute-done | bytes 53280 | tf_op jit(solution)/shard_map/ppermute | solution.py:363
  23.0 3.0 %collective-permute-start.8 = (bf16[104,256]{1,0:T(8,128)(2,1)S(1)}, bf16[104,256]{1,0:T(8,128)(2,1)S(1)}, u32[]{:S(2)}, u32[]{:S(2)}) collective-permute-start(bf16[104,256]{1,0:T(8,128)(2,1)S(1)} %fusion.3), channel_id=1, source_target_pairs={{0,3},{1,2},{2,1},{3,0},{4,7},{5,6},{6,5},{7,4},{8,11},{9,10},{10,... | collective-permute-start | bytes 159752 | tf_op jit(solution)/shard_map/ppermute | solution.py:363
  26.0 1.5 %collective-permute-start.6 = (bf16[104,256]{1,0:T(8,128)(2,1)S(1)}, bf16[104,256]{1,0:T(8,128)(2,1)S(1)}, u32[]{:S(2)}, u32[]{:S(2)}) collective-permute-start(bf16[104,256]{1,0:T(8,128)(2,1)S(1)} %fusion.3), channel_id=1, source_target_pairs={{0,1},{1,0},{2,3},{3,2},{4,5},{5,4},{6,7},{7,6},{8,9},{9,8},{10,11... | collective-permute-start | bytes 159752 | tf_op jit(solution)/shard_map/ppermute | solution.py:363
  27.5 1.5 %rim_back.1 = (bf16[256,256]{1,0:T(8,128)(2,1)S(1)}, bf16[256,256]{1,0:T(8,128)(2,1)S(1)}, f32[512,256]{1,0:T(8,128)S(1)}, bf16[1024,256]{1,0:T(8,128)(2,1)}, bf16[1024,256]{1,0:T(8,128)(2,1)}) custom-call(f32[1024,1]{1,0:T(8,128)S(1)} %get-tuple-element.41.valid_ref, bf16[512,256]{1,0:T(8,128)(2,1)S(1)} %get-tuple-element.42.up_ref, ...), custom_call_target="tpu_custom_call" | custom-call | flops 335544320 | bytes 4194304 | tf_op jit(solution)/shard_map/rim_back/pallas_call | solution.py:411
  28.9 2.4 %collective-permute-start.12 = (bf16[256,256]{1,0:T(8,128)(2,1)S(1)}, bf16[256,256]{1,0:T(8,128)(2,1)S(1)}, u32[]{:S(2)}, u32[]{:S(2)}) collective-permute-start(bf16[256,256]{1,0:T(8,128)(2,1)S(1)} %get-tuple-element.62), channel_id=1, source_target_pairs={{0,31},{1,2},{2,1},{3,4},{4,3},{5,6},{6,5},{7,8},{8,7},{9,10},{10,... | collective-permute-start | bytes 393224 | tf_op jit(solution)/shard_map/ppermute | solution.py:521
  31.7 1.3 %collective-permute-start.11 = (bf16[104,256]{1,0:T(8,128)(2,1)S(1)}, bf16[104,256]{1,0:T(8,128)(2,1)S(1)}, u32[]{:S(2)}, u32[]{:S(2)}) collective-permute-start(bf16[104,256]{1,0:T(8,128)(2,1)S(1)} %add_convert_fusion.refs_0_), channel_id=1, source_target_pairs={{0,24},{4,28},{8,16},{12,20},{16,8},{20,12},{24,0},{28,4},{1,25},{... | collective-permute-start | bytes 159752 | tf_op jit(solution)/shard_map/ppermute | solution.py:363
  33.0 0.9 %collective-permute-start.10 = (bf16[104,256]{1,0:T(8,128)(2,1)S(1)}, bf16[104,256]{1,0:T(8,128)(2,1)S(1)}, u32[]{:S(2)}, u32[]{:S(2)}) collective-permute-start(bf16[104,256]{1,0:T(8,128)(2,1)S(1)} %add_convert_fusion.refs_0_), channel_id=1, source_target_pairs={{0,16},{4,20},{8,24},{12,28},{16,0},{20,4},{24,8},{28,12},{1,17},{... | collective-permute-start | bytes 159752 | tf_op jit(solution)/shard_map/ppermute | solution.py:363
  33.9 1.4 %collective-permute-start.9 = (bf16[104,256]{1,0:T(8,128)(2,1)S(1)}, bf16[104,256]{1,0:T(8,128)(2,1)S(1)}, u32[]{:S(2)}, u32[]{:S(2)}) collective-permute-start(bf16[104,256]{1,0:T(8,128)(2,1)S(1)} %add_convert_fusion.refs_0_), channel_id=1, source_target_pairs={{0,8},{4,12},{8,0},{12,4},{16,24},{20,28},{24,16},{28,20},{1,9},{5... | collective-permute-start | bytes 159752 | tf_op jit(solution)/shard_map/ppermute | solution.py:363
  35.2 3.2 %collective-permute-done.12.odd_ref = bf16[256,256]{1,0:T(8,128)(2,1)S(1)} collective-permute-done((bf16[256,256]{1,0:T(8,128)(2,1)S(1)}, bf16[256,256]{1,0:T(8,128)(2,1)S(1)}, u32[]{:S(2)}, u32[]{:S(2)}) %collective-permute-start.12) | collective-permute-done | bytes 131104 | tf_op jit(solution)/shard_map/ppermute | solution.py:521
  38.4 0.7 %collective-permute-done.13.even_ref = bf16[256,256]{1,0:T(8,128)(2,1)S(1)} collective-permute-done((bf16[256,256]{1,0:T(8,128)(2,1)S(1)}, bf16[256,256]{1,0:T(8,128)(2,1)S(1)}, u32[]{:S(2)}, u32[]{:S(2)}) %collective-permute-start.13) | collective-permute-done | bytes 131104 | tf_op jit(solution)/shard_map/ppermute | solution.py:522
  39.5 0.8 %finish_state.1 = bf16[1024,256]{1,0:T(8,128)(2,1)} custom-call(bf16[1024,256]{1,0:T(8,128)(2,1)} %get-tuple-element.65.started_ref, f32[1024,1]{1,0:T(8,128)S(1)} %get-tuple-element.41.valid_ref, f32[512,256]{1,0:T(8,128)S(1)} %get-tuple-element.66.own_ref, bf16[256,256]{1,0:T(8,128)(2,1)S(1)} %collective-permute-done.12.odd_ref, ...), custom_call_target="tpu_custom_call", output_to_operand_aliasing={{}: (0, {})} | custom-call | tf_op jit(solution)/shard_map/finish_state/pallas_call | solution.py:411
  40.4 0.6 %collective-permute-done.14 = bf16[4,104,256]{2,1,0:T(8,128)(2,1)S(1)} collective-permute-done((bf16[4,104,256]{2,1,0:T(8,128)(2,1)S(1)}, bf16[4,104,256]{2,1,0:T(8,128)(2,1)S(1)}, u32[]{:S(2)}, u32[]{:S(2)}) %collective-permute-start.14) | collective-permute-done | bytes 213024 | tf_op jit(solution)/shard_map/ppermute | solution.py:363
  40.9 1.0 %unpack_sums.1 = (f32[512,256]{1,0:T(8,128)}, f32[256,256]{1,0:T(8,128)}, f32[1,256]{1,0:T(1,128)}) custom-call(bf16[104,256]{1,0:T(8,128)(2,1)S(1)} %add_convert_fusion.refs_0_, bf16[104,256]{1,0:T(8,128)(2,1)S(1)} %collective-permute-done.9.refs_1_, bf16[104,256]{1,0:T(8,128)(2,1)S(1)} %collective-permute-done.10.refs_2_, ...), custom_call_target="tpu_custom_call" | custom-call | tf_op jit(solution)/shard_map/unpack_sums/pallas_call | solution.py:411
  (19 shorter events, 1.1 us)
Async XLA Ops:
  1.7 10.7 %collective-permute-start = (bf16[256,256]{1,0:T(8,128)(2,1)S(1)}, bf16[256,256]{1,0:T(8,128)(2,1)S(1)}, u32[]{:S(2)}, u32[]{:S(2)}) collective-permute-start(bf16[256,256]{1,0:T(8,128)(2,1)S(1)} %get-tuple-element.53), channel_id=1, source_target_pairs={{0,1},{1,2},{2,3},{3,4},{4,5},{5,6},{6,7},{7,8},{8,9},{9,10},{10,1... | collective-permute-start | bytes 393224 | tf_op jit(solution)/shard_map/ppermute | solution.py:445
  4.8 7.8 %collective-permute-start.1 = (bf16[256,256]{1,0:T(8,128)(2,1)S(1)}, bf16[256,256]{1,0:T(8,128)(2,1)S(1)}, u32[]{:S(2)}, u32[]{:S(2)}) collective-permute-start(bf16[256,256]{1,0:T(8,128)(2,1)S(1)} %get-tuple-element.54), channel_id=1, source_target_pairs={{0,31},{1,0},{2,1},{3,2},{4,3},{5,4},{6,5},{7,6},{8,7},{9,8},{10,9... | collective-permute-start | bytes 393224 | tf_op jit(solution)/shard_map/ppermute | solution.py:446
  13.9 1.5 %collective-permute-start.2 = (bf16[4,104,256]{2,1,0:T(8,128)(2,1)S(1)}, bf16[4,104,256]{2,1,0:T(8,128)(2,1)S(1)}, u32[]{:S(2)}, u32[]{:S(2)}) collective-permute-start(bf16[4,104,256]{2,1,0:T(8,128)(2,1)S(1)} %slice_bitcast_fusion), channel_id=1, source_target_pairs={{0,4},{4,0},{8,12},{12,8},{16,20},{20,16},{24,28},{28,24},{1,5},{5... | collective-permute-start | bytes 638984 | tf_op jit(solution)/shard_map/ppermute | solution.py:363
  15.5 4.2 %collective-permute-start.3 = (bf16[104,256]{1,0:T(8,128)(2,1)S(1)}, bf16[104,256]{1,0:T(8,128)(2,1)S(1)}, u32[]{:S(2)}, u32[]{:S(2)}) collective-permute-start(bf16[104,256]{1,0:T(8,128)(2,1)S(1)} %get-tuple-element.81), channel_id=1, source_target_pairs={{0,8},{4,12},{8,0},{12,4},{16,24},{20,28},{24,16},{28,20},{1,9},{5... | collective-permute-start | bytes 159752 | tf_op jit(solution)/shard_map/ppermute | solution.py:363
  17.1 5.1 %collective-permute-start.5 = (bf16[104,256]{1,0:T(8,128)(2,1)S(1)}, bf16[104,256]{1,0:T(8,128)(2,1)S(1)}, u32[]{:S(2)}, u32[]{:S(2)}) collective-permute-start(bf16[104,256]{1,0:T(8,128)(2,1)S(1)} %get-tuple-element.82), channel_id=1, source_target_pairs={{0,24},{4,28},{8,16},{12,20},{16,8},{20,12},{24,0},{28,4},{1,25},{... | collective-permute-start | bytes 159752 | tf_op jit(solution)/shard_map/ppermute | solution.py:363
  18.8 4.2 %collective-permute-start.4 = (bf16[104,256]{1,0:T(8,128)(2,1)S(1)}, bf16[104,256]{1,0:T(8,128)(2,1)S(1)}, u32[]{:S(2)}, u32[]{:S(2)}) collective-permute-start(bf16[104,256]{1,0:T(8,128)(2,1)S(1)} %get-tuple-element.83), channel_id=1, source_target_pairs={{0,16},{4,20},{8,24},{12,28},{16,0},{20,4},{24,8},{28,12},{1,17},{... | collective-permute-start | bytes 159752 | tf_op jit(solution)/shard_map/ppermute | solution.py:363
  23.0 8.3 %collective-permute-start.8 = (bf16[104,256]{1,0:T(8,128)(2,1)S(1)}, bf16[104,256]{1,0:T(8,128)(2,1)S(1)}, u32[]{:S(2)}, u32[]{:S(2)}) collective-permute-start(bf16[104,256]{1,0:T(8,128)(2,1)S(1)} %fusion.3), channel_id=1, source_target_pairs={{0,3},{1,2},{2,1},{3,0},{4,7},{5,6},{6,5},{7,4},{8,11},{9,10},{10,... | collective-permute-start | bytes 159752 | tf_op jit(solution)/shard_map/ppermute | solution.py:363
  26.0 5.7 %collective-permute-start.7 = (bf16[104,256]{1,0:T(8,128)(2,1)S(1)}, bf16[104,256]{1,0:T(8,128)(2,1)S(1)}, u32[]{:S(2)}, u32[]{:S(2)}) collective-permute-start(bf16[104,256]{1,0:T(8,128)(2,1)S(1)} %fusion.3), channel_id=1, source_target_pairs={{0,2},{1,3},{2,0},{3,1},{4,6},{5,7},{6,4},{7,5},{8,10},{9,11},{10,... | collective-permute-start | bytes 159752 | tf_op jit(solution)/shard_map/ppermute | solution.py:363
  26.0 5.6 %collective-permute-start.6 = (bf16[104,256]{1,0:T(8,128)(2,1)S(1)}, bf16[104,256]{1,0:T(8,128)(2,1)S(1)}, u32[]{:S(2)}, u32[]{:S(2)}) collective-permute-start(bf16[104,256]{1,0:T(8,128)(2,1)S(1)} %fusion.3), channel_id=1, source_target_pairs={{0,1},{1,0},{2,3},{3,2},{4,5},{5,4},{6,7},{7,6},{8,9},{9,8},{10,11... | collective-permute-start | bytes 159752 | tf_op jit(solution)/shard_map/ppermute | solution.py:363
  28.9 9.5 %collective-permute-start.12 = (bf16[256,256]{1,0:T(8,128)(2,1)S(1)}, bf16[256,256]{1,0:T(8,128)(2,1)S(1)}, u32[]{:S(2)}, u32[]{:S(2)}) collective-permute-start(bf16[256,256]{1,0:T(8,128)(2,1)S(1)} %get-tuple-element.62), channel_id=1, source_target_pairs={{0,31},{1,2},{2,1},{3,4},{4,3},{5,6},{6,5},{7,8},{8,7},{9,10},{10,... | collective-permute-start | bytes 393224 | tf_op jit(solution)/shard_map/ppermute | solution.py:521
  31.3 7.8 %collective-permute-start.13 = (bf16[256,256]{1,0:T(8,128)(2,1)S(1)}, bf16[256,256]{1,0:T(8,128)(2,1)S(1)}, u32[]{:S(2)}, u32[]{:S(2)}) collective-permute-start(bf16[256,256]{1,0:T(8,128)(2,1)S(1)} %get-tuple-element.63), channel_id=1, source_target_pairs={{0,1},{1,0},{2,3},{3,2},{4,5},{5,4},{6,7},{7,6},{8,9},{9,8},{10,11... | collective-permute-start | bytes 393224 | tf_op jit(solution)/shard_map/ppermute | solution.py:522
  31.7 7.5 %collective-permute-start.11 = (bf16[104,256]{1,0:T(8,128)(2,1)S(1)}, bf16[104,256]{1,0:T(8,128)(2,1)S(1)}, u32[]{:S(2)}, u32[]{:S(2)}) collective-permute-start(bf16[104,256]{1,0:T(8,128)(2,1)S(1)} %add_convert_fusion.refs_0_), channel_id=1, source_target_pairs={{0,24},{4,28},{8,16},{12,20},{16,8},{20,12},{24,0},{28,4},{1,25},{... | collective-permute-start | bytes 159752 | tf_op jit(solution)/shard_map/ppermute | solution.py:363
  33.0 6.3 %collective-permute-start.10 = (bf16[104,256]{1,0:T(8,128)(2,1)S(1)}, bf16[104,256]{1,0:T(8,128)(2,1)S(1)}, u32[]{:S(2)}, u32[]{:S(2)}) collective-permute-start(bf16[104,256]{1,0:T(8,128)(2,1)S(1)} %add_convert_fusion.refs_0_), channel_id=1, source_target_pairs={{0,16},{4,20},{8,24},{12,28},{16,0},{20,4},{24,8},{28,12},{1,17},{... | collective-permute-start | bytes 159752 | tf_op jit(solution)/shard_map/ppermute | solution.py:363
  33.9 5.5 %collective-permute-start.9 = (bf16[104,256]{1,0:T(8,128)(2,1)S(1)}, bf16[104,256]{1,0:T(8,128)(2,1)S(1)}, u32[]{:S(2)}, u32[]{:S(2)}) collective-permute-start(bf16[104,256]{1,0:T(8,128)(2,1)S(1)} %add_convert_fusion.refs_0_), channel_id=1, source_target_pairs={{0,8},{4,12},{8,0},{12,4},{16,24},{20,28},{24,16},{28,20},{1,9},{5... | collective-permute-start | bytes 159752 | tf_op jit(solution)/shard_map/ppermute | solution.py:363
  39.4 1.5 %collective-permute-start.14 = (bf16[4,104,256]{2,1,0:T(8,128)(2,1)S(1)}, bf16[4,104,256]{2,1,0:T(8,128)(2,1)S(1)}, u32[]{:S(2)}, u32[]{:S(2)}) collective-permute-start(bf16[4,104,256]{2,1,0:T(8,128)(2,1)S(1)} %pad_maximum_fusion), channel_id=1, source_target_pairs={{0,4},{4,0},{8,12},{12,8},{16,20},{20,16},{24,28},{28,24},{1,5},{5... | collective-permute-start | bytes 638984 | tf_op jit(solution)/shard_map/ppermute | solution.py:363

commit v5 on v4

--- a/solution.py
+++ b/solution.py
@@ -317,25 +317,18 @@
     inside.wait()
 
 
-def finish_kernel(started_ref, valid_ref, own_ref, odd_ref, even_ref, out_ref, held_ref, sems):
+def finish_kernel(turned, started_ref, valid_ref, own_ref, back_ref, out_ref, held_ref, sem):
     rows = valid_ref.shape[0]
-    rim = odd_ref.shape[0]
+    rim = back_ref.shape[0]
     side, _ = place()
-    odd = odd_ref[...].astype(F32)
-    even = even_ref[...].astype(F32)
-    copies = []
-    for end in range(2):
-        first = end * (rows - rim)
-        there = slice(end * rim, (end + 1) * rim)
-        back = jnp.where(side == end, odd, even)
-        held_ref[there, :] = (own_ref[there, :] + back * valid_ref[first : first + rim, :]).astype(BF16)
-        copy = pltpu.make_async_copy(
-            held_ref.at[pl.ds(end * rim, rim), :], out_ref.at[pl.ds(first, rim), :], sems.at[end]
-        )
-        copy.start()
-        copies.append(copy)
-    for copy in copies:
-        copy.wait()
+    end = 1 - side if turned else side
+    at = pl.multiple_of(end * (rows - rim), rim)
+    there = pl.ds(pl.multiple_of(end * rim, rim), rim)
+    back = back_ref[...].astype(F32) * valid_ref[pl.ds(at, rim), :]
+    held_ref[...] = (own_ref[there, :] + back).astype(BF16)
+    copy = pltpu.make_async_copy(held_ref, out_ref.at[pl.ds(at, rim), :], sem)
+    copy.start()
+    copy.wait()
 
 
 def unpack_kernel(*refs):
@@ -501,9 +494,6 @@
     )
 
     valid, _, up_rim, w_in_near, _, _ = kept
-    other = swap(send[1], "dom", 1)
-    held = (send[0].astype(F32) + other.astype(F32)).astype(BF16)
-    held = [held[k] for k in range(dom // 2)]
     spill_odd, spill_even, own_rim, new_state, grad_state = kernel(
         back_kernel,
         "rim_back",
@@ -514,23 +504,37 @@
         flops=2 * inside * latent * (2 * latent + width),
         moved=4 * 1024 * 1024,
     )(valid, up_rim, w_in_near, band, pre_rim, new_inner, new_rim, own_inner, spread_inner)
+    back_odd = lax.ppermute(spill_odd, ring, odd_pairs)
+    back_even = lax.ppermute(spill_even, ring, even_pairs)
+    (grad_state,) = kernel(
+        functools.partial(finish_kernel, True),
+        "finish_even",
+        (1, 3),
+        (pltpu.HBM((rows, latent), BF16),),
+        [pltpu.VMEM((rim, latent), BF16), pltpu.SemaphoreType.DMA],
+        flops=0,
+        aliases={0: 0},
+    )(grad_state, valid, own_rim, back_even)
+    other = swap(send[1], "dom", 1)
+    held = (send[0].astype(F32) + other.astype(F32)).astype(BF16)
+    held = [held[k] for k in range(dom // 2)]
 
     parts = [held[0]] + [swap(held[k], "dom", 2 * k) for k in range(1, dom // 2)]
     quarter = sum(part.astype(F32) for part in parts).astype(BF16)
     planes = gathered(quarter, "rep")
-    back_odd = lax.ppermute(spill_odd, ring, odd_pairs)
-    back_even = lax.ppermute(spill_even, ring, even_pairs)
     mine = tree_sum(planes).astype(BF16)
+    mine, grad_state = lax.optimization_barrier((mine, grad_state))
     near = [mine] + [swap(mine, "dom", 2 * k) for k in range(1, dom // 2)]
-    near[-1], back_odd, back_even = lax.optimization_barrier((near[-1], back_odd, back_even))
+    near[-1], back_odd = lax.optimization_barrier((near[-1], back_odd))
     (grad_state,) = kernel(
-        finish_kernel,
-        "finish_state",
-        (1, 4),
+        functools.partial(finish_kernel, False),
+        "finish_odd",
+        (1, 3),
         (pltpu.HBM((rows, latent), BF16),),
-        [pltpu.VMEM((2 * rim, latent), BF16), pltpu.SemaphoreType.DMA((2,))],
+        [pltpu.VMEM((rim, latent), BF16), pltpu.SemaphoreType.DMA],
+        flops=0,
         aliases={0: 0},
-    )(grad_state, valid, own_rim, back_odd, back_even)
+    )(grad_state, valid, own_rim, back_odd)
     other = swap(jnp.stack(near), "dom", 1)
     other = [other[k] for k in range(dom // 2)]
     *other, grad_state = lax.optimization_barrier((*other, grad_state))

time: 42.1 us -> 40.9 us (0.971)
  waiting for transfers between devices: 10.5 us -> 7.08 us
  starting transfers between devices: 20.7 us -> 22.2 us
  Pallas kernels: 9.84 us -> 10.6 us
    ppermute x1, waiting for transfers between devices: 3.19 us -> 1.35 us  [local(): back_odd = lax.ppermute(spill_odd, ring, odd_pairs)]
    ppermute x1, starting transfers between devices: 0.01 us -> 1.63 us  [local(): back_even = lax.ppermute(spill_even, ring, even_pairs)]
    ppermute x11, waiting for transfers between devices: 6.38 us -> 5.56 us  [swap(): return lax.ppermute(x, axis, [(i, i ^ turn) for i in range(count)])]
    ppermute x1, waiting for transfers between devices: 0.74 us -> 0.01 us  [local(): back_even = lax.ppermute(spill_even, ring, even_pairs)]
    pallas_call x6 -> x7, Pallas kernels: 9.84 us -> 10.6 us  [run(): return call(*placed, *given[far:])]
  transfers between devices with their start and end apart: 15 -> 15, of which waited for: 10 -> 8; matrix products, arithmetic and copies ran while one was open for 0% -> 0% of each run, Pallas kernels for 15% -> 18%
where the time goes in v5:
time: 40.9 us; the launch traced here: 40.8 us
  starting transfers between devices  22.2 us (54%)
  Pallas kernels  10.6 us (26%)
  waiting for transfers between devices  7.08 us (17%)
  between operations  0.76 us (2%)
    ppermute x11, starting transfers between devices, swap(): return lax.ppermute(x, axis, [(i, i ^ turn) for i in range(count)])  11.7 us
    pallas_call x7, Pallas kernels, run(): return call(*placed, *given[far:])  10.6 us
    ppermute x11, waiting for transfers between devices, swap(): return lax.ppermute(x, axis, [(i, i ^ turn) for i in range(count)])  5.56 us
    ppermute x1, starting transfers between devices, local(): from_next = lax.ppermute(to_back, ring, back_pairs)  3.42 us
    ppermute x1, starting transfers between devices, local(): from_back = lax.ppermute(to_next, ring, next_pairs)  3.08 us
    ppermute x1, starting transfers between devices, local(): back_odd = lax.ppermute(spill_odd, ring, odd_pairs)  2.34 us
    ppermute x1, starting transfers between devices, local(): back_even = lax.ppermute(spill_even, ring, even_pairs)  1.63 us
    ppermute x1, waiting for transfers between devices, local(): back_odd = lax.ppermute(spill_odd, ring, odd_pairs)  1.35 us
  transfers between devices with their start and end apart: 15, of which 8 were waited for; matrix products, arithmetic and copies ran while one was open for 0% of the time, Pallas kernels for 18%

profile of v5, /device:TPU:0, one launch (start us, length us, event | category | flops | bytes accessed | tf_op | source)
XLA Modules:
  0.0 40.8 jit_solution(14992314447532153740)
XLA Ops:
  0.6 1.0 %pack_rims.1 = (bf16[256,256]{1,0:T(8,128)(2,1)S(1)}, bf16[256,256]{1,0:T(8,128)(2,1)S(1)}) custom-call(s32[8]{0:T(128)} %len_ref.1, bf16[1024,256]{1,0:T(8,128)(2,1)} %state_ref.1), custom_call_target="tpu_custom_call" | custom-call | tf_op jit(solution)/shard_map/pack_rims/pallas_call | solution.py:404
  1.7 3.1 %collective-permute-start = (bf16[256,256]{1,0:T(8,128)(2,1)S(1)}, bf16[256,256]{1,0:T(8,128)(2,1)S(1)}, u32[]{:S(2)}, u32[]{:S(2)}) collective-permute-start(bf16[256,256]{1,0:T(8,128)(2,1)S(1)} %get-tuple-element.54), channel_id=1, source_target_pairs={{0,1},{1,2},{2,3},{3,4},{4,5},{5,6},{6,7},{7,8},{8,9},{9,10},{10,1... | collective-permute-start | bytes 393224 | tf_op jit(solution)/shard_map/ppermute | solution.py:438
  4.8 3.4 %collective-permute-start.1 = (bf16[256,256]{1,0:T(8,128)(2,1)S(1)}, bf16[256,256]{1,0:T(8,128)(2,1)S(1)}, u32[]{:S(2)}, u32[]{:S(2)}) collective-permute-start(bf16[256,256]{1,0:T(8,128)(2,1)S(1)} %get-tuple-element.55), channel_id=1, source_target_pairs={{0,31},{1,0},{2,1},{3,2},{4,3},{5,4},{6,5},{7,6},{8,7},{9,8},{10,9... | collective-permute-start | bytes 393224 | tf_op jit(solution)/shard_map/ppermute | solution.py:439
  8.2 4.2 %inner_rows.1 = (bf16[512,256]{1,0:T(8,128)(2,1)S(1)}, f32[512,256]{1,0:T(8,128)S(1)}, f32[1024,256]{1,0:T(8,128)S(1)}, f32[512,256]{1,0:T(8,128)S(1)}, f32[256,...) custom-call(s32[8]{0:T(128)} %len_ref.1, ...), custom_call_target="tpu_custom_call" | custom-call | flops 1006632960 | bytes 10485760 | tf_op jit(solution)/shard_map/inner_rows/pallas_call | solution.py:404
  12.5 1.3 %rim_rows.1 = (bf16[2,4,104,256]{3,2,1,0:T(8,128)(2,1)S(1)}, bf16[512,256]{1,0:T(8,128)(2,1)S(1)}, bf16[512,256]{1,0:T(8,128)(2,1)S(1)}) custom-call(f32[1024,1]{1,0:T(8,128)S(1)} %get-tuple-element.42.valid_ref, bf16[512,256]{1,0:T(8,128)(2,1)S(1)} %get-tuple-element.46.state_ref, bf16[512,256]{1,0:T(8,128)(2,1)S(1)} %get-tuple-element.43.up_ref, ...), custom_call_target="tpu_custom_call" | custom-call | flops 1006632960 | bytes 8388608 | tf_op jit(solution)/shard_map/rim_rows/pallas_call | solution.py:404
  14.0 1.5 %collective-permute-done.2 = bf16[4,104,256]{2,1,0:T(8,128)(2,1)S(1)} collective-permute-done((bf16[4,104,256]{2,1,0:T(8,128)(2,1)S(1)}, bf16[4,104,256]{2,1,0:T(8,128)(2,1)S(1)}, u32[]{:S(2)}, u32[]{:S(2)}) %collective-permute-start.2) | collective-permute-done | bytes 213024 | tf_op jit(solution)/shard_map/ppermute | solution.py:356
  15.5 1.6 %collective-permute-start.3 = (bf16[104,256]{1,0:T(8,128)(2,1)S(1)}, bf16[104,256]{1,0:T(8,128)(2,1)S(1)}, u32[]{:S(2)}, u32[]{:S(2)}) collective-permute-start(bf16[104,256]{1,0:T(8,128)(2,1)S(1)} %get-tuple-element.83), channel_id=1, source_target_pairs={{0,8},{4,12},{8,0},{12,4},{16,24},{20,28},{24,16},{28,20},{1,9},{5... | collective-permute-start | bytes 159752 | tf_op jit(solution)/shard_map/ppermute | solution.py:356
  17.1 1.7 %collective-permute-start.5 = (bf16[104,256]{1,0:T(8,128)(2,1)S(1)}, bf16[104,256]{1,0:T(8,128)(2,1)S(1)}, u32[]{:S(2)}, u32[]{:S(2)}) collective-permute-start(bf16[104,256]{1,0:T(8,128)(2,1)S(1)} %get-tuple-element.84), channel_id=1, source_target_pairs={{0,24},{4,28},{8,16},{12,20},{16,8},{20,12},{24,0},{28,4},{1,25},{... | collective-permute-start | bytes 159752 | tf_op jit(solution)/shard_map/ppermute | solution.py:356
  19.1 1.5 %rim_back.1 = (bf16[256,256]{1,0:T(8,128)(2,1)S(1)}, bf16[256,256]{1,0:T(8,128)(2,1)S(1)}, f32[512,256]{1,0:T(8,128)S(1)}, bf16[1024,256]{1,0:T(8,128)(2,1)}, bf16[1024,256]{1,0:T(8,128)(2,1)}) custom-call(f32[1024,1]{1,0:T(8,128)S(1)} %get-tuple-element.42.valid_ref, bf16[512,256]{1,0:T(8,128)(2,1)S(1)} %get-tuple-element.43.up_ref, ...), custom_call_target="tpu_custom_call" | custom-call | flops 335544320 | bytes 4194304 | tf_op jit(solution)/shard_map/rim_back/pallas_call | solution.py:404
  20.6 1.6 %collective-permute-start.9 = (bf16[256,256]{1,0:T(8,128)(2,1)S(1)}, bf16[256,256]{1,0:T(8,128)(2,1)S(1)}, u32[]{:S(2)}, u32[]{:S(2)}) collective-permute-start(bf16[256,256]{1,0:T(8,128)(2,1)S(1)} %get-tuple-element.65), channel_id=1, source_target_pairs={{0,1},{1,0},{2,3},{3,2},{4,5},{5,4},{6,7},{7,6},{8,9},{9,8},{10,11... | collective-permute-start | bytes 393224 | tf_op jit(solution)/shard_map/ppermute | solution.py:508
  22.2 0.8 %collective-permute-done.4 = bf16[104,256]{1,0:T(8,128)(2,1)S(1)} collective-permute-done((bf16[104,256]{1,0:T(8,128)(2,1)S(1)}, bf16[104,256]{1,0:T(8,128)(2,1)S(1)}, u32[]{:S(2)}, u32[]{:S(2)}) %collective-permute-start.4) | collective-permute-done | bytes 53280 | tf_op jit(solution)/shard_map/ppermute | solution.py:356
  23.0 3.0 %collective-permute-start.8 = (bf16[104,256]{1,0:T(8,128)(2,1)S(1)}, bf16[104,256]{1,0:T(8,128)(2,1)S(1)}, u32[]{:S(2)}, u32[]{:S(2)}) collective-permute-start(bf16[104,256]{1,0:T(8,128)(2,1)S(1)} %fusion.3), channel_id=1, source_target_pairs={{0,3},{1,2},{2,1},{3,0},{4,7},{5,6},{6,5},{7,4},{8,11},{9,10},{10,... | collective-permute-start | bytes 159752 | tf_op jit(solution)/shard_map/ppermute | solution.py:356
  26.0 1.5 %collective-permute-start.6 = (bf16[104,256]{1,0:T(8,128)(2,1)S(1)}, bf16[104,256]{1,0:T(8,128)(2,1)S(1)}, u32[]{:S(2)}, u32[]{:S(2)}) collective-permute-start(bf16[104,256]{1,0:T(8,128)(2,1)S(1)} %fusion.3), channel_id=1, source_target_pairs={{0,1},{1,0},{2,3},{3,2},{4,5},{5,4},{6,7},{7,6},{8,9},{9,8},{10,11... | collective-permute-start | bytes 159752 | tf_op jit(solution)/shard_map/ppermute | solution.py:356
  27.5 2.3 %collective-permute-start.13 = (bf16[256,256]{1,0:T(8,128)(2,1)S(1)}, bf16[256,256]{1,0:T(8,128)(2,1)S(1)}, u32[]{:S(2)}, u32[]{:S(2)}) collective-permute-start(bf16[256,256]{1,0:T(8,128)(2,1)S(1)} %get-tuple-element.67), channel_id=1, source_target_pairs={{0,31},{1,2},{2,1},{3,4},{4,3},{5,6},{6,5},{7,8},{8,7},{9,10},{10,... | collective-permute-start | bytes 393224 | tf_op jit(solution)/shard_map/ppermute | solution.py:507
  29.8 0.8 %finish_even.1.started_ref = bf16[1024,256]{1,0:T(8,128)(2,1)} custom-call(bf16[1024,256]{1,0:T(8,128)(2,1)} %get-tuple-element.63.started_ref, f32[1024,1]{1,0:T(8,128)S(1)} %get-tuple-element.42.valid_ref, f32[512,256]{1,0:T(8,128)S(1)} %get-tuple-element.64.own_ref, ...), custom_call_target="tpu_custom_call", output_to_operand_aliasing={{}: (0, {})} | custom-call | tf_op jit(solution)/shard_map/finish_even/pallas_call | solution.py:404
  30.6 1.0 %collective-permute-done.7 = bf16[104,256]{1,0:T(8,128)(2,1)S(1)} collective-permute-done((bf16[104,256]{1,0:T(8,128)(2,1)S(1)}, bf16[104,256]{1,0:T(8,128)(2,1)S(1)}, u32[]{:S(2)}, u32[]{:S(2)}) %collective-permute-start.7) | collective-permute-done | bytes 53280 | tf_op jit(solution)/shard_map/ppermute | solution.py:356
  31.7 1.6 %collective-permute-start.12 = (bf16[104,256]{1,0:T(8,128)(2,1)S(1)}, bf16[104,256]{1,0:T(8,128)(2,1)S(1)}, u32[]{:S(2)}, u32[]{:S(2)}) collective-permute-start(bf16[104,256]{1,0:T(8,128)(2,1)S(1)} %add_convert_fusion.refs_0_), channel_id=1, source_target_pairs={{0,24},{4,28},{8,16},{12,20},{16,8},{20,12},{24,0},{28,4},{1,25},{... | collective-permute-start | bytes 159752 | tf_op jit(solution)/shard_map/ppermute | solution.py:356
  33.3 0.6 %collective-permute-start.11 = (bf16[104,256]{1,0:T(8,128)(2,1)S(1)}, bf16[104,256]{1,0:T(8,128)(2,1)S(1)}, u32[]{:S(2)}, u32[]{:S(2)}) collective-permute-start(bf16[104,256]{1,0:T(8,128)(2,1)S(1)} %add_convert_fusion.refs_0_), channel_id=1, source_target_pairs={{0,16},{4,20},{8,24},{12,28},{16,0},{20,4},{24,8},{28,12},{1,17},{... | collective-permute-start | bytes 159752 | tf_op jit(solution)/shard_map/ppermute | solution.py:356
  33.9 1.3 %collective-permute-start.10 = (bf16[104,256]{1,0:T(8,128)(2,1)S(1)}, bf16[104,256]{1,0:T(8,128)(2,1)S(1)}, u32[]{:S(2)}, u32[]{:S(2)}) collective-permute-start(bf16[104,256]{1,0:T(8,128)(2,1)S(1)} %add_convert_fusion.refs_0_), channel_id=1, source_target_pairs={{0,8},{4,12},{8,0},{12,4},{16,24},{20,28},{24,16},{28,20},{1,9},{5... | collective-permute-start | bytes 159752 | tf_op jit(solution)/shard_map/ppermute | solution.py:356
  35.2 1.4 %collective-permute-done.13.back_ref = bf16[256,256]{1,0:T(8,128)(2,1)S(1)} collective-permute-done((bf16[256,256]{1,0:T(8,128)(2,1)S(1)}, bf16[256,256]{1,0:T(8,128)(2,1)S(1)}, u32[]{:S(2)}, u32[]{:S(2)}) %collective-permute-start.13) | collective-permute-done | bytes 131104 | tf_op jit(solution)/shard_map/ppermute | solution.py:507
  36.6 1.1 %collective-permute-done.12.refs_3_ = bf16[104,256]{1,0:T(8,128)(2,1)S(1)} collective-permute-done((bf16[104,256]{1,0:T(8,128)(2,1)S(1)}, bf16[104,256]{1,0:T(8,128)(2,1)S(1)}, u32[]{:S(2)}, u32[]{:S(2)}) %collective-permute-start.12) | collective-permute-done | bytes 53280 | tf_op jit(solution)/shard_map/ppermute | solution.py:356
  38.3 0.8 %finish_odd.1 = bf16[1024,256]{1,0:T(8,128)(2,1)} custom-call(bf16[1024,256]{1,0:T(8,128)(2,1)} %finish_even.1.started_ref, f32[1024,1]{1,0:T(8,128)S(1)} %get-tuple-element.42.valid_ref, f32[512,256]{1,0:T(8,128)S(1)} %get-tuple-element.64.own_ref, bf16[256,256]{1,0:T(8,128)(2,1)S(1)} %collective-permute-done.13.back_ref), custom_call_target="tpu_custom_call", output_to_operand_aliasing={{}: (0, {})} | custom-call | tf_op jit(solution)/shard_map/finish_odd/pallas_call | solution.py:404
  39.1 0.7 %collective-permute-done.14 = bf16[4,104,256]{2,1,0:T(8,128)(2,1)S(1)} collective-permute-done((bf16[4,104,256]{2,1,0:T(8,128)(2,1)S(1)}, bf16[4,104,256]{2,1,0:T(8,128)(2,1)S(1)}, u32[]{:S(2)}, u32[]{:S(2)}) %collective-permute-start.14) | collective-permute-done | bytes 213024 | tf_op jit(solution)/shard_map/ppermute | solution.py:356
  39.8 1.0 %unpack_sums.1 = (f32[512,256]{1,0:T(8,128)}, f32[256,256]{1,0:T(8,128)}, f32[1,256]{1,0:T(1,128)}) custom-call(bf16[104,256]{1,0:T(8,128)(2,1)S(1)} %add_convert_fusion.refs_0_, bf16[104,256]{1,0:T(8,128)(2,1)S(1)} %collective-permute-done.10.refs_1_, bf16[104,256]{1,0:T(8,128)(2,1)S(1)} %collective-permute-done.11.refs_2_, ...), custom_call_target="tpu_custom_call" | custom-call | tf_op jit(solution)/shard_map/unpack_sums/pallas_call | solution.py:404
  (20 shorter events, 1.4 us)
Async XLA Ops:
  1.7 10.7 %collective-permute-start = (bf16[256,256]{1,0:T(8,128)(2,1)S(1)}, bf16[256,256]{1,0:T(8,128)(2,1)S(1)}, u32[]{:S(2)}, u32[]{:S(2)}) collective-permute-start(bf16[256,256]{1,0:T(8,128)(2,1)S(1)} %get-tuple-element.54), channel_id=1, source_target_pairs={{0,1},{1,2},{2,3},{3,4},{4,5},{5,6},{6,7},{7,8},{8,9},{9,10},{10,1... | collective-permute-start | bytes 393224 | tf_op jit(solution)/shard_map/ppermute | solution.py:438
  4.8 7.8 %collective-permute-start.1 = (bf16[256,256]{1,0:T(8,128)(2,1)S(1)}, bf16[256,256]{1,0:T(8,128)(2,1)S(1)}, u32[]{:S(2)}, u32[]{:S(2)}) collective-permute-start(bf16[256,256]{1,0:T(8,128)(2,1)S(1)} %get-tuple-element.55), channel_id=1, source_target_pairs={{0,31},{1,0},{2,1},{3,2},{4,3},{5,4},{6,5},{7,6},{8,7},{9,8},{10,9... | collective-permute-start | bytes 393224 | tf_op jit(solution)/shard_map/ppermute | solution.py:439
  13.9 1.5 %collective-permute-start.2 = (bf16[4,104,256]{2,1,0:T(8,128)(2,1)S(1)}, bf16[4,104,256]{2,1,0:T(8,128)(2,1)S(1)}, u32[]{:S(2)}, u32[]{:S(2)}) collective-permute-start(bf16[4,104,256]{2,1,0:T(8,128)(2,1)S(1)} %slice_bitcast_fusion), channel_id=1, source_target_pairs={{0,4},{4,0},{8,12},{12,8},{16,20},{20,16},{24,28},{28,24},{1,5},{5... | collective-permute-start | bytes 638984 | tf_op jit(solution)/shard_map/ppermute | solution.py:356
  15.5 6.7 %collective-permute-start.3 = (bf16[104,256]{1,0:T(8,128)(2,1)S(1)}, bf16[104,256]{1,0:T(8,128)(2,1)S(1)}, u32[]{:S(2)}, u32[]{:S(2)}) collective-permute-start(bf16[104,256]{1,0:T(8,128)(2,1)S(1)} %get-tuple-element.83), channel_id=1, source_target_pairs={{0,8},{4,12},{8,0},{12,4},{16,24},{20,28},{24,16},{28,20},{1,9},{5... | collective-permute-start | bytes 159752 | tf_op jit(solution)/shard_map/ppermute | solution.py:356
  17.1 5.1 %collective-permute-start.5 = (bf16[104,256]{1,0:T(8,128)(2,1)S(1)}, bf16[104,256]{1,0:T(8,128)(2,1)S(1)}, u32[]{:S(2)}, u32[]{:S(2)}) collective-permute-start(bf16[104,256]{1,0:T(8,128)(2,1)S(1)} %get-tuple-element.84), channel_id=1, source_target_pairs={{0,24},{4,28},{8,16},{12,20},{16,8},{20,12},{24,0},{28,4},{1,25},{... | collective-permute-start | bytes 159752 | tf_op jit(solution)/shard_map/ppermute | solution.py:356
  18.8 4.2 %collective-permute-start.4 = (bf16[104,256]{1,0:T(8,128)(2,1)S(1)}, bf16[104,256]{1,0:T(8,128)(2,1)S(1)}, u32[]{:S(2)}, u32[]{:S(2)}) collective-permute-start(bf16[104,256]{1,0:T(8,128)(2,1)S(1)} %get-tuple-element.85), channel_id=1, source_target_pairs={{0,16},{4,20},{8,24},{12,28},{16,0},{20,4},{24,8},{28,12},{1,17},{... | collective-permute-start | bytes 159752 | tf_op jit(solution)/shard_map/ppermute | solution.py:356
  20.6 9.2 %collective-permute-start.9 = (bf16[256,256]{1,0:T(8,128)(2,1)S(1)}, bf16[256,256]{1,0:T(8,128)(2,1)S(1)}, u32[]{:S(2)}, u32[]{:S(2)}) collective-permute-start(bf16[256,256]{1,0:T(8,128)(2,1)S(1)} %get-tuple-element.65), channel_id=1, source_target_pairs={{0,1},{1,0},{2,3},{3,2},{4,5},{5,4},{6,7},{7,6},{8,9},{9,8},{10,11... | collective-permute-start | bytes 393224 | tf_op jit(solution)/shard_map/ppermute | solution.py:508
  23.0 7.6 %collective-permute-start.8 = (bf16[104,256]{1,0:T(8,128)(2,1)S(1)}, bf16[104,256]{1,0:T(8,128)(2,1)S(1)}, u32[]{:S(2)}, u32[]{:S(2)}) collective-permute-start(bf16[104,256]{1,0:T(8,128)(2,1)S(1)} %fusion.3), channel_id=1, source_target_pairs={{0,3},{1,2},{2,1},{3,0},{4,7},{5,6},{6,5},{7,4},{8,11},{9,10},{10,... | collective-permute-start | bytes 159752 | tf_op jit(solution)/shard_map/ppermute | solution.py:356
  26.0 5.7 %collective-permute-start.7 = (bf16[104,256]{1,0:T(8,128)(2,1)S(1)}, bf16[104,256]{1,0:T(8,128)(2,1)S(1)}, u32[]{:S(2)}, u32[]{:S(2)}) collective-permute-start(bf16[104,256]{1,0:T(8,128)(2,1)S(1)} %fusion.3), channel_id=1, source_target_pairs={{0,2},{1,3},{2,0},{3,1},{4,6},{5,7},{6,4},{7,5},{8,10},{9,11},{10,... | collective-permute-start | bytes 159752 | tf_op jit(solution)/shard_map/ppermute | solution.py:356
  26.0 5.6 %collective-permute-start.6 = (bf16[104,256]{1,0:T(8,128)(2,1)S(1)}, bf16[104,256]{1,0:T(8,128)(2,1)S(1)}, u32[]{:S(2)}, u32[]{:S(2)}) collective-permute-start(bf16[104,256]{1,0:T(8,128)(2,1)S(1)} %fusion.3), channel_id=1, source_target_pairs={{0,1},{1,0},{2,3},{3,2},{4,5},{5,4},{6,7},{7,6},{8,9},{9,8},{10,11... | collective-permute-start | bytes 159752 | tf_op jit(solution)/shard_map/ppermute | solution.py:356
  27.5 9.1 %collective-permute-start.13 = (bf16[256,256]{1,0:T(8,128)(2,1)S(1)}, bf16[256,256]{1,0:T(8,128)(2,1)S(1)}, u32[]{:S(2)}, u32[]{:S(2)}) collective-permute-start(bf16[256,256]{1,0:T(8,128)(2,1)S(1)} %get-tuple-element.67), channel_id=1, source_target_pairs={{0,31},{1,2},{2,1},{3,4},{4,3},{5,6},{6,5},{7,8},{8,7},{9,10},{10,... | collective-permute-start | bytes 393224 | tf_op jit(solution)/shard_map/ppermute | solution.py:507
  31.7 6.0 %collective-permute-start.12 = (bf16[104,256]{1,0:T(8,128)(2,1)S(1)}, bf16[104,256]{1,0:T(8,128)(2,1)S(1)}, u32[]{:S(2)}, u32[]{:S(2)}) collective-permute-start(bf16[104,256]{1,0:T(8,128)(2,1)S(1)} %add_convert_fusion.refs_0_), channel_id=1, source_target_pairs={{0,24},{4,28},{8,16},{12,20},{16,8},{20,12},{24,0},{28,4},{1,25},{... | collective-permute-start | bytes 159752 | tf_op jit(solution)/shard_map/ppermute | solution.py:356
  33.3 4.9 %collective-permute-start.11 = (bf16[104,256]{1,0:T(8,128)(2,1)S(1)}, bf16[104,256]{1,0:T(8,128)(2,1)S(1)}, u32[]{:S(2)}, u32[]{:S(2)}) collective-permute-start(bf16[104,256]{1,0:T(8,128)(2,1)S(1)} %add_convert_fusion.refs_0_), channel_id=1, source_target_pairs={{0,16},{4,20},{8,24},{12,28},{16,0},{20,4},{24,8},{28,12},{1,17},{... | collective-permute-start | bytes 159752 | tf_op jit(solution)/shard_map/ppermute | solution.py:356
  33.9 4.3 %collective-permute-start.10 = (bf16[104,256]{1,0:T(8,128)(2,1)S(1)}, bf16[104,256]{1,0:T(8,128)(2,1)S(1)}, u32[]{:S(2)}, u32[]{:S(2)}) collective-permute-start(bf16[104,256]{1,0:T(8,128)(2,1)S(1)} %add_convert_fusion.refs_0_), channel_id=1, source_target_pairs={{0,8},{4,12},{8,0},{12,4},{16,24},{20,28},{24,16},{28,20},{1,9},{5... | collective-permute-start | bytes 159752 | tf_op jit(solution)/shard_map/ppermute | solution.py:356
  38.2 1.5 %collective-permute-start.14 = (bf16[4,104,256]{2,1,0:T(8,128)(2,1)S(1)}, bf16[4,104,256]{2,1,0:T(8,128)(2,1)S(1)}, u32[]{:S(2)}, u32[]{:S(2)}) collective-permute-start(bf16[4,104,256]{2,1,0:T(8,128)(2,1)S(1)} %pad_maximum_fusion), channel_id=1, source_target_pairs={{0,4},{4,0},{8,12},{12,8},{16,20},{20,16},{24,28},{28,24},{1,5},{5... | collective-permute-start | bytes 638984 | tf_op jit(solution)/shard_map/ppermute | solution.py:356

commit v6 on v5

--- a/solution.py
+++ b/solution.py
@@ -317,18 +317,29 @@
     inside.wait()
 
 
-def finish_kernel(turned, started_ref, valid_ref, own_ref, back_ref, out_ref, held_ref, sem):
+def even_kernel(valid_ref, own_ref, back_ref, sum_ref):
     rows = valid_ref.shape[0]
     rim = back_ref.shape[0]
     side, _ = place()
-    end = 1 - side if turned else side
-    at = pl.multiple_of(end * (rows - rim), rim)
-    there = pl.ds(pl.multiple_of(end * rim, rim), rim)
-    back = back_ref[...].astype(F32) * valid_ref[pl.ds(at, rim), :]
-    held_ref[...] = (own_ref[there, :] + back).astype(BF16)
-    copy = pltpu.make_async_copy(held_ref, out_ref.at[pl.ds(at, rim), :], sem)
-    copy.start()
-    copy.wait()
+    end = 1 - side
+    back = back_ref[...].astype(F32) * valid_ref[pl.ds(pl.multiple_of(end * (rows - rim), rim), rim), :]
+    sum_ref[...] = (own_ref[pl.ds(pl.multiple_of(end * rim, rim), rim), :] + back).astype(BF16)
+
+
+def finish_kernel(started_ref, valid_ref, own_ref, even_ref, back_ref, out_ref, held_ref, sems):
+    rows = valid_ref.shape[0]
+    rim = back_ref.shape[0]
+    side, _ = place()
+    at_even = pl.multiple_of((1 - side) * (rows - rim), rim)
+    at_odd = pl.multiple_of(side * (rows - rim), rim)
+    first = pltpu.make_async_copy(even_ref, out_ref.at[pl.ds(at_even, rim), :], sems.at[0])
+    first.start()
+    back = back_ref[...].astype(F32) * valid_ref[pl.ds(at_odd, rim), :]
+    held_ref[...] = (own_ref[pl.ds(pl.multiple_of(side * rim, rim), rim), :] + back).astype(BF16)
+    second = pltpu.make_async_copy(held_ref, out_ref.at[pl.ds(at_odd, rim), :], sems.at[1])
+    second.start()
+    first.wait()
+    second.wait()
 
 
 def unpack_kernel(*refs):
@@ -506,15 +517,12 @@
     )(valid, up_rim, w_in_near, band, pre_rim, new_inner, new_rim, own_inner, spread_inner)
     back_odd = lax.ppermute(spill_odd, ring, odd_pairs)
     back_even = lax.ppermute(spill_even, ring, even_pairs)
-    (grad_state,) = kernel(
-        functools.partial(finish_kernel, True),
-        "finish_even",
-        (1, 3),
-        (pltpu.HBM((rows, latent), BF16),),
-        [pltpu.VMEM((rim, latent), BF16), pltpu.SemaphoreType.DMA],
-        flops=0,
-        aliases={0: 0},
-    )(grad_state, valid, own_rim, back_even)
+    (even_rows,) = kernel(
+        even_kernel,
+        "even_rows",
+        (0, 3),
+        shapes(((rim, latent), BF16)),
+    )(valid, own_rim, back_even)
     other = swap(send[1], "dom", 1)
     held = (send[0].astype(F32) + other.astype(F32)).astype(BF16)
     held = [held[k] for k in range(dom // 2)]
@@ -523,18 +531,17 @@
     quarter = sum(part.astype(F32) for part in parts).astype(BF16)
     planes = gathered(quarter, "rep")
     mine = tree_sum(planes).astype(BF16)
-    mine, grad_state = lax.optimization_barrier((mine, grad_state))
+    mine, even_rows = lax.optimization_barrier((mine, even_rows))
     near = [mine] + [swap(mine, "dom", 2 * k) for k in range(1, dom // 2)]
     near[-1], back_odd = lax.optimization_barrier((near[-1], back_odd))
     (grad_state,) = kernel(
-        functools.partial(finish_kernel, False),
-        "finish_odd",
-        (1, 3),
+        finish_kernel,
+        "finish_state",
+        (1, 4),
         (pltpu.HBM((rows, latent), BF16),),
-        [pltpu.VMEM((rim, latent), BF16), pltpu.SemaphoreType.DMA],
-        flops=0,
+        [pltpu.VMEM((rim, latent), BF16), pltpu.SemaphoreType.DMA((2,))],
         aliases={0: 0},
-    )(grad_state, valid, own_rim, back_odd)
+    )(grad_state, valid, own_rim, even_rows, back_odd)
     other = swap(jnp.stack(near), "dom", 1)
     other = [other[k] for k in range(dom // 2)]
     *other, grad_state = lax.optimization_barrier((*other, grad_state))

time: 40.9 us -> 40.8 us (level)
  Pallas kernels: 10.6 us -> 9.91 us
  waiting for transfers between devices: 7.08 us -> 7.58 us
    pallas_call x7, Pallas kernels: 10.6 us -> 9.91 us  [run(): return call(*placed, *given[far:])]
    ppermute x11, waiting for transfers between devices: 5.56 us -> 6.1 us  [swap(): return lax.ppermute(x, axis, [(i, i ^ turn) for i in range(count)])]
  transfers between devices with their start and end apart: 15 -> 15, of which waited for: 8 -> 9; matrix products, arithmetic and copies ran while one was open for 0% -> 0% of each run, Pallas kernels for 18% -> 16%
where the time goes in v6:
time: 40.8 us; the launch traced here: 40.6 us
  starting transfers between devices  22.2 us (54%)
  Pallas kernels  9.91 us (24%)
  waiting for transfers between devices  7.58 us (19%)
  between operations  0.75 us (2%)
    ppermute x11, starting transfers between devices, swap(): return lax.ppermute(x, axis, [(i, i ^ turn) for i in range(count)])  11.7 us
    pallas_call x7, Pallas kernels, run(): return call(*placed, *given[far:])  9.91 us
    ppermute x11, waiting for transfers between devices, swap(): return lax.ppermute(x, axis, [(i, i ^ turn) for i in range(count)])  6.1 us
    ppermute x1, starting transfers between devices, local(): from_next = lax.ppermute(to_back, ring, back_pairs)  3.42 us
    ppermute x1, starting transfers between devices, local(): from_back = lax.ppermute(to_next, ring, next_pairs)  3.08 us
    ppermute x1, starting transfers between devices, local(): back_odd = lax.ppermute(spill_odd, ring, odd_pairs)  2.34 us
    ppermute x1, starting transfers between devices, local(): back_even = lax.ppermute(spill_even, ring, even_pairs)  1.62 us
    ppermute x1, waiting for transfers between devices, local(): back_odd = lax.ppermute(spill_odd, ring, odd_pairs)  1.31 us
  transfers between devices with their start and end apart: 15, of which 9 were waited for; matrix products, arithmetic and copies ran while one was open for 0% of the time, Pallas kernels for 16%

profile of v6, /device:TPU:0, one launch (start us, length us, event | category | flops | bytes accessed | tf_op | source)
XLA Modules:
  0.0 40.6 jit_solution(4540622067823450231)
XLA Ops:
  0.6 1.0 %pack_rims.1 = (bf16[256,256]{1,0:T(8,128)(2,1)S(1)}, bf16[256,256]{1,0:T(8,128)(2,1)S(1)}) custom-call(s32[8]{0:T(128)} %len_ref.1, bf16[1024,256]{1,0:T(8,128)(2,1)} %state_ref.1), custom_call_target="tpu_custom_call" | custom-call | tf_op jit(solution)/shard_map/pack_rims/pallas_call | solution.py:415
  1.7 3.1 %collective-permute-start = (bf16[256,256]{1,0:T(8,128)(2,1)S(1)}, bf16[256,256]{1,0:T(8,128)(2,1)S(1)}, u32[]{:S(2)}, u32[]{:S(2)}) collective-permute-start(bf16[256,256]{1,0:T(8,128)(2,1)S(1)} %get-tuple-element.54), channel_id=1, source_target_pairs={{0,1},{1,2},{2,3},{3,4},{4,5},{5,6},{6,7},{7,8},{8,9},{9,10},{10,1... | collective-permute-start | bytes 393224 | tf_op jit(solution)/shard_map/ppermute | solution.py:449
  4.8 3.4 %collective-permute-start.1 = (bf16[256,256]{1,0:T(8,128)(2,1)S(1)}, bf16[256,256]{1,0:T(8,128)(2,1)S(1)}, u32[]{:S(2)}, u32[]{:S(2)}) collective-permute-start(bf16[256,256]{1,0:T(8,128)(2,1)S(1)} %get-tuple-element.55), channel_id=1, source_target_pairs={{0,31},{1,0},{2,1},{3,2},{4,3},{5,4},{6,5},{7,6},{8,7},{9,8},{10,9... | collective-permute-start | bytes 393224 | tf_op jit(solution)/shard_map/ppermute | solution.py:450
  8.2 4.2 %inner_rows.1 = (bf16[512,256]{1,0:T(8,128)(2,1)S(1)}, f32[512,256]{1,0:T(8,128)S(1)}, f32[1024,256]{1,0:T(8,128)S(1)}, f32[512,256]{1,0:T(8,128)S(1)}, f32[256,...) custom-call(s32[8]{0:T(128)} %len_ref.1, ...), custom_call_target="tpu_custom_call" | custom-call | flops 1006632960 | bytes 10485760 | tf_op jit(solution)/shard_map/inner_rows/pallas_call | solution.py:415
  12.5 1.3 %rim_rows.1 = (bf16[2,4,104,256]{3,2,1,0:T(8,128)(2,1)S(1)}, bf16[512,256]{1,0:T(8,128)(2,1)S(1)}, bf16[512,256]{1,0:T(8,128)(2,1)S(1)}) custom-call(f32[1024,1]{1,0:T(8,128)S(1)} %get-tuple-element.42.valid_ref, bf16[512,256]{1,0:T(8,128)(2,1)S(1)} %get-tuple-element.46.state_ref, bf16[512,256]{1,0:T(8,128)(2,1)S(1)} %get-tuple-element.43.up_ref, ...), custom_call_target="tpu_custom_call" | custom-call | flops 1006632960 | bytes 8388608 | tf_op jit(solution)/shard_map/rim_rows/pallas_call | solution.py:415
  14.0 1.5 %collective-permute-done.2 = bf16[4,104,256]{2,1,0:T(8,128)(2,1)S(1)} collective-permute-done((bf16[4,104,256]{2,1,0:T(8,128)(2,1)S(1)}, bf16[4,104,256]{2,1,0:T(8,128)(2,1)S(1)}, u32[]{:S(2)}, u32[]{:S(2)}) %collective-permute-start.2) | collective-permute-done | bytes 213024 | tf_op jit(solution)/shard_map/ppermute | solution.py:367
  15.5 1.6 %collective-permute-start.3 = (bf16[104,256]{1,0:T(8,128)(2,1)S(1)}, bf16[104,256]{1,0:T(8,128)(2,1)S(1)}, u32[]{:S(2)}, u32[]{:S(2)}) collective-permute-start(bf16[104,256]{1,0:T(8,128)(2,1)S(1)} %get-tuple-element.83), channel_id=1, source_target_pairs={{0,8},{4,12},{8,0},{12,4},{16,24},{20,28},{24,16},{28,20},{1,9},{5... | collective-permute-start | bytes 159752 | tf_op jit(solution)/shard_map/ppermute | solution.py:367
  17.1 1.7 %collective-permute-start.5 = (bf16[104,256]{1,0:T(8,128)(2,1)S(1)}, bf16[104,256]{1,0:T(8,128)(2,1)S(1)}, u32[]{:S(2)}, u32[]{:S(2)}) collective-permute-start(bf16[104,256]{1,0:T(8,128)(2,1)S(1)} %get-tuple-element.84), channel_id=1, source_target_pairs={{0,24},{4,28},{8,16},{12,20},{16,8},{20,12},{24,0},{28,4},{1,25},{... | collective-permute-start | bytes 159752 | tf_op jit(solution)/shard_map/ppermute | solution.py:367
  19.1 1.5 %rim_back.1 = (bf16[256,256]{1,0:T(8,128)(2,1)S(1)}, bf16[256,256]{1,0:T(8,128)(2,1)S(1)}, f32[512,256]{1,0:T(8,128)S(1)}, bf16[1024,256]{1,0:T(8,128)(2,1)}, bf16[1024,256]{1,0:T(8,128)(2,1)}) custom-call(f32[1024,1]{1,0:T(8,128)S(1)} %get-tuple-element.42.valid_ref, bf16[512,256]{1,0:T(8,128)(2,1)S(1)} %get-tuple-element.43.up_ref, ...), custom_call_target="tpu_custom_call" | custom-call | flops 335544320 | bytes 4194304 | tf_op jit(solution)/shard_map/rim_back/pallas_call | solution.py:415
  20.6 1.6 %collective-permute-start.9 = (bf16[256,256]{1,0:T(8,128)(2,1)S(1)}, bf16[256,256]{1,0:T(8,128)(2,1)S(1)}, u32[]{:S(2)}, u32[]{:S(2)}) collective-permute-start(bf16[256,256]{1,0:T(8,128)(2,1)S(1)} %get-tuple-element.64), channel_id=1, source_target_pairs={{0,1},{1,0},{2,3},{3,2},{4,5},{5,4},{6,7},{7,6},{8,9},{9,8},{10,11... | collective-permute-start | bytes 393224 | tf_op jit(solution)/shard_map/ppermute | solution.py:519
  22.2 0.8 %collective-permute-done.4 = bf16[104,256]{1,0:T(8,128)(2,1)S(1)} collective-permute-done((bf16[104,256]{1,0:T(8,128)(2,1)S(1)}, bf16[104,256]{1,0:T(8,128)(2,1)S(1)}, u32[]{:S(2)}, u32[]{:S(2)}) %collective-permute-start.4) | collective-permute-done | bytes 53280 | tf_op jit(solution)/shard_map/ppermute | solution.py:367
  23.0 3.0 %collective-permute-start.8 = (bf16[104,256]{1,0:T(8,128)(2,1)S(1)}, bf16[104,256]{1,0:T(8,128)(2,1)S(1)}, u32[]{:S(2)}, u32[]{:S(2)}) collective-permute-start(bf16[104,256]{1,0:T(8,128)(2,1)S(1)} %fusion.3), channel_id=1, source_target_pairs={{0,3},{1,2},{2,1},{3,0},{4,7},{5,6},{6,5},{7,4},{8,11},{9,10},{10,... | collective-permute-start | bytes 159752 | tf_op jit(solution)/shard_map/ppermute | solution.py:367
  26.0 1.5 %collective-permute-start.6 = (bf16[104,256]{1,0:T(8,128)(2,1)S(1)}, bf16[104,256]{1,0:T(8,128)(2,1)S(1)}, u32[]{:S(2)}, u32[]{:S(2)}) collective-permute-start(bf16[104,256]{1,0:T(8,128)(2,1)S(1)} %fusion.3), channel_id=1, source_target_pairs={{0,1},{1,0},{2,3},{3,2},{4,5},{5,4},{6,7},{7,6},{8,9},{9,8},{10,11... | collective-permute-start | bytes 159752 | tf_op jit(solution)/shard_map/ppermute | solution.py:367
  27.5 2.3 %collective-permute-start.13 = (bf16[256,256]{1,0:T(8,128)(2,1)S(1)}, bf16[256,256]{1,0:T(8,128)(2,1)S(1)}, u32[]{:S(2)}, u32[]{:S(2)}) collective-permute-start(bf16[256,256]{1,0:T(8,128)(2,1)S(1)} %get-tuple-element.66), channel_id=1, source_target_pairs={{0,31},{1,2},{2,1},{3,4},{4,3},{5,6},{6,5},{7,8},{8,7},{9,10},{10,... | collective-permute-start | bytes 393224 | tf_op jit(solution)/shard_map/ppermute | solution.py:518
  29.9 1.7 %collective-permute-done.7 = bf16[104,256]{1,0:T(8,128)(2,1)S(1)} collective-permute-done((bf16[104,256]{1,0:T(8,128)(2,1)S(1)}, bf16[104,256]{1,0:T(8,128)(2,1)S(1)}, u32[]{:S(2)}, u32[]{:S(2)}) %collective-permute-start.7) | collective-permute-done | bytes 53280 | tf_op jit(solution)/shard_map/ppermute | solution.py:367
  31.7 1.6 %collective-permute-start.12 = (bf16[104,256]{1,0:T(8,128)(2,1)S(1)}, bf16[104,256]{1,0:T(8,128)(2,1)S(1)}, u32[]{:S(2)}, u32[]{:S(2)}) collective-permute-start(bf16[104,256]{1,0:T(8,128)(2,1)S(1)} %add_convert_fusion.refs_0_), channel_id=1, source_target_pairs={{0,24},{4,28},{8,16},{12,20},{16,8},{20,12},{24,0},{28,4},{1,25},{... | collective-permute-start | bytes 159752 | tf_op jit(solution)/shard_map/ppermute | solution.py:367
  33.3 0.6 %collective-permute-start.11 = (bf16[104,256]{1,0:T(8,128)(2,1)S(1)}, bf16[104,256]{1,0:T(8,128)(2,1)S(1)}, u32[]{:S(2)}, u32[]{:S(2)}) collective-permute-start(bf16[104,256]{1,0:T(8,128)(2,1)S(1)} %add_convert_fusion.refs_0_), channel_id=1, source_target_pairs={{0,16},{4,20},{8,24},{12,28},{16,0},{20,4},{24,8},{28,12},{1,17},{... | collective-permute-start | bytes 159752 | tf_op jit(solution)/shard_map/ppermute | solution.py:367
  33.9 1.3 %collective-permute-start.10 = (bf16[104,256]{1,0:T(8,128)(2,1)S(1)}, bf16[104,256]{1,0:T(8,128)(2,1)S(1)}, u32[]{:S(2)}, u32[]{:S(2)}) collective-permute-start(bf16[104,256]{1,0:T(8,128)(2,1)S(1)} %add_convert_fusion.refs_0_), channel_id=1, source_target_pairs={{0,8},{4,12},{8,0},{12,4},{16,24},{20,28},{24,16},{28,20},{1,9},{5... | collective-permute-start | bytes 159752 | tf_op jit(solution)/shard_map/ppermute | solution.py:367
  35.2 1.3 %collective-permute-done.13.back_ref = bf16[256,256]{1,0:T(8,128)(2,1)S(1)} collective-permute-done((bf16[256,256]{1,0:T(8,128)(2,1)S(1)}, bf16[256,256]{1,0:T(8,128)(2,1)S(1)}, u32[]{:S(2)}, u32[]{:S(2)}) %collective-permute-start.13) | collective-permute-done | bytes 131104 | tf_op jit(solution)/shard_map/ppermute | solution.py:518
  36.5 1.0 %collective-permute-done.12.refs_3_ = bf16[104,256]{1,0:T(8,128)(2,1)S(1)} collective-permute-done((bf16[104,256]{1,0:T(8,128)(2,1)S(1)}, bf16[104,256]{1,0:T(8,128)(2,1)S(1)}, u32[]{:S(2)}, u32[]{:S(2)}) %collective-permute-start.12) | collective-permute-done | bytes 53280 | tf_op jit(solution)/shard_map/ppermute | solution.py:367
  37.5 0.3 collective-permute-done.11.refs_2_
  38.2 0.8 %finish_state.1 = bf16[1024,256]{1,0:T(8,128)(2,1)} custom-call(bf16[1024,256]{1,0:T(8,128)(2,1)} %get-tuple-element.68.started_ref, f32[1024,1]{1,0:T(8,128)S(1)} %get-tuple-element.42.valid_ref, f32[512,256]{1,0:T(8,128)S(1)} %get-tuple-element.63.own_ref, bf16[256,256]{1,0:T(8,128)(2,1)S(1)} %even_rows.1.even_ref, ...), custom_call_target="tpu_custom_call", output_to_operand_aliasing={{}: (0, {})} | custom-call | tf_op jit(solution)/shard_map/finish_state/pallas_call | solution.py:415
  39.0 0.6 %collective-permute-done.14 = bf16[4,104,256]{2,1,0:T(8,128)(2,1)S(1)} collective-permute-done((bf16[4,104,256]{2,1,0:T(8,128)(2,1)S(1)}, bf16[4,104,256]{2,1,0:T(8,128)(2,1)S(1)}, u32[]{:S(2)}, u32[]{:S(2)}) %collective-permute-start.14) | collective-permute-done | bytes 213024 | tf_op jit(solution)/shard_map/ppermute | solution.py:367
  39.6 1.0 %unpack_sums.1 = (f32[512,256]{1,0:T(8,128)}, f32[256,256]{1,0:T(8,128)}, f32[1,256]{1,0:T(1,128)}) custom-call(bf16[104,256]{1,0:T(8,128)(2,1)S(1)} %add_convert_fusion.refs_0_, bf16[104,256]{1,0:T(8,128)(2,1)S(1)} %collective-permute-done.10.refs_1_, bf16[104,256]{1,0:T(8,128)(2,1)S(1)} %collective-permute-done.11.refs_2_, ...), custom_call_target="tpu_custom_call" | custom-call | tf_op jit(solution)/shard_map/unpack_sums/pallas_call | solution.py:415
  (20 shorter events, 1.1 us)
Async XLA Ops:
  1.7 10.7 %collective-permute-start = (bf16[256,256]{1,0:T(8,128)(2,1)S(1)}, bf16[256,256]{1,0:T(8,128)(2,1)S(1)}, u32[]{:S(2)}, u32[]{:S(2)}) collective-permute-start(bf16[256,256]{1,0:T(8,128)(2,1)S(1)} %get-tuple-element.54), channel_id=1, source_target_pairs={{0,1},{1,2},{2,3},{3,4},{4,5},{5,6},{6,7},{7,8},{8,9},{9,10},{10,1... | collective-permute-start | bytes 393224 | tf_op jit(solution)/shard_map/ppermute | solution.py:449
  4.8 7.8 %collective-permute-start.1 = (bf16[256,256]{1,0:T(8,128)(2,1)S(1)}, bf16[256,256]{1,0:T(8,128)(2,1)S(1)}, u32[]{:S(2)}, u32[]{:S(2)}) collective-permute-start(bf16[256,256]{1,0:T(8,128)(2,1)S(1)} %get-tuple-element.55), channel_id=1, source_target_pairs={{0,31},{1,0},{2,1},{3,2},{4,3},{5,4},{6,5},{7,6},{8,7},{9,8},{10,9... | collective-permute-start | bytes 393224 | tf_op jit(solution)/shard_map/ppermute | solution.py:450
  13.9 1.5 %collective-permute-start.2 = (bf16[4,104,256]{2,1,0:T(8,128)(2,1)S(1)}, bf16[4,104,256]{2,1,0:T(8,128)(2,1)S(1)}, u32[]{:S(2)}, u32[]{:S(2)}) collective-permute-start(bf16[4,104,256]{2,1,0:T(8,128)(2,1)S(1)} %slice_bitcast_fusion), channel_id=1, source_target_pairs={{0,4},{4,0},{8,12},{12,8},{16,20},{20,16},{24,28},{28,24},{1,5},{5... | collective-permute-start | bytes 638984 | tf_op jit(solution)/shard_map/ppermute | solution.py:367
  15.5 6.7 %collective-permute-start.3 = (bf16[104,256]{1,0:T(8,128)(2,1)S(1)}, bf16[104,256]{1,0:T(8,128)(2,1)S(1)}, u32[]{:S(2)}, u32[]{:S(2)}) collective-permute-start(bf16[104,256]{1,0:T(8,128)(2,1)S(1)} %get-tuple-element.83), channel_id=1, source_target_pairs={{0,8},{4,12},{8,0},{12,4},{16,24},{20,28},{24,16},{28,20},{1,9},{5... | collective-permute-start | bytes 159752 | tf_op jit(solution)/shard_map/ppermute | solution.py:367
  17.1 5.1 %collective-permute-start.5 = (bf16[104,256]{1,0:T(8,128)(2,1)S(1)}, bf16[104,256]{1,0:T(8,128)(2,1)S(1)}, u32[]{:S(2)}, u32[]{:S(2)}) collective-permute-start(bf16[104,256]{1,0:T(8,128)(2,1)S(1)} %get-tuple-element.84), channel_id=1, source_target_pairs={{0,24},{4,28},{8,16},{12,20},{16,8},{20,12},{24,0},{28,4},{1,25},{... | collective-permute-start | bytes 159752 | tf_op jit(solution)/shard_map/ppermute | solution.py:367
  18.8 4.2 %collective-permute-start.4 = (bf16[104,256]{1,0:T(8,128)(2,1)S(1)}, bf16[104,256]{1,0:T(8,128)(2,1)S(1)}, u32[]{:S(2)}, u32[]{:S(2)}) collective-permute-start(bf16[104,256]{1,0:T(8,128)(2,1)S(1)} %get-tuple-element.85), channel_id=1, source_target_pairs={{0,16},{4,20},{8,24},{12,28},{16,0},{20,4},{24,8},{28,12},{1,17},{... | collective-permute-start | bytes 159752 | tf_op jit(solution)/shard_map/ppermute | solution.py:367
  20.6 9.2 %collective-permute-start.9 = (bf16[256,256]{1,0:T(8,128)(2,1)S(1)}, bf16[256,256]{1,0:T(8,128)(2,1)S(1)}, u32[]{:S(2)}, u32[]{:S(2)}) collective-permute-start(bf16[256,256]{1,0:T(8,128)(2,1)S(1)} %get-tuple-element.64), channel_id=1, source_target_pairs={{0,1},{1,0},{2,3},{3,2},{4,5},{5,4},{6,7},{7,6},{8,9},{9,8},{10,11... | collective-permute-start | bytes 393224 | tf_op jit(solution)/shard_map/ppermute | solution.py:519
  23.0 6.9 %collective-permute-start.8 = (bf16[104,256]{1,0:T(8,128)(2,1)S(1)}, bf16[104,256]{1,0:T(8,128)(2,1)S(1)}, u32[]{:S(2)}, u32[]{:S(2)}) collective-permute-start(bf16[104,256]{1,0:T(8,128)(2,1)S(1)} %fusion.3), channel_id=1, source_target_pairs={{0,3},{1,2},{2,1},{3,0},{4,7},{5,6},{6,5},{7,4},{8,11},{9,10},{10,... | collective-permute-start | bytes 159752 | tf_op jit(solution)/shard_map/ppermute | solution.py:367
  26.0 5.7 %collective-permute-start.7 = (bf16[104,256]{1,0:T(8,128)(2,1)S(1)}, bf16[104,256]{1,0:T(8,128)(2,1)S(1)}, u32[]{:S(2)}, u32[]{:S(2)}) collective-permute-start(bf16[104,256]{1,0:T(8,128)(2,1)S(1)} %fusion.3), channel_id=1, source_target_pairs={{0,2},{1,3},{2,0},{3,1},{4,6},{5,7},{6,4},{7,5},{8,10},{9,11},{10,... | collective-permute-start | bytes 159752 | tf_op jit(solution)/shard_map/ppermute | solution.py:367
  26.0 5.6 %collective-permute-start.6 = (bf16[104,256]{1,0:T(8,128)(2,1)S(1)}, bf16[104,256]{1,0:T(8,128)(2,1)S(1)}, u32[]{:S(2)}, u32[]{:S(2)}) collective-permute-start(bf16[104,256]{1,0:T(8,128)(2,1)S(1)} %fusion.3), channel_id=1, source_target_pairs={{0,1},{1,0},{2,3},{3,2},{4,5},{5,4},{6,7},{7,6},{8,9},{9,8},{10,11... | collective-permute-start | bytes 159752 | tf_op jit(solution)/shard_map/ppermute | solution.py:367
  27.5 9.1 %collective-permute-start.13 = (bf16[256,256]{1,0:T(8,128)(2,1)S(1)}, bf16[256,256]{1,0:T(8,128)(2,1)S(1)}, u32[]{:S(2)}, u32[]{:S(2)}) collective-permute-start(bf16[256,256]{1,0:T(8,128)(2,1)S(1)} %get-tuple-element.66), channel_id=1, source_target_pairs={{0,31},{1,2},{2,1},{3,4},{4,3},{5,6},{6,5},{7,8},{8,7},{9,10},{10,... | collective-permute-start | bytes 393224 | tf_op jit(solution)/shard_map/ppermute | solution.py:518
  31.7 5.9 %collective-permute-start.12 = (bf16[104,256]{1,0:T(8,128)(2,1)S(1)}, bf16[104,256]{1,0:T(8,128)(2,1)S(1)}, u32[]{:S(2)}, u32[]{:S(2)}) collective-permute-start(bf16[104,256]{1,0:T(8,128)(2,1)S(1)} %add_convert_fusion.refs_0_), channel_id=1, source_target_pairs={{0,24},{4,28},{8,16},{12,20},{16,8},{20,12},{24,0},{28,4},{1,25},{... | collective-permute-start | bytes 159752 | tf_op jit(solution)/shard_map/ppermute | solution.py:367
  33.3 4.6 %collective-permute-start.11 = (bf16[104,256]{1,0:T(8,128)(2,1)S(1)}, bf16[104,256]{1,0:T(8,128)(2,1)S(1)}, u32[]{:S(2)}, u32[]{:S(2)}) collective-permute-start(bf16[104,256]{1,0:T(8,128)(2,1)S(1)} %add_convert_fusion.refs_0_), channel_id=1, source_target_pairs={{0,16},{4,20},{8,24},{12,28},{16,0},{20,4},{24,8},{28,12},{1,17},{... | collective-permute-start | bytes 159752 | tf_op jit(solution)/shard_map/ppermute | solution.py:367
  33.9 4.1 %collective-permute-start.10 = (bf16[104,256]{1,0:T(8,128)(2,1)S(1)}, bf16[104,256]{1,0:T(8,128)(2,1)S(1)}, u32[]{:S(2)}, u32[]{:S(2)}) collective-permute-start(bf16[104,256]{1,0:T(8,128)(2,1)S(1)} %add_convert_fusion.refs_0_), channel_id=1, source_target_pairs={{0,8},{4,12},{8,0},{12,4},{16,24},{20,28},{24,16},{28,20},{1,9},{5... | collective-permute-start | bytes 159752 | tf_op jit(solution)/shard_map/ppermute | solution.py:367
  38.1 1.5 %collective-permute-start.14 = (bf16[4,104,256]{2,1,0:T(8,128)(2,1)S(1)}, bf16[4,104,256]{2,1,0:T(8,128)(2,1)S(1)}, u32[]{:S(2)}, u32[]{:S(2)}) collective-permute-start(bf16[4,104,256]{2,1,0:T(8,128)(2,1)S(1)} %pad_maximum_fusion), channel_id=1, source_target_pairs={{0,4},{4,0},{8,12},{12,8},{16,20},{20,16},{24,28},{28,24},{1,5},{5... | collective-permute-start | bytes 638984 | tf_op jit(solution)/shard_map/ppermute | solution.py:367

commit v7 on v6

--- a/solution.py
+++ b/solution.py
@@ -326,10 +326,31 @@
     sum_ref[...] = (own_ref[pl.ds(pl.multiple_of(end * rim, rim), rim), :] + back).astype(BF16)
 
 
-def finish_kernel(started_ref, valid_ref, own_ref, even_ref, back_ref, out_ref, held_ref, sems):
+def write_pieces(pieces, turns, me, count, grad_in_ref, grad_out_ref, in_ref, out_ref, sems):
+    n_in = grad_in_ref.shape[0] // count
+    n_out = grad_out_ref.shape[0] // count
+    copies = []
+    gain = jnp.zeros((1, grad_in_ref.shape[1]), F32)
+    for n, (source, turn) in enumerate(zip(pieces, turns)):
+        piece = lax.bitwise_xor(me, turn)
+        at_in = pl.ds(pl.multiple_of(piece * n_in, n_in), n_in)
+        at_out = pl.ds(pl.multiple_of(piece * n_out, n_out), n_out)
+        in_ref[n] = source[:n_in, :].astype(F32)
+        copies.append(pltpu.make_async_copy(in_ref.at[n], grad_in_ref.at[at_in, :], sems.at[2 * n]))
+        copies[-1].start()
+        out_ref[n] = source[n_in : n_in + n_out, :].astype(F32)
+        copies.append(pltpu.make_async_copy(out_ref.at[n], grad_out_ref.at[at_out, :], sems.at[2 * n + 1]))
+        copies[-1].start()
+        gain = gain + source[n_in + n_out :, :].astype(F32)[:1, :]
+    return gain, copies
+
+
+def finish_kernel(started_ref, valid_ref, own_ref, even_ref, back_ref, *refs):
+    near = refs[:-9]
+    out_ref, grad_in_ref, grad_out_ref, gain_ref, held_ref, in_ref, piece_out_ref, sems, piece_sems = refs[-9:]
     rows = valid_ref.shape[0]
     rim = back_ref.shape[0]
-    side, _ = place()
+    side, me = place()
     at_even = pl.multiple_of((1 - side) * (rows - rim), rim)
     at_odd = pl.multiple_of(side * (rows - rim), rim)
     first = pltpu.make_async_copy(even_ref, out_ref.at[pl.ds(at_even, rim), :], sems.at[0])
@@ -338,28 +359,29 @@
     held_ref[...] = (own_ref[pl.ds(pl.multiple_of(side * rim, rim), rim), :] + back).astype(BF16)
     second = pltpu.make_async_copy(held_ref, out_ref.at[pl.ds(at_odd, rim), :], sems.at[1])
     second.start()
+    turns = range(0, 2 * len(near), 2)
+    gain_ref[...], copies = write_pieces(
+        near, turns, me, 2 * len(near), grad_in_ref, grad_out_ref, in_ref, piece_out_ref, piece_sems
+    )
     first.wait()
     second.wait()
-
-
-def unpack_kernel(*refs):
-    pieces = refs[:-3]
-    grad_in_ref, grad_out_ref, gain_ref = refs[-3:]
+    for copy in copies:
+        copy.wait()
+
+
+def unpack_kernel(begun_in_ref, begun_out_ref, gain_near_ref, *refs):
+    grad_in_ref, grad_out_ref, gain_ref, in_ref, piece_out_ref, total_ref, sems, gain_sem = refs[-8:]
+    far = refs[:-8]
     _, me = place()
-    count = len(pieces)
-    n_in = grad_in_ref.shape[0] // count
-    n_out = grad_out_ref.shape[0] // count
-    for turn in range(count):
-        source = pieces[turn // 2 + turn % 2 * (count // 2)]
-        piece = lax.bitwise_xor(me, turn)
-        at_in = pl.ds(pl.multiple_of(piece * n_in, n_in), n_in)
-        at_out = pl.ds(pl.multiple_of(piece * n_out, n_out), n_out)
-        grad_in_ref[at_in, :] = source[:n_in, :].astype(F32)
-        grad_out_ref[at_out, :] = source[n_in : n_in + n_out, :].astype(F32)
-
-        @pl.when(piece == 0)
-        def _():
-            gain_ref[...] = source[n_in + n_out :, :].astype(F32)[:1, :]
+    turns = range(1, 2 * len(far), 2)
+    gain, copies = write_pieces(
+        far, turns, me, 2 * len(far), grad_in_ref, grad_out_ref, in_ref, piece_out_ref, sems
+    )
+    total_ref[...] = gain_near_ref[...] + gain
+    copies.append(pltpu.make_async_copy(total_ref, gain_ref, gain_sem))
+    copies[-1].start()
+    for copy in copies:
+        copy.wait()
 
 
 def swap(x, axis, turn):
@@ -534,23 +556,32 @@
     mine, even_rows = lax.optimization_barrier((mine, even_rows))
     near = [mine] + [swap(mine, "dom", 2 * k) for k in range(1, dom // 2)]
     near[-1], back_odd = lax.optimization_barrier((near[-1], back_odd))
-    (grad_state,) = kernel(
+    other = swap(jnp.stack(near), "dom", 1)
+    pieces = dom // 2
+    piece_scratch = [
+        pltpu.VMEM((pieces, n_in, latent), F32),
+        pltpu.VMEM((pieces, n_out, latent), F32),
+    ]
+    sums = (pltpu.HBM(w_in.shape, F32), pltpu.HBM(w_out.shape, F32)) + shapes(((1, latent), F32))
+    grad_state, grad_w_in, grad_w_out, gain_near = kernel(
         finish_kernel,
         "finish_state",
-        (1, 4),
-        (pltpu.HBM((rows, latent), BF16),),
-        [pltpu.VMEM((rim, latent), BF16), pltpu.SemaphoreType.DMA((2,))],
+        (1, 4 + pieces),
+        (pltpu.HBM((rows, latent), BF16),) + sums,
+        [pltpu.VMEM((rim, latent), BF16)]
+        + piece_scratch
+        + [pltpu.SemaphoreType.DMA((2,)), pltpu.SemaphoreType.DMA((2 * pieces,))],
         aliases={0: 0},
-    )(grad_state, valid, own_rim, even_rows, back_odd)
-    other = swap(jnp.stack(near), "dom", 1)
-    other = [other[k] for k in range(dom // 2)]
-    *other, grad_state = lax.optimization_barrier((*other, grad_state))
+    )(grad_state, valid, own_rim, even_rows, back_odd, *near)
     grad_w_in, grad_w_out, grad_gain = kernel(
         unpack_kernel,
         "unpack_sums",
-        (0, dom),
-        shapes((w_in.shape, F32), (w_out.shape, F32), ((1, latent), F32)),
-    )(*near, *other)
+        (2, 1 + pieces),
+        sums[:2] + (pltpu.HBM((1, latent), F32),),
+        piece_scratch
+        + [pltpu.VMEM((1, latent), F32), pltpu.SemaphoreType.DMA((2 * pieces,)), pltpu.SemaphoreType.DMA],
+        aliases={0: 0, 1: 1},
+    )(grad_w_in, grad_w_out, gain_near, *[other[k] for k in range(pieces)])
     return new_state, grad_state, grad_w_in, grad_w_out, grad_gain.reshape(latent)
 
 

time: 40.8 us -> 40.6 us (level)
  transfers between devices with their start and end apart: 15 -> 15, of which waited for: 9 -> 9; matrix products, arithmetic and copies ran while one was open for 0% -> 0% of each run, Pallas kernels for 16% -> 17%
where the time goes in v7:
time: 40.6 us; the launch traced here: 40.5 us
  starting transfers between devices  22.2 us (55%)
  Pallas kernels  9.93 us (24%)
  waiting for transfers between devices  7.42 us (18%)
  between operations  0.75 us (2%)
    ppermute x11, starting transfers between devices, swap(): return lax.ppermute(x, axis, [(i, i ^ turn) for i in range(count)])  11.7 us
    pallas_call x7, Pallas kernels, run(): return call(*placed, *given[far:])  9.93 us
    ppermute x11, waiting for transfers between devices, swap(): return lax.ppermute(x, axis, [(i, i ^ turn) for i in range(count)])  6.02 us
    ppermute x1, starting transfers between devices, local(): from_next = lax.ppermute(to_back, ring, back_pairs)  3.42 us
    ppermute x1, starting transfers between devices, local(): from_back = lax.ppermute(to_next, ring, next_pairs)  3.08 us
    ppermute x1, starting transfers between devices, local(): back_odd = lax.ppermute(spill_odd, ring, odd_pairs)  2.34 us
    ppermute x1, starting transfers between devices, local(): back_even = lax.ppermute(spill_even, ring, even_pairs)  1.62 us
    ppermute x1, waiting for transfers between devices, local(): back_odd = lax.ppermute(spill_odd, ring, odd_pairs)  1.23 us
  transfers between devices with their start and end apart: 15, of which 9 were waited for; matrix products, arithmetic and copies ran while one was open for 0% of the time, Pallas kernels for 17%

profile of v7, /device:TPU:0, one launch (start us, length us, event | category | flops | bytes accessed | tf_op | source)
XLA Modules:
  0.0 40.5 jit_solution(15826196950184583019)
XLA Ops:
  0.6 1.0 %pack_rims.1 = (bf16[256,256]{1,0:T(8,128)(2,1)S(1)}, bf16[256,256]{1,0:T(8,128)(2,1)S(1)}) custom-call(s32[8]{0:T(128)} %len_ref.1, bf16[1024,256]{1,0:T(8,128)(2,1)} %state_ref.1), custom_call_target="tpu_custom_call" | custom-call | tf_op jit(solution)/shard_map/pack_rims/pallas_call | solution.py:437
  1.7 3.1 %collective-permute-start = (bf16[256,256]{1,0:T(8,128)(2,1)S(1)}, bf16[256,256]{1,0:T(8,128)(2,1)S(1)}, u32[]{:S(2)}, u32[]{:S(2)}) collective-permute-start(bf16[256,256]{1,0:T(8,128)(2,1)S(1)} %get-tuple-element.53), channel_id=1, source_target_pairs={{0,1},{1,2},{2,3},{3,4},{4,5},{5,6},{6,7},{7,8},{8,9},{9,10},{10,1... | collective-permute-start | bytes 393224 | tf_op jit(solution)/shard_map/ppermute | solution.py:471
  4.8 3.4 %collective-permute-start.1 = (bf16[256,256]{1,0:T(8,128)(2,1)S(1)}, bf16[256,256]{1,0:T(8,128)(2,1)S(1)}, u32[]{:S(2)}, u32[]{:S(2)}) collective-permute-start(bf16[256,256]{1,0:T(8,128)(2,1)S(1)} %get-tuple-element.54), channel_id=1, source_target_pairs={{0,31},{1,0},{2,1},{3,2},{4,3},{5,4},{6,5},{7,6},{8,7},{9,8},{10,9... | collective-permute-start | bytes 393224 | tf_op jit(solution)/shard_map/ppermute | solution.py:472
  8.2 4.2 %inner_rows.1 = (bf16[512,256]{1,0:T(8,128)(2,1)S(1)}, f32[512,256]{1,0:T(8,128)S(1)}, f32[1024,256]{1,0:T(8,128)S(1)}, f32[512,256]{1,0:T(8,128)S(1)}, f32[256,...) custom-call(s32[8]{0:T(128)} %len_ref.1, ...), custom_call_target="tpu_custom_call" | custom-call | flops 1006632960 | bytes 10485760 | tf_op jit(solution)/shard_map/inner_rows/pallas_call | solution.py:437
  12.5 1.3 %rim_rows.1 = (bf16[2,4,104,256]{3,2,1,0:T(8,128)(2,1)S(1)}, bf16[512,256]{1,0:T(8,128)(2,1)S(1)}, bf16[512,256]{1,0:T(8,128)(2,1)S(1)}) custom-call(f32[1024,1]{1,0:T(8,128)S(1)} %get-tuple-element.41.valid_ref, bf16[512,256]{1,0:T(8,128)(2,1)S(1)} %get-tuple-element.45.state_ref, bf16[512,256]{1,0:T(8,128)(2,1)S(1)} %get-tuple-element.42.up_ref, ...), custom_call_target="tpu_custom_call" | custom-call | flops 1006632960 | bytes 8388608 | tf_op jit(solution)/shard_map/rim_rows/pallas_call | solution.py:437
  14.0 1.5 %collective-permute-done.2 = bf16[4,104,256]{2,1,0:T(8,128)(2,1)S(1)} collective-permute-done((bf16[4,104,256]{2,1,0:T(8,128)(2,1)S(1)}, bf16[4,104,256]{2,1,0:T(8,128)(2,1)S(1)}, u32[]{:S(2)}, u32[]{:S(2)}) %collective-permute-start.2) | collective-permute-done | bytes 213024 | tf_op jit(solution)/shard_map/ppermute | solution.py:389
  15.5 1.6 %collective-permute-start.3 = (bf16[104,256]{1,0:T(8,128)(2,1)S(1)}, bf16[104,256]{1,0:T(8,128)(2,1)S(1)}, u32[]{:S(2)}, u32[]{:S(2)}) collective-permute-start(bf16[104,256]{1,0:T(8,128)(2,1)S(1)} %get-tuple-element.81), channel_id=1, source_target_pairs={{0,8},{4,12},{8,0},{12,4},{16,24},{20,28},{24,16},{28,20},{1,9},{5... | collective-permute-start | bytes 159752 | tf_op jit(solution)/shard_map/ppermute | solution.py:389
  17.1 1.7 %collective-permute-start.5 = (bf16[104,256]{1,0:T(8,128)(2,1)S(1)}, bf16[104,256]{1,0:T(8,128)(2,1)S(1)}, u32[]{:S(2)}, u32[]{:S(2)}) collective-permute-start(bf16[104,256]{1,0:T(8,128)(2,1)S(1)} %get-tuple-element.82), channel_id=1, source_target_pairs={{0,24},{4,28},{8,16},{12,20},{16,8},{20,12},{24,0},{28,4},{1,25},{... | collective-permute-start | bytes 159752 | tf_op jit(solution)/shard_map/ppermute | solution.py:389
  19.1 1.5 %rim_back.1 = (bf16[256,256]{1,0:T(8,128)(2,1)S(1)}, bf16[256,256]{1,0:T(8,128)(2,1)S(1)}, f32[512,256]{1,0:T(8,128)S(1)}, bf16[1024,256]{1,0:T(8,128)(2,1)}, bf16[1024,256]{1,0:T(8,128)(2,1)}) custom-call(f32[1024,1]{1,0:T(8,128)S(1)} %get-tuple-element.41.valid_ref, bf16[512,256]{1,0:T(8,128)(2,1)S(1)} %get-tuple-element.42.up_ref, ...), custom_call_target="tpu_custom_call" | custom-call | flops 335544320 | bytes 4194304 | tf_op jit(solution)/shard_map/rim_back/pallas_call | solution.py:437
  20.6 1.6 %collective-permute-start.9 = (bf16[256,256]{1,0:T(8,128)(2,1)S(1)}, bf16[256,256]{1,0:T(8,128)(2,1)S(1)}, u32[]{:S(2)}, u32[]{:S(2)}) collective-permute-start(bf16[256,256]{1,0:T(8,128)(2,1)S(1)} %get-tuple-element.64), channel_id=1, source_target_pairs={{0,1},{1,0},{2,3},{3,2},{4,5},{5,4},{6,7},{7,6},{8,9},{9,8},{10,11... | collective-permute-start | bytes 393224 | tf_op jit(solution)/shard_map/ppermute | solution.py:541
  22.2 0.8 %collective-permute-done.4 = bf16[104,256]{1,0:T(8,128)(2,1)S(1)} collective-permute-done((bf16[104,256]{1,0:T(8,128)(2,1)S(1)}, bf16[104,256]{1,0:T(8,128)(2,1)S(1)}, u32[]{:S(2)}, u32[]{:S(2)}) %collective-permute-start.4) | collective-permute-done | bytes 53280 | tf_op jit(solution)/shard_map/ppermute | solution.py:389
  23.0 3.0 %collective-permute-start.8 = (bf16[104,256]{1,0:T(8,128)(2,1)S(1)}, bf16[104,256]{1,0:T(8,128)(2,1)S(1)}, u32[]{:S(2)}, u32[]{:S(2)}) collective-permute-start(bf16[104,256]{1,0:T(8,128)(2,1)S(1)} %fusion.3), channel_id=1, source_target_pairs={{0,3},{1,2},{2,1},{3,0},{4,7},{5,6},{6,5},{7,4},{8,11},{9,10},{10,... | collective-permute-start | bytes 159752 | tf_op jit(solution)/shard_map/ppermute | solution.py:389
  26.0 1.5 %collective-permute-start.6 = (bf16[104,256]{1,0:T(8,128)(2,1)S(1)}, bf16[104,256]{1,0:T(8,128)(2,1)S(1)}, u32[]{:S(2)}, u32[]{:S(2)}) collective-permute-start(bf16[104,256]{1,0:T(8,128)(2,1)S(1)} %fusion.3), channel_id=1, source_target_pairs={{0,1},{1,0},{2,3},{3,2},{4,5},{5,4},{6,7},{7,6},{8,9},{9,8},{10,11... | collective-permute-start | bytes 159752 | tf_op jit(solution)/shard_map/ppermute | solution.py:389
  27.5 2.3 %collective-permute-start.11 = (bf16[256,256]{1,0:T(8,128)(2,1)S(1)}, bf16[256,256]{1,0:T(8,128)(2,1)S(1)}, u32[]{:S(2)}, u32[]{:S(2)}) collective-permute-start(bf16[256,256]{1,0:T(8,128)(2,1)S(1)} %get-tuple-element.67), channel_id=1, source_target_pairs={{0,31},{1,2},{2,1},{3,4},{4,3},{5,6},{6,5},{7,8},{8,7},{9,10},{10,... | collective-permute-start | bytes 393224 | tf_op jit(solution)/shard_map/ppermute | solution.py:540
  29.9 1.7 %collective-permute-done.7 = bf16[104,256]{1,0:T(8,128)(2,1)S(1)} collective-permute-done((bf16[104,256]{1,0:T(8,128)(2,1)S(1)}, bf16[104,256]{1,0:T(8,128)(2,1)S(1)}, u32[]{:S(2)}, u32[]{:S(2)}) %collective-permute-start.7) | collective-permute-done | bytes 53280 | tf_op jit(solution)/shard_map/ppermute | solution.py:389
  31.7 1.6 %collective-permute-start.10 = (bf16[104,256]{1,0:T(8,128)(2,1)S(1)}, bf16[104,256]{1,0:T(8,128)(2,1)S(1)}, u32[]{:S(2)}, u32[]{:S(2)}) collective-permute-start(bf16[104,256]{1,0:T(8,128)(2,1)S(1)} %add_convert_fusion.refs_0_), channel_id=1, source_target_pairs={{0,24},{4,28},{8,16},{12,20},{16,8},{20,12},{24,0},{28,4},{1,25},{... | collective-permute-start | bytes 159752 | tf_op jit(solution)/shard_map/ppermute | solution.py:389
  33.3 0.6 %collective-permute-start.13 = (bf16[104,256]{1,0:T(8,128)(2,1)S(1)}, bf16[104,256]{1,0:T(8,128)(2,1)S(1)}, u32[]{:S(2)}, u32[]{:S(2)}) collective-permute-start(bf16[104,256]{1,0:T(8,128)(2,1)S(1)} %add_convert_fusion.refs_0_), channel_id=1, source_target_pairs={{0,16},{4,20},{8,24},{12,28},{16,0},{20,4},{24,8},{28,12},{1,17},{... | collective-permute-start | bytes 159752 | tf_op jit(solution)/shard_map/ppermute | solution.py:389
  33.9 1.3 %collective-permute-start.12 = (bf16[104,256]{1,0:T(8,128)(2,1)S(1)}, bf16[104,256]{1,0:T(8,128)(2,1)S(1)}, u32[]{:S(2)}, u32[]{:S(2)}) collective-permute-start(bf16[104,256]{1,0:T(8,128)(2,1)S(1)} %add_convert_fusion.refs_0_), channel_id=1, source_target_pairs={{0,8},{4,12},{8,0},{12,4},{16,24},{20,28},{24,16},{28,20},{1,9},{5... | collective-permute-start | bytes 159752 | tf_op jit(solution)/shard_map/ppermute | solution.py:389
  35.2 1.2 %collective-permute-done.11.back_ref = bf16[256,256]{1,0:T(8,128)(2,1)S(1)} collective-permute-done((bf16[256,256]{1,0:T(8,128)(2,1)S(1)}, bf16[256,256]{1,0:T(8,128)(2,1)S(1)}, u32[]{:S(2)}, u32[]{:S(2)}) %collective-permute-start.11) | collective-permute-done | bytes 131104 | tf_op jit(solution)/shard_map/ppermute | solution.py:540
  36.5 1.1 %collective-permute-done.10.refs_3_ = bf16[104,256]{1,0:T(8,128)(2,1)S(1)} collective-permute-done((bf16[104,256]{1,0:T(8,128)(2,1)S(1)}, bf16[104,256]{1,0:T(8,128)(2,1)S(1)}, u32[]{:S(2)}, u32[]{:S(2)}) %collective-permute-start.10) | collective-permute-done | bytes 53280 | tf_op jit(solution)/shard_map/ppermute | solution.py:389
  37.5 0.4 collective-permute-done.13.refs_2_
  38.2 1.0 %finish_state.1 = (bf16[1024,256]{1,0:T(8,128)(2,1)}, f32[512,256]{1,0:T(8,128)}, f32[256,256]{1,0:T(8,128)}, f32[1,256]{1,0:T(1,128)S(1)}) custom-call(bf16[1024,256]{1,0:T(8,128)(2,1)} %get-tuple-element.61.started_ref, f32[1024,1]{1,0:T(8,128)S(1)} %get-tuple-element.41.valid_ref, ...), custom_call_target="tpu_custom_call", output_to_operand_aliasing={{0}: (0, {})} | custom-call | tf_op jit(solution)/shard_map/finish_state/pallas_call | solution.py:437
  39.1 0.5 %collective-permute-done.14 = bf16[4,104,256]{2,1,0:T(8,128)(2,1)S(1)} collective-permute-done((bf16[4,104,256]{2,1,0:T(8,128)(2,1)S(1)}, bf16[4,104,256]{2,1,0:T(8,128)(2,1)S(1)}, u32[]{:S(2)}, u32[]{:S(2)}) %collective-permute-start.14) | collective-permute-done | bytes 213024 | tf_op jit(solution)/shard_map/ppermute | solution.py:389
  39.6 0.8 %unpack_sums.1 = (f32[512,256]{1,0:T(8,128)}, f32[256,256]{1,0:T(8,128)}, f32[1,256]{1,0:T(1,128)}) custom-call(f32[512,256]{1,0:T(8,128)} %get-tuple-element.71.begun_in_ref, f32[256,256]{1,0:T(8,128)} %get-tuple-element.72.begun_out_ref, f32[1,256]{1,0:T(1,128)S(1)} %get-tuple-element.73.gain_near_ref, ...), custom_call_target="tpu_custom_call", output_to_operand_aliasing={{0}: (0, {}), {1}: (1, {})} | custom-call | tf_op jit(solution)/shard_map/unpack_sums/pallas_call | solution.py:437
  (20 shorter events, 1.1 us)
Async XLA Ops:
  1.7 10.7 %collective-permute-start = (bf16[256,256]{1,0:T(8,128)(2,1)S(1)}, bf16[256,256]{1,0:T(8,128)(2,1)S(1)}, u32[]{:S(2)}, u32[]{:S(2)}) collective-permute-start(bf16[256,256]{1,0:T(8,128)(2,1)S(1)} %get-tuple-element.53), channel_id=1, source_target_pairs={{0,1},{1,2},{2,3},{3,4},{4,5},{5,6},{6,7},{7,8},{8,9},{9,10},{10,1... | collective-permute-start | bytes 393224 | tf_op jit(solution)/shard_map/ppermute | solution.py:471
  4.8 7.8 %collective-permute-start.1 = (bf16[256,256]{1,0:T(8,128)(2,1)S(1)}, bf16[256,256]{1,0:T(8,128)(2,1)S(1)}, u32[]{:S(2)}, u32[]{:S(2)}) collective-permute-start(bf16[256,256]{1,0:T(8,128)(2,1)S(1)} %get-tuple-element.54), channel_id=1, source_target_pairs={{0,31},{1,0},{2,1},{3,2},{4,3},{5,4},{6,5},{7,6},{8,7},{9,8},{10,9... | collective-permute-start | bytes 393224 | tf_op jit(solution)/shard_map/ppermute | solution.py:472
  13.9 1.5 %collective-permute-start.2 = (bf16[4,104,256]{2,1,0:T(8,128)(2,1)S(1)}, bf16[4,104,256]{2,1,0:T(8,128)(2,1)S(1)}, u32[]{:S(2)}, u32[]{:S(2)}) collective-permute-start(bf16[4,104,256]{2,1,0:T(8,128)(2,1)S(1)} %slice_bitcast_fusion), channel_id=1, source_target_pairs={{0,4},{4,0},{8,12},{12,8},{16,20},{20,16},{24,28},{28,24},{1,5},{5... | collective-permute-start | bytes 638984 | tf_op jit(solution)/shard_map/ppermute | solution.py:389
  15.5 6.7 %collective-permute-start.3 = (bf16[104,256]{1,0:T(8,128)(2,1)S(1)}, bf16[104,256]{1,0:T(8,128)(2,1)S(1)}, u32[]{:S(2)}, u32[]{:S(2)}) collective-permute-start(bf16[104,256]{1,0:T(8,128)(2,1)S(1)} %get-tuple-element.81), channel_id=1, source_target_pairs={{0,8},{4,12},{8,0},{12,4},{16,24},{20,28},{24,16},{28,20},{1,9},{5... | collective-permute-start | bytes 159752 | tf_op jit(solution)/shard_map/ppermute | solution.py:389
  17.1 5.1 %collective-permute-start.5 = (bf16[104,256]{1,0:T(8,128)(2,1)S(1)}, bf16[104,256]{1,0:T(8,128)(2,1)S(1)}, u32[]{:S(2)}, u32[]{:S(2)}) collective-permute-start(bf16[104,256]{1,0:T(8,128)(2,1)S(1)} %get-tuple-element.82), channel_id=1, source_target_pairs={{0,24},{4,28},{8,16},{12,20},{16,8},{20,12},{24,0},{28,4},{1,25},{... | collective-permute-start | bytes 159752 | tf_op jit(solution)/shard_map/ppermute | solution.py:389
  18.8 4.2 %collective-permute-start.4 = (bf16[104,256]{1,0:T(8,128)(2,1)S(1)}, bf16[104,256]{1,0:T(8,128)(2,1)S(1)}, u32[]{:S(2)}, u32[]{:S(2)}) collective-permute-start(bf16[104,256]{1,0:T(8,128)(2,1)S(1)} %get-tuple-element.83), channel_id=1, source_target_pairs={{0,16},{4,20},{8,24},{12,28},{16,0},{20,4},{24,8},{28,12},{1,17},{... | collective-permute-start | bytes 159752 | tf_op jit(solution)/shard_map/ppermute | solution.py:389
  20.6 9.2 %collective-permute-start.9 = (bf16[256,256]{1,0:T(8,128)(2,1)S(1)}, bf16[256,256]{1,0:T(8,128)(2,1)S(1)}, u32[]{:S(2)}, u32[]{:S(2)}) collective-permute-start(bf16[256,256]{1,0:T(8,128)(2,1)S(1)} %get-tuple-element.64), channel_id=1, source_target_pairs={{0,1},{1,0},{2,3},{3,2},{4,5},{5,4},{6,7},{7,6},{8,9},{9,8},{10,11... | collective-permute-start | bytes 393224 | tf_op jit(solution)/shard_map/ppermute | solution.py:541
  23.0 6.9 %collective-permute-start.8 = (bf16[104,256]{1,0:T(8,128)(2,1)S(1)}, bf16[104,256]{1,0:T(8,128)(2,1)S(1)}, u32[]{:S(2)}, u32[]{:S(2)}) collective-permute-start(bf16[104,256]{1,0:T(8,128)(2,1)S(1)} %fusion.3), channel_id=1, source_target_pairs={{0,3},{1,2},{2,1},{3,0},{4,7},{5,6},{6,5},{7,4},{8,11},{9,10},{10,... | collective-permute-start | bytes 159752 | tf_op jit(solution)/shard_map/ppermute | solution.py:389
  26.0 5.7 %collective-permute-start.7 = (bf16[104,256]{1,0:T(8,128)(2,1)S(1)}, bf16[104,256]{1,0:T(8,128)(2,1)S(1)}, u32[]{:S(2)}, u32[]{:S(2)}) collective-permute-start(bf16[104,256]{1,0:T(8,128)(2,1)S(1)} %fusion.3), channel_id=1, source_target_pairs={{0,2},{1,3},{2,0},{3,1},{4,6},{5,7},{6,4},{7,5},{8,10},{9,11},{10,... | collective-permute-start | bytes 159752 | tf_op jit(solution)/shard_map/ppermute | solution.py:389
  26.0 5.6 %collective-permute-start.6 = (bf16[104,256]{1,0:T(8,128)(2,1)S(1)}, bf16[104,256]{1,0:T(8,128)(2,1)S(1)}, u32[]{:S(2)}, u32[]{:S(2)}) collective-permute-start(bf16[104,256]{1,0:T(8,128)(2,1)S(1)} %fusion.3), channel_id=1, source_target_pairs={{0,1},{1,0},{2,3},{3,2},{4,5},{5,4},{6,7},{7,6},{8,9},{9,8},{10,11... | collective-permute-start | bytes 159752 | tf_op jit(solution)/shard_map/ppermute | solution.py:389
  27.5 9.0 %collective-permute-start.11 = (bf16[256,256]{1,0:T(8,128)(2,1)S(1)}, bf16[256,256]{1,0:T(8,128)(2,1)S(1)}, u32[]{:S(2)}, u32[]{:S(2)}) collective-permute-start(bf16[256,256]{1,0:T(8,128)(2,1)S(1)} %get-tuple-element.67), channel_id=1, source_target_pairs={{0,31},{1,2},{2,1},{3,4},{4,3},{5,6},{6,5},{7,8},{8,7},{9,10},{10,... | collective-permute-start | bytes 393224 | tf_op jit(solution)/shard_map/ppermute | solution.py:540
  31.7 5.8 %collective-permute-start.10 = (bf16[104,256]{1,0:T(8,128)(2,1)S(1)}, bf16[104,256]{1,0:T(8,128)(2,1)S(1)}, u32[]{:S(2)}, u32[]{:S(2)}) collective-permute-start(bf16[104,256]{1,0:T(8,128)(2,1)S(1)} %add_convert_fusion.refs_0_), channel_id=1, source_target_pairs={{0,24},{4,28},{8,16},{12,20},{16,8},{20,12},{24,0},{28,4},{1,25},{... | collective-permute-start | bytes 159752 | tf_op jit(solution)/shard_map/ppermute | solution.py:389
  33.3 4.6 %collective-permute-start.13 = (bf16[104,256]{1,0:T(8,128)(2,1)S(1)}, bf16[104,256]{1,0:T(8,128)(2,1)S(1)}, u32[]{:S(2)}, u32[]{:S(2)}) collective-permute-start(bf16[104,256]{1,0:T(8,128)(2,1)S(1)} %add_convert_fusion.refs_0_), channel_id=1, source_target_pairs={{0,16},{4,20},{8,24},{12,28},{16,0},{20,4},{24,8},{28,12},{1,17},{... | collective-permute-start | bytes 159752 | tf_op jit(solution)/shard_map/ppermute | solution.py:389
  33.9 4.1 %collective-permute-start.12 = (bf16[104,256]{1,0:T(8,128)(2,1)S(1)}, bf16[104,256]{1,0:T(8,128)(2,1)S(1)}, u32[]{:S(2)}, u32[]{:S(2)}) collective-permute-start(bf16[104,256]{1,0:T(8,128)(2,1)S(1)} %add_convert_fusion.refs_0_), channel_id=1, source_target_pairs={{0,8},{4,12},{8,0},{12,4},{16,24},{20,28},{24,16},{28,20},{1,9},{5... | collective-permute-start | bytes 159752 | tf_op jit(solution)/shard_map/ppermute | solution.py:389
  38.1 1.5 %collective-permute-start.14 = (bf16[4,104,256]{2,1,0:T(8,128)(2,1)S(1)}, bf16[4,104,256]{2,1,0:T(8,128)(2,1)S(1)}, u32[]{:S(2)}, u32[]{:S(2)}) collective-permute-start(bf16[4,104,256]{2,1,0:T(8,128)(2,1)S(1)} %pad_maximum_fusion), channel_id=1, source_target_pairs={{0,4},{4,0},{8,12},{12,8},{16,20},{20,16},{24,28},{28,24},{1,5},{5... | collective-permute-start | bytes 638984 | tf_op jit(solution)/shard_map/ppermute | solution.py:389

commit v8 on v7

--- a/solution.py
+++ b/solution.py
@@ -219,7 +219,8 @@
     inner_gain_ref,
     low_ref,
     high_ref,
-    send_ref,
+    keep_ref,
+    give_ref,
     new_ref,
     pre_ref,
     grad_in_ref,
@@ -245,23 +246,19 @@
     grad_in_ref[latent:, :] = inner_in_ref[latent:, :] + dot(message, grad_pre, (0, 0))
     pre_ref[...] = grad_pre
 
-    count = send_ref.shape[0] * send_ref.shape[1]
+    count = 2 * keep_ref.shape[0]
     n_in = grad_in_ref.shape[0] // count
     n_out = grad_out_ref.shape[0] // count
     top = lax.broadcasted_iota(jnp.int32, (GAIN_ROWS, latent), 0) == 0
-    for piece in range(count):
-        turn = lax.bitwise_xor(me, piece)
-        half = lax.bitwise_and(turn, 1)
-        slot = lax.shift_right_logical(turn, 1)
-        send_ref[half, slot, :n_in, :] = (grad_in_ref[piece * n_in : (piece + 1) * n_in, :] * scale).astype(BF16)
-        send_ref[half, slot, n_in : n_in + n_out, :] = (
-            grad_out_ref[piece * n_out : (piece + 1) * n_out, :] * scale
-        ).astype(BF16)
-        if piece == 0:
-            tail = jnp.where(top, gain_sum * scale, 0.0)
-        else:
-            tail = jnp.zeros((GAIN_ROWS, latent), F32)
-        send_ref[half, slot, n_in + n_out :, :] = tail.astype(BF16)
+    gain_rows = jnp.where(top, gain_sum * scale, 0.0)
+    for turn in range(count):
+        piece = lax.bitwise_xor(me, turn)
+        target = (give_ref if turn % 2 else keep_ref).at[turn // 2]
+        at_in = pl.ds(pl.multiple_of(piece * n_in, n_in), n_in)
+        at_out = pl.ds(pl.multiple_of(piece * n_out, n_out), n_out)
+        target[:n_in, :] = (grad_in_ref[at_in, :] * scale).astype(BF16)
+        target[n_in : n_in + n_out, :] = (grad_out_ref[at_out, :] * scale).astype(BF16)
+        target[n_in + n_out :, :] = jnp.where(piece == 0, gain_rows, 0.0).astype(BF16)
 
 
 def back_kernel(
@@ -371,7 +368,7 @@
 
 def unpack_kernel(begun_in_ref, begun_out_ref, gain_near_ref, *refs):
     grad_in_ref, grad_out_ref, gain_ref, in_ref, piece_out_ref, total_ref, sems, gain_sem = refs[-8:]
-    far = refs[:-8]
+    far = [refs[0].at[n] for n in range(refs[0].shape[0])]
     _, me = place()
     turns = range(1, 2 * len(far), 2)
     gain, copies = write_pieces(
@@ -509,12 +506,13 @@
 
     n_in, n_out = w_in.shape[0] // dom, w_out.shape[0] // dom
     piece_rows = n_in + n_out + GAIN_ROWS
-    send, new_rim, pre_rim = kernel(
+    keep, give, new_rim, pre_rim = kernel(
         functools.partial(rim_kernel, scale),
         "rim_rows",
         (0, 14),
         shapes(
-            ((2, dom // 2, piece_rows, latent), BF16),
+            ((dom // 2, piece_rows, latent), BF16),
+            ((dom // 2, piece_rows, latent), BF16),
             ((2 * rim, latent), BF16),
             ((2 * rim, latent), BF16),
         ),
@@ -545,8 +543,8 @@
         (0, 3),
         shapes(((rim, latent), BF16)),
     )(valid, own_rim, back_even)
-    other = swap(send[1], "dom", 1)
-    held = (send[0].astype(F32) + other.astype(F32)).astype(BF16)
+    other = swap(give, "dom", 1)
+    held = (keep.astype(F32) + other.astype(F32)).astype(BF16)
     held = [held[k] for k in range(dom // 2)]
 
     parts = [held[0]] + [swap(held[k], "dom", 2 * k) for k in range(1, dom // 2)]
@@ -576,12 +574,12 @@
     grad_w_in, grad_w_out, grad_gain = kernel(
         unpack_kernel,
         "unpack_sums",
-        (2, 1 + pieces),
+        (2, 2),
         sums[:2] + (pltpu.HBM((1, latent), F32),),
         piece_scratch
         + [pltpu.VMEM((1, latent), F32), pltpu.SemaphoreType.DMA((2 * pieces,)), pltpu.SemaphoreType.DMA],
         aliases={0: 0, 1: 1},
-    )(grad_w_in, grad_w_out, gain_near, *[other[k] for k in range(pieces)])
+    )(grad_w_in, grad_w_out, gain_near, other)
     return new_state, grad_state, grad_w_in, grad_w_out, grad_gain.reshape(latent)
 
 

time: 40.6 us -> 40.6 us (level)
  no operation moved by 1% of the time
where the time goes in v8:
time: 40.6 us; the launch traced here: 40.4 us
  starting transfers between devices  22.2 us (55%)
  Pallas kernels  9.94 us (24%)
  waiting for transfers between devices  7.44 us (18%)
  between operations  0.74 us (2%)
    ppermute x11, starting transfers between devices, swap(): return lax.ppermute(x, axis, [(i, i ^ turn) for i in range(count)])  11.7 us
    pallas_call x7, Pallas kernels, run(): return call(*placed, *given[far:])  9.94 us
    ppermute x11, waiting for transfers between devices, swap(): return lax.ppermute(x, axis, [(i, i ^ turn) for i in range(count)])  6.04 us
    ppermute x1, starting transfers between devices, local(): from_next = lax.ppermute(to_back, ring, back_pairs)  3.42 us
    ppermute x1, starting transfers between devices, local(): from_back = lax.ppermute(to_next, ring, next_pairs)  3.08 us
    ppermute x1, starting transfers between devices, local(): back_odd = lax.ppermute(spill_odd, ring, odd_pairs)  2.33 us
    ppermute x1, starting transfers between devices, local(): back_even = lax.ppermute(spill_even, ring, even_pairs)  1.63 us
    ppermute x1, waiting for transfers between devices, local(): back_odd = lax.ppermute(spill_odd, ring, odd_pairs)  1.22 us
  transfers between devices with their start and end apart: 15, of which 9 were waited for; matrix products, arithmetic and copies ran while one was open for 0% of the time, Pallas kernels for 17%

profile of v8, /device:TPU:0, one launch (start us, length us, event | category | flops | bytes accessed | tf_op | source)
XLA Modules:
  0.0 40.4 jit_solution(9946462741250015022)
XLA Ops:
  0.6 1.0 %pack_rims.1 = (bf16[256,256]{1,0:T(8,128)(2,1)S(1)}, bf16[256,256]{1,0:T(8,128)(2,1)S(1)}) custom-call(s32[8]{0:T(128)} %len_ref.1, bf16[1024,256]{1,0:T(8,128)(2,1)} %state_ref.1), custom_call_target="tpu_custom_call" | custom-call | tf_op jit(solution)/shard_map/pack_rims/pallas_call | solution.py:434
  1.7 3.1 %collective-permute-start = (bf16[256,256]{1,0:T(8,128)(2,1)S(1)}, bf16[256,256]{1,0:T(8,128)(2,1)S(1)}, u32[]{:S(2)}, u32[]{:S(2)}) collective-permute-start(bf16[256,256]{1,0:T(8,128)(2,1)S(1)} %get-tuple-element.54), channel_id=1, source_target_pairs={{0,1},{1,2},{2,3},{3,4},{4,5},{5,6},{6,7},{7,8},{8,9},{9,10},{10,1... | collective-permute-start | bytes 393224 | tf_op jit(solution)/shard_map/ppermute | solution.py:468
  4.8 3.4 %collective-permute-start.1 = (bf16[256,256]{1,0:T(8,128)(2,1)S(1)}, bf16[256,256]{1,0:T(8,128)(2,1)S(1)}, u32[]{:S(2)}, u32[]{:S(2)}) collective-permute-start(bf16[256,256]{1,0:T(8,128)(2,1)S(1)} %get-tuple-element.55), channel_id=1, source_target_pairs={{0,31},{1,0},{2,1},{3,2},{4,3},{5,4},{6,5},{7,6},{8,7},{9,8},{10,9... | collective-permute-start | bytes 393224 | tf_op jit(solution)/shard_map/ppermute | solution.py:469
  8.2 4.2 %inner_rows.1 = (bf16[512,256]{1,0:T(8,128)(2,1)S(1)}, f32[512,256]{1,0:T(8,128)S(1)}, f32[1024,256]{1,0:T(8,128)S(1)}, f32[512,256]{1,0:T(8,128)S(1)}, f32[256,...) custom-call(s32[8]{0:T(128)} %len_ref.1, ...), custom_call_target="tpu_custom_call" | custom-call | flops 1006632960 | bytes 10485760 | tf_op jit(solution)/shard_map/inner_rows/pallas_call | solution.py:434
  12.5 1.4 %rim_rows.1 = (bf16[4,104,256]{2,1,0:T(8,128)(2,1)S(1)}, bf16[4,104,256]{2,1,0:T(8,128)(2,1)S(1)}, bf16[512,256]{1,0:T(8,128)(2,1)S(1)}, bf16[512,256]{1,0:T(8,128)(2,1)S(1)}) custom-call(f32[1024,1]{1,0:T(8,128)S(1)} %get-tuple-element.42.valid_ref, bf16[512,256]{1,0:T(8,128)(2,1)S(1)} %get-tuple-element.46.state_ref, ...), custom_call_target="tpu_custom_call" | custom-call | flops 1006632960 | bytes 8388608 | tf_op jit(solution)/shard_map/rim_rows/pallas_call | solution.py:434
  14.0 1.5 %collective-permute-done.2 = bf16[4,104,256]{2,1,0:T(8,128)(2,1)S(1)} collective-permute-done((bf16[4,104,256]{2,1,0:T(8,128)(2,1)S(1)}, bf16[4,104,256]{2,1,0:T(8,128)(2,1)S(1)}, u32[]{:S(2)}, u32[]{:S(2)}) %collective-permute-start.2) | collective-permute-done | bytes 213024 | tf_op jit(solution)/shard_map/ppermute | solution.py:386
  15.5 1.6 %collective-permute-start.3 = (bf16[104,256]{1,0:T(8,128)(2,1)S(1)}, bf16[104,256]{1,0:T(8,128)(2,1)S(1)}, u32[]{:S(2)}, u32[]{:S(2)}) collective-permute-start(bf16[104,256]{1,0:T(8,128)(2,1)S(1)} %get-tuple-element.79), channel_id=1, source_target_pairs={{0,8},{4,12},{8,0},{12,4},{16,24},{20,28},{24,16},{28,20},{1,9},{5... | collective-permute-start | bytes 159752 | tf_op jit(solution)/shard_map/ppermute | solution.py:386
  17.1 1.7 %collective-permute-start.5 = (bf16[104,256]{1,0:T(8,128)(2,1)S(1)}, bf16[104,256]{1,0:T(8,128)(2,1)S(1)}, u32[]{:S(2)}, u32[]{:S(2)}) collective-permute-start(bf16[104,256]{1,0:T(8,128)(2,1)S(1)} %get-tuple-element.80), channel_id=1, source_target_pairs={{0,24},{4,28},{8,16},{12,20},{16,8},{20,12},{24,0},{28,4},{1,25},{... | collective-permute-start | bytes 159752 | tf_op jit(solution)/shard_map/ppermute | solution.py:386
  19.1 1.5 %rim_back.1 = (bf16[256,256]{1,0:T(8,128)(2,1)S(1)}, bf16[256,256]{1,0:T(8,128)(2,1)S(1)}, f32[512,256]{1,0:T(8,128)S(1)}, bf16[1024,256]{1,0:T(8,128)(2,1)}, bf16[1024,256]{1,0:T(8,128)(2,1)}) custom-call(f32[1024,1]{1,0:T(8,128)S(1)} %get-tuple-element.42.valid_ref, bf16[512,256]{1,0:T(8,128)(2,1)S(1)} %get-tuple-element.43.up_ref, ...), custom_call_target="tpu_custom_call" | custom-call | flops 335544320 | bytes 4194304 | tf_op jit(solution)/shard_map/rim_back/pallas_call | solution.py:434
  20.6 1.6 %collective-permute-start.9 = (bf16[256,256]{1,0:T(8,128)(2,1)S(1)}, bf16[256,256]{1,0:T(8,128)(2,1)S(1)}, u32[]{:S(2)}, u32[]{:S(2)}) collective-permute-start(bf16[256,256]{1,0:T(8,128)(2,1)S(1)} %get-tuple-element.66), channel_id=1, source_target_pairs={{0,1},{1,0},{2,3},{3,2},{4,5},{5,4},{6,7},{7,6},{8,9},{9,8},{10,11... | collective-permute-start | bytes 393224 | tf_op jit(solution)/shard_map/ppermute | solution.py:539
  22.2 0.8 %collective-permute-done.4 = bf16[104,256]{1,0:T(8,128)(2,1)S(1)} collective-permute-done((bf16[104,256]{1,0:T(8,128)(2,1)S(1)}, bf16[104,256]{1,0:T(8,128)(2,1)S(1)}, u32[]{:S(2)}, u32[]{:S(2)}) %collective-permute-start.4) | collective-permute-done | bytes 53280 | tf_op jit(solution)/shard_map/ppermute | solution.py:386
  23.0 3.0 %collective-permute-start.8 = (bf16[104,256]{1,0:T(8,128)(2,1)S(1)}, bf16[104,256]{1,0:T(8,128)(2,1)S(1)}, u32[]{:S(2)}, u32[]{:S(2)}) collective-permute-start(bf16[104,256]{1,0:T(8,128)(2,1)S(1)} %fusion.2), channel_id=1, source_target_pairs={{0,3},{1,2},{2,1},{3,0},{4,7},{5,6},{6,5},{7,4},{8,11},{9,10},{10,... | collective-permute-start | bytes 159752 | tf_op jit(solution)/shard_map/ppermute | solution.py:386
  26.0 1.5 %collective-permute-start.6 = (bf16[104,256]{1,0:T(8,128)(2,1)S(1)}, bf16[104,256]{1,0:T(8,128)(2,1)S(1)}, u32[]{:S(2)}, u32[]{:S(2)}) collective-permute-start(bf16[104,256]{1,0:T(8,128)(2,1)S(1)} %fusion.2), channel_id=1, source_target_pairs={{0,1},{1,0},{2,3},{3,2},{4,5},{5,4},{6,7},{7,6},{8,9},{9,8},{10,11... | collective-permute-start | bytes 159752 | tf_op jit(solution)/shard_map/ppermute | solution.py:386
  27.4 2.3 %collective-permute-start.11 = (bf16[256,256]{1,0:T(8,128)(2,1)S(1)}, bf16[256,256]{1,0:T(8,128)(2,1)S(1)}, u32[]{:S(2)}, u32[]{:S(2)}) collective-permute-start(bf16[256,256]{1,0:T(8,128)(2,1)S(1)} %get-tuple-element.69), channel_id=1, source_target_pairs={{0,31},{1,2},{2,1},{3,4},{4,3},{5,6},{6,5},{7,8},{8,7},{9,10},{10,... | collective-permute-start | bytes 393224 | tf_op jit(solution)/shard_map/ppermute | solution.py:538
  29.9 1.7 %collective-permute-done.7 = bf16[104,256]{1,0:T(8,128)(2,1)S(1)} collective-permute-done((bf16[104,256]{1,0:T(8,128)(2,1)S(1)}, bf16[104,256]{1,0:T(8,128)(2,1)S(1)}, u32[]{:S(2)}, u32[]{:S(2)}) %collective-permute-start.7) | collective-permute-done | bytes 53280 | tf_op jit(solution)/shard_map/ppermute | solution.py:386
  31.7 1.6 %collective-permute-start.10 = (bf16[104,256]{1,0:T(8,128)(2,1)S(1)}, bf16[104,256]{1,0:T(8,128)(2,1)S(1)}, u32[]{:S(2)}, u32[]{:S(2)}) collective-permute-start(bf16[104,256]{1,0:T(8,128)(2,1)S(1)} %add_convert_fusion.1.refs_0_), channel_id=1, source_target_pairs={{0,24},{4,28},{8,16},{12,20},{16,8},{20,12},{24,0},{28,4},{1,25},{... | collective-permute-start | bytes 159752 | tf_op jit(solution)/shard_map/ppermute | solution.py:386
  33.3 0.6 %collective-permute-start.13 = (bf16[104,256]{1,0:T(8,128)(2,1)S(1)}, bf16[104,256]{1,0:T(8,128)(2,1)S(1)}, u32[]{:S(2)}, u32[]{:S(2)}) collective-permute-start(bf16[104,256]{1,0:T(8,128)(2,1)S(1)} %add_convert_fusion.1.refs_0_), channel_id=1, source_target_pairs={{0,16},{4,20},{8,24},{12,28},{16,0},{20,4},{24,8},{28,12},{1,17},{... | collective-permute-start | bytes 159752 | tf_op jit(solution)/shard_map/ppermute | solution.py:386
  33.9 1.3 %collective-permute-start.12 = (bf16[104,256]{1,0:T(8,128)(2,1)S(1)}, bf16[104,256]{1,0:T(8,128)(2,1)S(1)}, u32[]{:S(2)}, u32[]{:S(2)}) collective-permute-start(bf16[104,256]{1,0:T(8,128)(2,1)S(1)} %add_convert_fusion.1.refs_0_), channel_id=1, source_target_pairs={{0,8},{4,12},{8,0},{12,4},{16,24},{20,28},{24,16},{28,20},{1,9},{5... | collective-permute-start | bytes 159752 | tf_op jit(solution)/shard_map/ppermute | solution.py:386
  35.2 1.2 %collective-permute-done.11.back_ref = bf16[256,256]{1,0:T(8,128)(2,1)S(1)} collective-permute-done((bf16[256,256]{1,0:T(8,128)(2,1)S(1)}, bf16[256,256]{1,0:T(8,128)(2,1)S(1)}, u32[]{:S(2)}, u32[]{:S(2)}) %collective-permute-start.11) | collective-permute-done | bytes 131104 | tf_op jit(solution)/shard_map/ppermute | solution.py:538
  36.4 1.1 %collective-permute-done.10.refs_3_ = bf16[104,256]{1,0:T(8,128)(2,1)S(1)} collective-permute-done((bf16[104,256]{1,0:T(8,128)(2,1)S(1)}, bf16[104,256]{1,0:T(8,128)(2,1)S(1)}, u32[]{:S(2)}, u32[]{:S(2)}) %collective-permute-start.10) | collective-permute-done | bytes 53280 | tf_op jit(solution)/shard_map/ppermute | solution.py:386
  37.5 0.4 collective-permute-done.13.refs_2_
  38.2 1.0 %finish_state.1 = (bf16[1024,256]{1,0:T(8,128)(2,1)}, f32[512,256]{1,0:T(8,128)}, f32[256,256]{1,0:T(8,128)}, f32[1,256]{1,0:T(1,128)S(1)}) custom-call(bf16[1024,256]{1,0:T(8,128)(2,1)} %get-tuple-element.62.started_ref, f32[1024,1]{1,0:T(8,128)S(1)} %get-tuple-element.42.valid_ref, ...), custom_call_target="tpu_custom_call", output_to_operand_aliasing={{0}: (0, {})} | custom-call | tf_op jit(solution)/shard_map/finish_state/pallas_call | solution.py:434
  39.1 0.5 %collective-permute-done.14.refs_0_ = bf16[4,104,256]{2,1,0:T(8,128)(2,1)S(1)} collective-permute-done((bf16[4,104,256]{2,1,0:T(8,128)(2,1)S(1)}, bf16[4,104,256]{2,1,0:T(8,128)(2,1)S(1)}, u32[]{:S(2)}, u32[]{:S(2)}) %collective-permute-start.14) | collective-permute-done | bytes 213024 | tf_op jit(solution)/shard_map/ppermute | solution.py:386
  39.6 0.8 %unpack_sums.1 = (f32[512,256]{1,0:T(8,128)}, f32[256,256]{1,0:T(8,128)}, f32[1,256]{1,0:T(1,128)}) custom-call(f32[512,256]{1,0:T(8,128)} %get-tuple-element.73.begun_in_ref, f32[256,256]{1,0:T(8,128)} %get-tuple-element.74.begun_out_ref, f32[1,256]{1,0:T(1,128)S(1)} %get-tuple-element.75.gain_near_ref, ...), custom_call_target="tpu_custom_call", output_to_operand_aliasing={{0}: (0, {}), {1}: (1, {})} | custom-call | tf_op jit(solution)/shard_map/unpack_sums/pallas_call | solution.py:434
  (18 shorter events, 1.1 us)
Async XLA Ops:
  1.7 10.7 %collective-permute-start = (bf16[256,256]{1,0:T(8,128)(2,1)S(1)}, bf16[256,256]{1,0:T(8,128)(2,1)S(1)}, u32[]{:S(2)}, u32[]{:S(2)}) collective-permute-start(bf16[256,256]{1,0:T(8,128)(2,1)S(1)} %get-tuple-element.54), channel_id=1, source_target_pairs={{0,1},{1,2},{2,3},{3,4},{4,5},{5,6},{6,7},{7,8},{8,9},{9,10},{10,1... | collective-permute-start | bytes 393224 | tf_op jit(solution)/shard_map/ppermute | solution.py:468
  4.8 7.8 %collective-permute-start.1 = (bf16[256,256]{1,0:T(8,128)(2,1)S(1)}, bf16[256,256]{1,0:T(8,128)(2,1)S(1)}, u32[]{:S(2)}, u32[]{:S(2)}) collective-permute-start(bf16[256,256]{1,0:T(8,128)(2,1)S(1)} %get-tuple-element.55), channel_id=1, source_target_pairs={{0,31},{1,0},{2,1},{3,2},{4,3},{5,4},{6,5},{7,6},{8,7},{9,8},{10,9... | collective-permute-start | bytes 393224 | tf_op jit(solution)/shard_map/ppermute | solution.py:469
  13.9 1.5 %collective-permute-start.2 = (bf16[4,104,256]{2,1,0:T(8,128)(2,1)S(1)}, bf16[4,104,256]{2,1,0:T(8,128)(2,1)S(1)}, u32[]{:S(2)}, u32[]{:S(2)}) collective-permute-start(bf16[4,104,256]{2,1,0:T(8,128)(2,1)S(1)} %get-tuple-element.65), channel_id=1, source_target_pairs={{0,4},{4,0},{8,12},{12,8},{16,20},{20,16},{24,28},{28,24},{1,5},{5... | collective-permute-start | bytes 638984 | tf_op jit(solution)/shard_map/ppermute | solution.py:386
  15.5 6.7 %collective-permute-start.3 = (bf16[104,256]{1,0:T(8,128)(2,1)S(1)}, bf16[104,256]{1,0:T(8,128)(2,1)S(1)}, u32[]{:S(2)}, u32[]{:S(2)}) collective-permute-start(bf16[104,256]{1,0:T(8,128)(2,1)S(1)} %get-tuple-element.79), channel_id=1, source_target_pairs={{0,8},{4,12},{8,0},{12,4},{16,24},{20,28},{24,16},{28,20},{1,9},{5... | collective-permute-start | bytes 159752 | tf_op jit(solution)/shard_map/ppermute | solution.py:386
  17.1 5.1 %collective-permute-start.5 = (bf16[104,256]{1,0:T(8,128)(2,1)S(1)}, bf16[104,256]{1,0:T(8,128)(2,1)S(1)}, u32[]{:S(2)}, u32[]{:S(2)}) collective-permute-start(bf16[104,256]{1,0:T(8,128)(2,1)S(1)} %get-tuple-element.80), channel_id=1, source_target_pairs={{0,24},{4,28},{8,16},{12,20},{16,8},{20,12},{24,0},{28,4},{1,25},{... | collective-permute-start | bytes 159752 | tf_op jit(solution)/shard_map/ppermute | solution.py:386
  18.8 4.2 %collective-permute-start.4 = (bf16[104,256]{1,0:T(8,128)(2,1)S(1)}, bf16[104,256]{1,0:T(8,128)(2,1)S(1)}, u32[]{:S(2)}, u32[]{:S(2)}) collective-permute-start(bf16[104,256]{1,0:T(8,128)(2,1)S(1)} %get-tuple-element.81), channel_id=1, source_target_pairs={{0,16},{4,20},{8,24},{12,28},{16,0},{20,4},{24,8},{28,12},{1,17},{... | collective-permute-start | bytes 159752 | tf_op jit(solution)/shard_map/ppermute | solution.py:386
  20.6 9.2 %collective-permute-start.9 = (bf16[256,256]{1,0:T(8,128)(2,1)S(1)}, bf16[256,256]{1,0:T(8,128)(2,1)S(1)}, u32[]{:S(2)}, u32[]{:S(2)}) collective-permute-start(bf16[256,256]{1,0:T(8,128)(2,1)S(1)} %get-tuple-element.66), channel_id=1, source_target_pairs={{0,1},{1,0},{2,3},{3,2},{4,5},{5,4},{6,7},{7,6},{8,9},{9,8},{10,11... | collective-permute-start | bytes 393224 | tf_op jit(solution)/shard_map/ppermute | solution.py:539
  23.0 6.9 %collective-permute-start.8 = (bf16[104,256]{1,0:T(8,128)(2,1)S(1)}, bf16[104,256]{1,0:T(8,128)(2,1)S(1)}, u32[]{:S(2)}, u32[]{:S(2)}) collective-permute-start(bf16[104,256]{1,0:T(8,128)(2,1)S(1)} %fusion.2), channel_id=1, source_target_pairs={{0,3},{1,2},{2,1},{3,0},{4,7},{5,6},{6,5},{7,4},{8,11},{9,10},{10,... | collective-permute-start | bytes 159752 | tf_op jit(solution)/shard_map/ppermute | solution.py:386
  26.0 5.7 %collective-permute-start.7 = (bf16[104,256]{1,0:T(8,128)(2,1)S(1)}, bf16[104,256]{1,0:T(8,128)(2,1)S(1)}, u32[]{:S(2)}, u32[]{:S(2)}) collective-permute-start(bf16[104,256]{1,0:T(8,128)(2,1)S(1)} %fusion.2), channel_id=1, source_target_pairs={{0,2},{1,3},{2,0},{3,1},{4,6},{5,7},{6,4},{7,5},{8,10},{9,11},{10,... | collective-permute-start | bytes 159752 | tf_op jit(solution)/shard_map/ppermute | solution.py:386
  26.0 5.6 %collective-permute-start.6 = (bf16[104,256]{1,0:T(8,128)(2,1)S(1)}, bf16[104,256]{1,0:T(8,128)(2,1)S(1)}, u32[]{:S(2)}, u32[]{:S(2)}) collective-permute-start(bf16[104,256]{1,0:T(8,128)(2,1)S(1)} %fusion.2), channel_id=1, source_target_pairs={{0,1},{1,0},{2,3},{3,2},{4,5},{5,4},{6,7},{7,6},{8,9},{9,8},{10,11... | collective-permute-start | bytes 159752 | tf_op jit(solution)/shard_map/ppermute | solution.py:386
  27.4 9.0 %collective-permute-start.11 = (bf16[256,256]{1,0:T(8,128)(2,1)S(1)}, bf16[256,256]{1,0:T(8,128)(2,1)S(1)}, u32[]{:S(2)}, u32[]{:S(2)}) collective-permute-start(bf16[256,256]{1,0:T(8,128)(2,1)S(1)} %get-tuple-element.69), channel_id=1, source_target_pairs={{0,31},{1,2},{2,1},{3,4},{4,3},{5,6},{6,5},{7,8},{8,7},{9,10},{10,... | collective-permute-start | bytes 393224 | tf_op jit(solution)/shard_map/ppermute | solution.py:538
  31.7 5.8 %collective-permute-start.10 = (bf16[104,256]{1,0:T(8,128)(2,1)S(1)}, bf16[104,256]{1,0:T(8,128)(2,1)S(1)}, u32[]{:S(2)}, u32[]{:S(2)}) collective-permute-start(bf16[104,256]{1,0:T(8,128)(2,1)S(1)} %add_convert_fusion.1.refs_0_), channel_id=1, source_target_pairs={{0,24},{4,28},{8,16},{12,20},{16,8},{20,12},{24,0},{28,4},{1,25},{... | collective-permute-start | bytes 159752 | tf_op jit(solution)/shard_map/ppermute | solution.py:386
  33.3 4.6 %collective-permute-start.13 = (bf16[104,256]{1,0:T(8,128)(2,1)S(1)}, bf16[104,256]{1,0:T(8,128)(2,1)S(1)}, u32[]{:S(2)}, u32[]{:S(2)}) collective-permute-start(bf16[104,256]{1,0:T(8,128)(2,1)S(1)} %add_convert_fusion.1.refs_0_), channel_id=1, source_target_pairs={{0,16},{4,20},{8,24},{12,28},{16,0},{20,4},{24,8},{28,12},{1,17},{... | collective-permute-start | bytes 159752 | tf_op jit(solution)/shard_map/ppermute | solution.py:386
  33.9 4.1 %collective-permute-start.12 = (bf16[104,256]{1,0:T(8,128)(2,1)S(1)}, bf16[104,256]{1,0:T(8,128)(2,1)S(1)}, u32[]{:S(2)}, u32[]{:S(2)}) collective-permute-start(bf16[104,256]{1,0:T(8,128)(2,1)S(1)} %add_convert_fusion.1.refs_0_), channel_id=1, source_target_pairs={{0,8},{4,12},{8,0},{12,4},{16,24},{20,28},{24,16},{28,20},{1,9},{5... | collective-permute-start | bytes 159752 | tf_op jit(solution)/shard_map/ppermute | solution.py:386
  38.1 1.5 %collective-permute-start.14 = (bf16[4,104,256]{2,1,0:T(8,128)(2,1)S(1)}, bf16[4,104,256]{2,1,0:T(8,128)(2,1)S(1)}, u32[]{:S(2)}, u32[]{:S(2)}) collective-permute-start(bf16[4,104,256]{2,1,0:T(8,128)(2,1)S(1)} %pad_maximum_fusion), channel_id=1, source_target_pairs={{0,4},{4,0},{8,12},{12,8},{16,20},{20,16},{24,28},{28,24},{1,5},{5... | collective-permute-start | bytes 638984 | tf_op jit(solution)/shard_map/ppermute | solution.py:386
